TPU v7x, 32 devices: a whole 2x2x4 slice. The times are simulated.
32 devices in a mesh: ctx: 8 (over z, x), tp: 4 (over y, core).
Axes of the slice: x: 2, y: 2, z: 4, core: 2. Of those that a mesh axis runs over, the one named last changes fastest.
Arguments:
- tokens: int32 [2048], P('ctx'), may hold values from 0 to 3
- rc_map: int32 [4], replicated, may hold values from 0 to 3, each once
- embedding: bfloat16 [4, 2048], replicated, may hold values from -6 to 6
- norm_gain: float32 [2048], replicated, may hold values from 0.5 to 1.5
- w_values: bfloat16 [2048, 4096], P(None, 'tp'), may hold values from -0.125 to 0.125
- w_gates: bfloat16 [2048, 4096], P(None, 'tp'), may hold values from -0.125 to 0.125
- w_states: bfloat16 [2048, 256], replicated, may hold values from -0.125 to 0.125
- w_steps: bfloat16 [2048, 32], P(None, 'tp'), may hold values from -0.125 to 0.125
- conv_values: float32 [4, 4096], P(None, 'tp'), may hold values from -0.5 to 0.5
- conv_states: float32 [4, 256], replicated, may hold values from -0.5 to 0.5
- step_bias: float32 [32], P('tp'), may hold values from -1 to 1
- log_rate: float32 [32], P('tp'), as said below
- skip_gain: float32 [32], P('tp'), may hold values from 0.5 to 1.5
- head_gain: float32 [4096], P('tp'), may hold values from 0.5 to 1.5
- cotangent: bfloat16 [2048, 4096], P('ctx', 'tp'), may hold values from -6 to 6
Outputs:
- encoded: bfloat16 [2048, 4096], P('ctx', 'tp')
- grad_log_rate: float32 [32], replicated
- grad_step_bias: float32 [32], replicated
- grad_conv_states: float32 [4, 256], replicated
Inputs may be any that keep to these rules, and one draw needn't show every extreme that they name: `rc_map`: a permutation of the four ids. exp(log_rate) lies between 0.3 / 2048 and 0.1.
All inputs are finite; a program needn't handle non-finite values.
Results may differ from a plain program's by a relative error of at most 0.001.
The roundings to bfloat16 on the way count: a program that leaves them out, or rounds other values in their place, can miss the bound.
Values sent between devices are 32-bit elements; how exact they have to be, the bound alone decides.
No kernel may reach another device: no remote copies, remote signals or barrier semaphores. Data moves between devices by JAX's collectives and lax.ppermute only.
A program may use at most 128 MiB of HBM per device.

v0:
```python
import functools
import math

import jax
import jax.numpy as jnp
from jax import lax
from jax.experimental import pallas as pl
from jax.experimental.pallas import tpu as pltpu
from jax.sharding import PartitionSpec as P

HEAD = 128
STATE = 128
CONV = 4
IDS = 4
WINDOWS = IDS**CONV
ROWS = WINDOWS + 16
EPSILON = 1e-05

f32 = jnp.float32
bf16 = jnp.bfloat16
NN = (((1,), (0,)), ((), ()))
NT = (((1,), (1,)), ((), ()))
TN = (((0,), (0,)), ((), ()))


def iota(shape, dim):
    return lax.broadcasted_iota(jnp.int32, shape, dim)


def mm(a, b, dims=NN):
    return lax.dot_general(a, b, dims, preferred_element_type=f32)


def split(x):
    high = x.astype(bf16)
    return high, (x - high.astype(f32)).astype(bf16)


def mm3(a, b, dims=NN):
    return mm(a[0], b[0], dims) + (mm(a[0], b[1], dims) + mm(a[1], b[0], dims))


def sigmoid(v):
    return 1.0 / (1.0 + jnp.exp(-v))


def tables_kernel(emb_ref, gain_ref, wv_ref, wg_ref, ws_ref, wt_ref, tv_ref, tz_ref, tbc_ref, dt_ref):
    embedded = emb_ref[...].astype(f32)
    mean = jnp.mean(embedded * embedded, axis=1, keepdims=True)
    normed = (embedded * lax.rsqrt(mean + EPSILON) * gain_ref[...]).astype(bf16)
    for out, weights in ((tv_ref, wv_ref), (tz_ref, wg_ref), (tbc_ref, ws_ref)):
        out[0:IDS, :] = mm(normed, weights[...])
        out[IDS:, :] = jnp.zeros((8 - IDS, out.shape[1]), f32)
    dt_ref[...] = mm(wt_ref[...], normed, NT)


def tables(embedding, norm_gain, w_values, w_gates, w_states, w_steps):
    depth, width = w_values.shape
    heads = w_steps.shape[1]
    steps = width // 256
    state_blocks = w_states.shape[1] // 128
    whole = lambda shape: pl.BlockSpec(shape, lambda i: (0, 0))
    columns = lambda rows, size: pl.BlockSpec((rows, size), lambda i: (0, i))
    states = lambda rows: pl.BlockSpec((rows, 128), lambda i: (0, jnp.minimum(i, state_blocks - 1)))
    return pl.pallas_call(
        tables_kernel,
        grid=(steps,),
        in_specs=[
            whole(embedding.shape),
            whole((1, depth)),
            columns(depth, 256),
            columns(depth, 256),
            states(depth),
            whole((heads, depth)),
        ],
        out_specs=[columns(8, 256), columns(8, 256), states(8), whole((heads, IDS))],
        out_shape=[
            jax.ShapeDtypeStruct((8, width), f32),
            jax.ShapeDtypeStruct((8, width), f32),
            jax.ShapeDtypeStruct((8, w_states.shape[1]), f32),
            jax.ShapeDtypeStruct((heads, IDS), f32),
        ],
        compiler_params=pltpu.CompilerParams(vmem_limit_bytes=24 * 2**20),
        name="tables",
    )(embedding, norm_gain.reshape(1, depth), w_values, w_gates, w_states, w_steps.T)


def mixer_kernel(
    scale,
    tok_ref,
    rc_ref,
    place_ref,
    skip_ref,
    tv_ref,
    tbc_ref,
    tz_ref,
    dt_ref,
    cv_ref,
    cs_ref,
    bias_ref,
    rate_ref,
    gain_ref,
    cot_ref,
    enc_ref,
    grad_ref,
    tok_s,
    ids_s,
    count_s,
    onehot_s,
    weight_s,
    x_s,
    xh_s,
    xl_s,
    wh_s,
    wl_s,
    lh_s,
    ll_s,
    far_s,
    dh_s,
    dl_s,
    row_s,
    lcol_s,
    acol_s,
    tcol_s,
    gate_s,
    score_s,
    q_s,
    acc_s,
):
    devices, count = tok_ref.shape
    width = tv_ref.shape[1]
    heads = width // HEAD
    here = place_ref[0]
    tp_place = place_ref[1]

    for r in range(devices):
        tok_s[pl.ds(jnp.bitwise_xor(here, r), 1), :] = tok_ref[r : r + 1, :]
    tok = tok_s[...]
    rc = [rc_ref[t] for t in range(IDS)]
    rtok = jnp.zeros_like(tok)
    for t in range(IDS):
        rtok = jnp.where(tok == t, rc[t], rtok)
    lane = iota((devices, count), 1)
    row = iota((devices, count), 0)

    def before(ids, shift):
        turned = pltpu.roll(ids, shift, 1)
        return jnp.where(lane < shift, pltpu.roll(turned, 1, 0), turned)

    def after(ids, shift):
        turned = pltpu.roll(ids, count - shift, 1)
        return jnp.where(lane >= count - shift, pltpu.roll(turned, devices - 1, 0), turned)

    kf = before(tok, 3) + IDS * before(tok, 2) + IDS**2 * before(tok, 1) + IDS**3 * tok
    kr = after(rtok, 3) + IDS * after(rtok, 2) + IDS**2 * after(rtok, 1) + IDS**3 * rtok
    first = row * count + lane
    last = devices * count - 1 - first
    kf = jnp.where(first < CONV - 1, WINDOWS + first, kf)
    kr = jnp.where(last < CONV - 1, WINDOWS + CONV - 1 + last, kr)
    ids_s[0] = kf
    ids_s[1] = kr

    eye = iota((heads, heads), 0) == iota((heads, heads), 1)
    column = lambda ref: jnp.sum(jnp.where(eye, ref[...], 0.0), axis=1, keepdims=True)
    raw = dt_ref[...] + column(bias_ref)
    rate = jnp.exp(column(rate_ref))
    step = jnp.maximum(raw, 0.0) + jnp.log1p(jnp.exp(-jnp.abs(raw)))
    slope = sigmoid(raw)
    ratio = jnp.where(step > 1e-37, slope / jnp.maximum(step, 1e-37), 1.0)

    def per_strand(table):
        own = [table[:, t : t + 1] for t in range(IDS)]
        mapped = []
        for t in range(IDS):
            picked = own[0]
            for other in range(1, IDS):
                picked = jnp.where(rc[t] == other, own[other], picked)
            mapped.append(picked)
        return own, mapped

    step_of, slope_of, ratio_of = per_strand(step), per_strand(slope), per_strand(ratio)
    log_of, alog_of = per_strand(-rate * step), per_strand(-rate * slope)

    masks = [(tok == t).astype(f32) for t in range(IDS)]
    upper = (iota((count, count), 0) <= iota((count, count), 1)).astype(bf16)
    for t in range(IDS):
        count_s[t] = mm(masks[t].astype(bf16), upper)
    totals = [jnp.sum(m, axis=1, keepdims=True) for m in masks]
    row1 = iota((devices, 1), 0)
    far_counts = []
    for t in range(IDS):
        between = jnp.zeros((devices, 1), f32)
        for j in range(devices):
            inside = ((row1 < j) & (j < here)) | ((row1 > j) & (j > here))
            between = between + jnp.where(inside, totals[t][j : j + 1, :], 0.0)
        inclusive = count_s[t]
        far_counts.append(
            jnp.where(row < here, totals[t] - inclusive, inclusive - masks[t]) + between
        )

    window_rows = iota((ROWS, count), 0)
    for j in range(devices):
        forward = j < here
        reverse = j > here
        choose = lambda pair, t: jnp.where(forward, pair[0][t], pair[1][t])
        tok_j = tok[j : j + 1, :]
        log_sum = jnp.zeros((heads, count), f32)
        alog_sum = jnp.zeros((heads, count), f32)
        step_j = jnp.zeros((heads, count), f32)
        slope_j = jnp.zeros((heads, count), f32)
        for t in range(IDS):
            number = far_counts[t][j : j + 1, :]
            log_sum = log_sum + choose(log_of, t) * number
            alog_sum = alog_sum + choose(alog_of, t) * number
            step_j = jnp.where(tok_j == t, choose(step_of, t), step_j)
            slope_j = jnp.where(tok_j == t, choose(slope_of, t), slope_j)
        decay = jnp.exp(log_sum)
        weight = decay * step_j
        terms = jnp.concatenate([weight, weight * log_sum, decay * (slope_j + step_j * alog_sum)], axis=0)
        both = jnp.concatenate(
            [
                jnp.where(forward, terms, 0.0),
                jnp.where(reverse, terms, 0.0),
                jnp.zeros((64 - 6 * heads, count), f32),
            ],
            axis=0,
        )
        high, low = split(both)
        weight_s[0:64, j * count : (j + 1) * count] = high
        weight_s[64:128, j * count : (j + 1) * count] = low
        window_j = jnp.where(forward, kf[j : j + 1, :], kr[j : j + 1, :])
        onehot_s[:, j * count : (j + 1) * count] = (window_rows == window_j).astype(bf16)
    weights = mm(onehot_s[...], weight_s[...], NT)
    weights = weights + pltpu.roll(weights, 64, 1)

    lane_w = iota((WINDOWS, 128), 1)
    tap_w = (lane_w >> 3) & 3
    digit = (iota((WINDOWS, 128), 0) >> (2 * tap_w)) & 3
    lane_e = iota((16, 128), 1)
    row_e = iota((16, 128), 0)
    tap_e = (lane_e >> 3) & 3
    edge = jnp.full((16, 128), IDS, jnp.int32)
    for u in range(CONV - 1):
        for k in range(CONV - 1 - u, CONV):
            at = u - (CONV - 1) + k
            edge = jnp.where((row_e == u) & (tap_e == k), tok[0:1, at : at + 1], edge)
            edge = jnp.where(
                (row_e == CONV - 1 + u) & (tap_e == k),
                rtok[devices - 1 : devices, count - 1 - at : count - at],
                edge,
            )
    chosen = jnp.concatenate([digit, edge], axis=0)
    lane_r = iota((ROWS, 128), 1)
    pick = ((chosen == (lane_r & 7)) & (lane_r < 96)).astype(f32).astype(bf16)

    def windows(table, taps_ref):
        product = jnp.concatenate([taps_ref[k : k + 1, :] * table for k in range(CONV)], axis=0)
        p1 = product.astype(bf16)
        rest = product - p1.astype(f32)
        p2 = rest.astype(bf16)
        p3 = (rest - p2.astype(f32)).astype(bf16)
        return mm(pick, jnp.concatenate([p1, p2, p3, jnp.zeros_like(p1)], axis=0))

    summed = windows(tv_ref[...], cv_ref)
    x_all = summed * sigmoid(summed)
    x_s[...] = x_all
    xh_s[...], xl_s[...] = split(x_all)
    table_bc = tbc_ref[...]
    summed = windows(table_bc, cs_ref)
    sig = sigmoid(summed)
    bc_all = summed * sig
    bc_slope = sig * (1.0 + summed * (1.0 - sig))
    bc = split(bc_all)
    b_all = (bc[0][:, :STATE], bc[1][:, :STATE])

    own_tok = tok_s[pl.ds(here, 1), :]
    own_masks = [(own_tok == t).astype(f32) for t in range(IDS)]
    own_counts = [[], []]
    for t in range(IDS):
        inclusive = count_s[t, pl.ds(here, 1), :]
        total = jnp.sum(own_masks[t], axis=1, keepdims=True)
        own_counts[0].append(inclusive)
        own_counts[1].append(total - inclusive + own_masks[t])
    turned = []
    for s in range(2):
        logs = sum(log_of[s][t] * own_counts[s][t] for t in range(IDS))
        alogs = sum(alog_of[s][t] * own_counts[s][t] for t in range(IDS))
        row_s[s, 0] = logs
        row_s[s, 1] = sum(step_of[s][t] * own_masks[t] for t in range(IDS))
        row_s[s, 2] = sum(ratio_of[s][t] * own_masks[t] for t in range(IDS)) - alogs
        turned += [logs, alogs]
    own_ids = [ids_s[s, pl.ds(here, 1), :] for s in range(2)]
    extra = jnp.concatenate(
        [own_ids[0].astype(f32), own_ids[1].astype(f32), own_tok.astype(f32), jnp.zeros((5, count), f32)],
        axis=0,
    )
    turned = jnp.concatenate(turned + [extra, jnp.zeros((120 - 4 * heads, count), f32)], axis=0).T
    for s in range(2):
        for h in range(heads):
            at = 2 * s * heads + h
            lcol_s[s, h] = jnp.broadcast_to(turned[:, at : at + 1], (count, 128))
            acol_s[s, h] = jnp.broadcast_to(turned[:, at + heads : at + heads + 1], (count, 128))
    base = 4 * heads
    tcol_s[...] = jnp.broadcast_to(turned[:, base + 2 : base + 3], (count, 128))
    gates = tz_ref[...]
    gates = gates * sigmoid(gates)
    gate_s[0] = gates
    for t in range(IDS):
        picked = gates[0:1, :]
        for other in range(1, IDS):
            picked = jnp.where(rc[t] == other, gates[other : other + 1, :], picked)
        gate_s[1, t : t + 1, :] = picked

    own_onehot = []
    own_bc = []
    states = []
    lane_k = iota((count, ROWS), 1).astype(f32)
    for s in range(2):
        picks = (lane_k == turned[:, base + s : base + s + 1]).astype(f32).astype(bf16)
        own_onehot.append((window_rows == own_ids[s]).astype(f32).astype(bf16))
        lh_s[s] = mm(picks, xh_s[...]).astype(bf16)
        ll_s[s] = mm(picks, xl_s[...]).astype(bf16)
        own_bc.append((mm(picks, bc[0]).astype(bf16), mm(picks, bc[1]).astype(bf16)))
        own_b = tuple(part[:, :STATE] for part in own_bc[s])
        own_c = tuple(part[:, STATE:] for part in own_bc[s])
        score_s[s] = mm3(own_c, own_b, NT)
        for h in range(heads):
            at = 3 * s * heads + h
            columns = slice(h * HEAD, (h + 1) * HEAD)
            weighted = split(x_s[:, columns] * weights[:, at : at + 1])
            wh_s[s, :, columns], wl_s[s, :, columns] = weighted
        states.append(split(mm3(b_all, (wh_s[s], wl_s[s]), TN)))
        far_s[s] = mm3(own_c, states[s])

    q_s[...] = jnp.zeros_like(q_s)
    sub = iota((count, count), 0)
    lan = iota((count, count), 1)

    def one_head(h, _):
        columns = pl.ds(pl.multiple_of(h * HEAD, HEAD), HEAD)
        gain = gain_ref[:, columns]
        cot = cot_ref[:, columns].astype(f32) * scale * gain
        tcol = tcol_s[...]
        total_out = jnp.zeros((count, HEAD), f32)
        rate_row = jnp.zeros((1, 128), f32)
        bias_row = jnp.zeros((1, 128), f32)
        for s in range(2):
            lcol = lcol_s[s, h]
            log_row = row_s[s, 0, pl.ds(h, 1), :]
            step_row = row_s[s, 1, pl.ds(h, 1), :]
            mixed_row = row_s[s, 2, pl.ds(h, 1), :]
            causal = (sub >= lan) if s == 0 else (sub <= lan)
            wide = jnp.concatenate([lcol] * (count // 128), axis=1)
            factor = jnp.exp(jnp.where(causal, wide - log_row, -1e30)) * step_row
            mixing = score_s[s] * factor
            x = (lh_s[s, :, columns], ll_s[s, :, columns])
            grown = jnp.exp(lcol)
            y = mm3(split(mixing), x) + grown * far_s[s, :, columns]
            gate = gate_s[s, 0:1, columns]
            for t in range(1, IDS):
                gate = jnp.where(tcol == t, gate_s[s, t : t + 1, columns], gate)
            gated = (y + skip_ref[h] * (x[0].astype(f32) + x[1].astype(f32))) * gate
            inverse = lax.rsqrt(jnp.mean(gated * gated, axis=1, keepdims=True) + EPSILON)
            total_out = total_out + gated * inverse * gain
            shared = jnp.mean(cot * gated, axis=1, keepdims=True) * (inverse * inverse)
            dy = (cot - gated * shared) * inverse * gate
            e = mm3(split(dy), x, NT)
            q_s[s] += e * factor
            column_sum = jnp.sum(e * mixing, axis=0, keepdims=True)
            row_terms = dy * y
            fold = lambda v: sum(v[:, i * 128 : (i + 1) * 128] for i in range(count // 128))
            rate_row += jnp.sum(lcol * row_terms, axis=0, keepdims=True) - fold(log_row * column_sum)
            bias_row += jnp.sum(acol_s[s, h] * row_terms, axis=0, keepdims=True) + fold(mixed_row * column_sum)
            dh_s[s, :, columns], dl_s[s, :, columns] = split(grown * dy)
        enc_ref[:, columns] = total_out.astype(enc_ref.dtype)
        acc_s[0, pl.ds(h, 1), :] = rate_row
        acc_s[1, pl.ds(h, 1), :] = bias_row
        return 0

    lax.fori_loop(0, heads, one_head, 0)

    db_all = jnp.zeros((ROWS, STATE), f32)
    dc_all = jnp.zeros((ROWS, STATE), f32)
    for s in range(2):
        own_b = tuple(part[:, :STATE] for part in own_bc[s])
        own_c = tuple(part[:, STATE:] for part in own_bc[s])
        q = split(q_s[s])
        grown = (dh_s[s], dl_s[s])
        dc_own = split(mm3(q, own_b) + mm3(grown, states[s], NT))
        db_own = split(mm3(q, own_c, TN))
        back = split(mm3(own_c, grown, TN))
        dc_all = dc_all + (mm(own_onehot[s], dc_own[0]) + mm(own_onehot[s], dc_own[1]))
        db_all = db_all + (mm(own_onehot[s], db_own[0]) + mm(own_onehot[s], db_own[1]))
        db_all = db_all + mm3((wh_s[s], wl_s[s]), back, NT)
        reach = mm3(b_all, back)
        for h in range(heads):
            at = 3 * s * heads + heads + h
            columns = slice(h * HEAD, (h + 1) * HEAD)
            terms = reach[:, columns] * x_s[:, columns]
            acc_s[0, h : h + 1, :] += jnp.sum(terms * weights[:, at : at + 1], axis=0, keepdims=True)
            acc_s[1, h : h + 1, :] += jnp.sum(
                terms * weights[:, at + heads : at + heads + 1], axis=0, keepdims=True
            )
    d_summed = split(jnp.concatenate([db_all, dc_all], axis=1) * bc_slope)
    by_tap = mm(pick, d_summed[0], TN) + mm(pick, d_summed[1], TN)
    grad_ref[...] = jnp.zeros_like(grad_ref)
    for k in range(CONV):
        grad_ref[k : k + 1, :] = jnp.sum(by_tap[8 * k : 8 * k + 8, :] * table_bc, axis=0, keepdims=True)
    place = iota((heads, 128), 1) == iota((heads, 128), 0) + tp_place * heads
    for i in range(2):
        sums = jnp.sum(acc_s[i], axis=1, keepdims=True)
        grad_ref[CONV + i : CONV + i + 1, 0:128] = jnp.sum(jnp.where(place, sums, 0.0), axis=0, keepdims=True)


def mixer(tokens, rc_map, place, skip, tabs, conv_values, conv_states, bias, rate, gain, cotangent, scale):
    devices, count = tokens.shape
    width = conv_values.shape[1]
    heads = width // HEAD
    tv, tz, tbc, dt = tabs
    vmem = pl.BlockSpec(memory_space=pltpu.VMEM)
    smem = pl.BlockSpec(memory_space=pltpu.SMEM)
    scratch = [
        ((devices, count), jnp.int32),
        ((2, devices, count), jnp.int32),
        ((IDS, devices, count), f32),
        ((ROWS, devices * count), bf16),
        ((128, devices * count), bf16),
        ((ROWS, width), f32),
        ((ROWS, width), bf16),
        ((ROWS, width), bf16),
        ((2, ROWS, width), bf16),
        ((2, ROWS, width), bf16),
        ((2, count, width), bf16),
        ((2, count, width), bf16),
        ((2, count, width), f32),
        ((2, count, width), bf16),
        ((2, count, width), bf16),
        ((2, 3, heads, count), f32),
        ((2, heads, count, 128), f32),
        ((2, heads, count, 128), f32),
        ((count, 128), f32),
        ((2, 8, width), f32),
        ((2, count, count), f32),
        ((2, count, count), f32),
        ((2, heads, 128), f32),
    ]
    return pl.pallas_call(
        functools.partial(mixer_kernel, scale),
        in_specs=[vmem, smem, smem, smem] + [vmem] * 10,
        out_specs=[vmem, vmem],
        out_shape=[
            jax.ShapeDtypeStruct((count, width), bf16),
            jax.ShapeDtypeStruct((8, 2 * STATE), f32),
        ],
        scratch_shapes=[pltpu.VMEM(shape, kind) for shape, kind in scratch],
        compiler_params=pltpu.CompilerParams(vmem_limit_bytes=52 * 2**20),
        name="mixer",
    )(
        tokens,
        rc_map,
        place,
        skip,
        tv,
        tbc,
        tz,
        dt,
        conv_values,
        conv_states,
        bias.reshape(1, heads),
        rate.reshape(1, heads),
        gain.reshape(1, width),
        cotangent,
    )


def exchange(value, axis, distance):
    size = lax.axis_size(axis)
    return lax.ppermute(value, axis, [(i, i ^ distance) for i in range(size)])


def on_device(
    tokens,
    rc_map,
    embedding,
    norm_gain,
    w_values,
    w_gates,
    w_states,
    w_steps,
    conv_values,
    conv_states,
    step_bias,
    log_rate,
    skip_gain,
    head_gain,
    cotangent,
):
    devices = lax.axis_size("ctx")
    count = tokens.shape[0]
    everyone = tokens.reshape(1, count)
    distance = 1
    while distance < devices:
        everyone = jnp.concatenate([everyone, exchange(everyone, "ctx", distance)], axis=0)
        distance *= 2
    tabs = tables(embedding, norm_gain, w_values, w_gates, w_states, w_steps)
    place = jnp.stack([lax.axis_index("ctx"), lax.axis_index("tp")]).astype(jnp.int32)
    scale = 1.0 / math.sqrt(count * devices * HEAD)
    encoded, grads = mixer(
        everyone,
        rc_map,
        place,
        skip_gain,
        tabs,
        conv_values,
        conv_states,
        step_bias,
        log_rate,
        head_gain,
        cotangent,
        scale,
    )
    for axis in ("tp", "ctx"):
        distance = 1
        while distance < lax.axis_size(axis):
            grads = grads + exchange(grads, axis, distance)
            distance *= 2
    head_total = log_rate.shape[0] * lax.axis_size("tp")
    return (encoded, grads[CONV, :head_total], grads[CONV + 1, :head_total], grads[:CONV])


def solution(mesh):
    placed = (
        P("ctx"),
        P(),
        P(),
        P(),
        P(None, "tp"),
        P(None, "tp"),
        P(),
        P(None, "tp"),
        P(None, "tp"),
        P(),
        P("tp"),
        P("tp"),
        P("tp"),
        P("tp"),
        P("ctx", "tp"),
    )
    return jax.shard_map(
        on_device,
        mesh=mesh,
        in_specs=placed,
        out_specs=(P("ctx", "tp"), P(), P(), P()),
        check_vma=False,
    )
```

profile of v0, /device:TPU:0, one launch (start us, length us, event | category | flops | bytes accessed | tf_op | source)
XLA Modules:
  0.0 63.7 jit_solution(17832409072709770630)
XLA Ops:
  0.6 3.0 %collective-permute-start = (s32[1,256]{1,0:T(1,128)}, s32[1,256]{1,0:T(1,128)S(1)}, u32[]{:S(2)}, u32[]{:S(2)}) collective-permute-start(s32[1,256]{1,0:T(1,128)} %bitcast.17), channel_id=1, source_target_pairs={{0,4},{4,0},{8,12},{12,8},{16,20},{20,16},{24,28},{28,24},{1,5},{5... | collective-permute-start | bytes 3080 | tf_op jit(solution)/shard_map/ppermute | solution.py:478
  3.6 1.8 %collective-permute-done = s32[1,256]{1,0:T(1,128)S(1)} collective-permute-done((s32[1,256]{1,0:T(1,128)}, s32[1,256]{1,0:T(1,128)S(1)}, u32[]{:S(2)}, u32[]{:S(2)}) %collective-permute-start) | collective-permute-done | bytes 1056 | tf_op jit(solution)/shard_map/ppermute | solution.py:478
  5.4 0.7 %pad_add_fusion.2 = s32[2,256]{1,0:T(2,128)S(1)} fusion(s32[1,256]{1,0:T(1,128)S(1)} %collective-permute-done, s32[1,256]{1,0:T(1,128)} %bitcast.18), kind=kLoop, calls=%fused_computation.2 | loop fusion | flops 512 | bytes 4096 | tf_op jit(solution)/shard_map/concatenate | solution.py:503
  6.1 2.1 %collective-permute-start.1 = (s32[2,256]{1,0:T(2,128)S(1)}, s32[2,256]{1,0:T(2,128)S(1)}, u32[]{:S(2)}, u32[]{:S(2)}) collective-permute-start(s32[2,256]{1,0:T(2,128)S(1)} %pad_add_fusion.2), channel_id=1, source_target_pairs={{0,8},{4,12},{8,0},{12,4},{16,24},{20,28},{24,16},{28,20},{1,9},{5... | collective-permute-start | bytes 6152 | tf_op jit(solution)/shard_map/ppermute | solution.py:478
  8.2 1.6 %collective-permute-done.1 = s32[2,256]{1,0:T(2,128)S(1)} collective-permute-done((s32[2,256]{1,0:T(2,128)S(1)}, s32[2,256]{1,0:T(2,128)S(1)}, u32[]{:S(2)}, u32[]{:S(2)}) %collective-permute-start.1) | collective-permute-done | bytes 2080 | tf_op jit(solution)/shard_map/ppermute | solution.py:478
  9.7 0.7 %pad_add_fusion.1 = s32[4,256]{1,0:T(4,128)S(1)} fusion(s32[2,256]{1,0:T(2,128)S(1)} %collective-permute-done.1, s32[1,256]{1,0:T(1,128)S(1)} %collective-permute-done, s32[1,256]{1,0:T(1,128)} %bitcast.19), kind=kLoop, calls=%fused_computation.1 | loop fusion | flops 2048 | bytes 8192 | tf_op jit(solution)/shard_map/concatenate | solution.py:503
  10.4 3.0 %collective-permute-start.2 = (s32[4,256]{1,0:T(4,128)S(1)}, s32[4,256]{1,0:T(4,128)S(1)}, u32[]{:S(2)}, u32[]{:S(2)}) collective-permute-start(s32[4,256]{1,0:T(4,128)S(1)} %pad_add_fusion.1), channel_id=1, source_target_pairs={{0,16},{4,20},{8,24},{12,28},{16,0},{20,4},{24,8},{28,12},{1,17},{... | collective-permute-start | bytes 12296 | tf_op jit(solution)/shard_map/ppermute | solution.py:478
  13.5 0.1 pad_add_fusion.3.place_ref
  13.5 0.0 copy-start
  13.5 2.2 %copy-done = bf16[2048,1024]{1,0:T(8,128)(2,1)S(1)} copy-done((bf16[2048,1024]{1,0:T(8,128)(2,1)S(1)}, bf16[2048,1024]{1,0:T(8,128)(2,1)}, u32[]{:S(2)}) %copy-start) | copy-done | bytes 4194328
  15.7 0.0 copy-start.1
  15.7 2.2 %copy-done.1 = bf16[2048,1024]{1,0:T(8,128)(2,1)S(1)} copy-done((bf16[2048,1024]{1,0:T(8,128)(2,1)S(1)}, bf16[2048,1024]{1,0:T(8,128)(2,1)}, u32[]{:S(2)}) %copy-start.1) | copy-done | bytes 4194328
  17.9 0.0 copy-start.2
  17.9 1.2 %copy-done.2 = bf16[2048,256]{1,0:T(8,128)(2,1)S(1)} copy-done((bf16[2048,256]{1,0:T(8,128)(2,1)S(1)}, bf16[2048,256]{1,0:T(8,128)(2,1)}, u32[]{:S(2)}) %copy-start.2) | copy-done | bytes 1048600
  19.1 0.0 copy-start.4
  19.2 0.8 %copy-done.4 = bf16[2048,8]{0,1:T(8,128)(2,1)S(1)} copy-done((bf16[2048,8]{0,1:T(8,128)(2,1)S(1)}, bf16[2048,8]{0,1:T(8,128)(2,1)}, u32[]{:S(2)}) %copy-start.4) | copy-done | bytes 32792
  19.9 0.0 copy-start.5
  19.9 0.7 %copy-done.5 = bf16[4,2048]{1,0:T(4,128)(2,1)S(1)} copy-done((bf16[4,2048]{1,0:T(4,128)(2,1)S(1)}, bf16[4,2048]{1,0:T(4,128)(2,1)}, u32[]{:S(2)}) %copy-start.5) | copy-done | bytes 16408
  20.6 0.7 %copy-done.7 = f32[2048]{0:T(1024)S(1)} copy-done((f32[2048]{0:T(1024)S(1)}, f32[2048]{0:T(1024)}, u32[]{:S(2)}) %copy-start.7) | copy-done | bytes 8216
  21.3 0.0 copy-start.9
  21.3 0.0 copy-start.10
  21.4 0.0 copy-start.11
  21.4 0.0 copy-start.12
  21.4 0.0 copy-start.13
  21.4 3.5 %tables.1 = (f32[8,1024]{1,0:T(8,128)S(1)}, f32[8,1024]{1,0:T(8,128)S(1)}, f32[8,256]{1,0:T(8,128)S(1)}, f32[8,4]{1,0:T(8,128)S(1)}) custom-call(bf16[4,2048]{1,0:T(4,128)(2,1)S(1)} %copy-done.5, f32[1,2048]{1,0:T(1,128)S(1)} %bitcast.13, bf16[2048,1024]{1,0:T(8,128)(2,1)S(1)} %copy-done, bf16[2048,1024]{1,0:T(8,128)(2,1)S(1)} %copy-done.1, ...), custom_call_target="tpu_custom_call" | custom-call | tf_op jit(solution)/shard_map/tables/pallas_call | solution.py:65
  24.9 0.0 collective-permute-done.2
  25.0 0.0 copy-done.14
  25.0 0.0 copy-done.3
  25.0 0.0 copy-done.6
  25.0 0.0 copy-done.8
  25.0 0.0 copy-done.9
  25.0 0.0 copy-done.10
  25.0 0.0 copy-done.11
  25.0 0.0 copy-done.12
  25.1 0.0 copy-done.13
  25.1 20.7 %mixer.1 = (bf16[256,1024]{1,0:T(8,128)(2,1)}, f32[8,256]{1,0:T(8,128)S(1)}) custom-call(s32[8,256]{1,0:T(8,128)S(1)} %pad_add_fusion.tok_ref, s32[4]{0:T(128)S(1)} %copy-done.10, s32[2]{0:T(128)S(1)} %pad_add_fusion.3.place_ref, f32[8]{0:T(128)S(1)} %copy-done.11, f32[8,1024]{1,0:T(8,128)S(1)} %get-tuple-element.10.tv_ref, ...), custom_call_target="tpu_custom_call" | custom-call | tf_op jit(solution)/shard_map/mixer/pallas_call | solution.py:447
  45.8 0.1 collective-permute-start.3
  45.9 1.2 %collective-permute-done.3 = f32[8,256]{1,0:T(8,128)S(1)} collective-permute-done((f32[8,256]{1,0:T(8,128)S(1)}, f32[8,256]{1,0:T(8,128)S(1)}, u32[]{:S(2)}, u32[]{:S(2)}) %collective-permute-start.3) | collective-permute-done | bytes 8224 | tf_op jit(solution)/shard_map/ppermute | solution.py:478
  47.0 1.5 %collective-permute-start.4 = (f32[8,256]{1,0:T(8,128)S(1)}, f32[8,256]{1,0:T(8,128)S(1)}, u32[]{:S(2)}, u32[]{:S(2)}) collective-permute-start(f32[8,256]{1,0:T(8,128)S(1)} %add.15), channel_id=1, source_target_pairs={{0,2},{1,3},{2,0},{3,1},{4,6},{5,7},{6,4},{7,5},{8,10},{9,11},{10,... | collective-permute-start | bytes 24584 | tf_op jit(solution)/shard_map/ppermute | solution.py:478
  48.6 2.1 %collective-permute-done.4 = f32[8,256]{1,0:T(8,128)S(1)} collective-permute-done((f32[8,256]{1,0:T(8,128)S(1)}, f32[8,256]{1,0:T(8,128)S(1)}, u32[]{:S(2)}, u32[]{:S(2)}) %collective-permute-start.4) | collective-permute-done | bytes 8224 | tf_op jit(solution)/shard_map/ppermute | solution.py:478
  50.7 1.5 %collective-permute-start.5 = (f32[8,256]{1,0:T(8,128)S(1)}, f32[8,256]{1,0:T(8,128)S(1)}, u32[]{:S(2)}, u32[]{:S(2)}) collective-permute-start(f32[8,256]{1,0:T(8,128)S(1)} %add.16), channel_id=1, source_target_pairs={{0,4},{4,0},{8,12},{12,8},{16,20},{20,16},{24,28},{28,24},{1,5},{5... | collective-permute-start | bytes 24584 | tf_op jit(solution)/shard_map/ppermute | solution.py:478
  52.2 2.2 %collective-permute-done.5 = f32[8,256]{1,0:T(8,128)S(1)} collective-permute-done((f32[8,256]{1,0:T(8,128)S(1)}, f32[8,256]{1,0:T(8,128)S(1)}, u32[]{:S(2)}, u32[]{:S(2)}) %collective-permute-start.5) | collective-permute-done | bytes 8224 | tf_op jit(solution)/shard_map/ppermute | solution.py:478
  54.4 1.6 %collective-permute-start.6 = (f32[8,256]{1,0:T(8,128)S(1)}, f32[8,256]{1,0:T(8,128)S(1)}, u32[]{:S(2)}, u32[]{:S(2)}) collective-permute-start(f32[8,256]{1,0:T(8,128)S(1)} %add.17), channel_id=1, source_target_pairs={{0,8},{4,12},{8,0},{12,4},{16,24},{20,28},{24,16},{28,20},{1,9},{5... | collective-permute-start | bytes 24584 | tf_op jit(solution)/shard_map/ppermute | solution.py:478
  55.9 2.1 %collective-permute-done.6 = f32[8,256]{1,0:T(8,128)S(1)} collective-permute-done((f32[8,256]{1,0:T(8,128)S(1)}, f32[8,256]{1,0:T(8,128)S(1)}, u32[]{:S(2)}, u32[]{:S(2)}) %collective-permute-start.6) | collective-permute-done | bytes 8224 | tf_op jit(solution)/shard_map/ppermute | solution.py:478
  58.0 0.0 collective-permute-start.7
  58.0 4.5 %collective-permute-done.7 = f32[8,256]{1,0:T(8,128)S(1)} collective-permute-done((f32[8,256]{1,0:T(8,128)S(1)}, f32[8,256]{1,0:T(8,128)S(1)}, u32[]{:S(2)}, u32[]{:S(2)}) %collective-permute-start.7) | collective-permute-done | bytes 8224 | tf_op jit(solution)/shard_map/ppermute | solution.py:478
  62.6 0.5 slice_bitcast_fusion
  63.1 0.6 slice.14
  (11 shorter events, 0.0 us)
Async XLA Ops:
  0.6 4.8 %collective-permute-start = (s32[1,256]{1,0:T(1,128)}, s32[1,256]{1,0:T(1,128)S(1)}, u32[]{:S(2)}, u32[]{:S(2)}) collective-permute-start(s32[1,256]{1,0:T(1,128)} %bitcast.17), channel_id=1, source_target_pairs={{0,4},{4,0},{8,12},{12,8},{16,20},{20,16},{24,28},{28,24},{1,5},{5... | collective-permute-start | bytes 3080 | tf_op jit(solution)/shard_map/ppermute | solution.py:478
  6.1 3.7 %collective-permute-start.1 = (s32[2,256]{1,0:T(2,128)S(1)}, s32[2,256]{1,0:T(2,128)S(1)}, u32[]{:S(2)}, u32[]{:S(2)}) collective-permute-start(s32[2,256]{1,0:T(2,128)S(1)} %pad_add_fusion.2), channel_id=1, source_target_pairs={{0,8},{4,12},{8,0},{12,4},{16,24},{20,28},{24,16},{28,20},{1,9},{5... | collective-permute-start | bytes 6152 | tf_op jit(solution)/shard_map/ppermute | solution.py:478
  10.4 14.5 %collective-permute-start.2 = (s32[4,256]{1,0:T(4,128)S(1)}, s32[4,256]{1,0:T(4,128)S(1)}, u32[]{:S(2)}, u32[]{:S(2)}) collective-permute-start(s32[4,256]{1,0:T(4,128)S(1)} %pad_add_fusion.1), channel_id=1, source_target_pairs={{0,16},{4,20},{8,24},{12,28},{16,0},{20,4},{24,8},{28,12},{1,17},{... | collective-permute-start | bytes 12296 | tf_op jit(solution)/shard_map/ppermute | solution.py:478
  13.5 2.2 %copy-start = (bf16[2048,1024]{1,0:T(8,128)(2,1)S(1)}, bf16[2048,1024]{1,0:T(8,128)(2,1)}, u32[]{:S(2)}) copy-start(bf16[2048,1024]{1,0:T(8,128)(2,1)} %wv_ref.1) | copy-start | bytes 12582916
  15.7 2.2 %copy-start.1 = (bf16[2048,1024]{1,0:T(8,128)(2,1)S(1)}, bf16[2048,1024]{1,0:T(8,128)(2,1)}, u32[]{:S(2)}) copy-start(bf16[2048,1024]{1,0:T(8,128)(2,1)} %wg_ref.1) | copy-start | bytes 12582916
  17.9 1.2 %copy-start.2 = (bf16[2048,256]{1,0:T(8,128)(2,1)S(1)}, bf16[2048,256]{1,0:T(8,128)(2,1)}, u32[]{:S(2)}) copy-start(bf16[2048,256]{1,0:T(8,128)(2,1)} %ws_ref.1) | copy-start | bytes 3145732
  19.1 0.8 %copy-start.4 = (bf16[2048,8]{0,1:T(8,128)(2,1)S(1)}, bf16[2048,8]{0,1:T(8,128)(2,1)}, u32[]{:S(2)}) copy-start(bf16[2048,8]{0,1:T(8,128)(2,1)} %param.22) | copy-start | bytes 98308
  19.9 0.7 %copy-start.5 = (bf16[4,2048]{1,0:T(4,128)(2,1)S(1)}, bf16[4,2048]{1,0:T(4,128)(2,1)}, u32[]{:S(2)}) copy-start(bf16[4,2048]{1,0:T(4,128)(2,1)} %emb_ref.1) | copy-start | bytes 49156
  20.6 0.7 %copy-start.7 = (f32[2048]{0:T(1024)S(1)}, f32[2048]{0:T(1024)}, u32[]{:S(2)}) copy-start(f32[2048]{0:T(1024)} %param.18) | copy-start | bytes 24580
  21.3 3.6 %copy-start.14 = (s32[256]{0:T(256)S(1)}, s32[256]{0:T(256)}, u32[]{:S(2)}) copy-start(s32[256]{0:T(256)} %param.15) | copy-start | bytes 3076
  21.3 3.7 %copy-start.3 = (bf16[256,1024]{1,0:T(8,128)(2,1)S(1)}, bf16[256,1024]{1,0:T(8,128)(2,1)}, u32[]{:S(2)}) copy-start(bf16[256,1024]{1,0:T(8,128)(2,1)} %cot_ref.1) | copy-start | bytes 1572868
  21.3 3.7 %copy-start.6 = (f32[4,1024]{1,0:T(4,128)S(1)}, f32[4,1024]{1,0:T(4,128)}, u32[]{:S(2)}) copy-start(f32[4,1024]{1,0:T(4,128)} %cv_ref.1) | copy-start | bytes 49156
  21.3 3.7 %copy-start.8 = (f32[4,256]{1,0:T(4,128)S(1)}, f32[4,256]{1,0:T(4,128)}, u32[]{:S(2)}) copy-start(f32[4,256]{1,0:T(4,128)} %cs_ref.1) | copy-start | bytes 12292
  21.3 3.7 %copy-start.9 = (f32[1024]{0:T(1024)S(1)}, f32[1024]{0:T(1024)}, u32[]{:S(2)}) copy-start(f32[1024]{0:T(1024)} %param.28) | copy-start | bytes 12292
  21.3 3.7 %copy-start.10 = (s32[4]{0:T(128)S(1)}, s32[4]{0:T(128)}, u32[]{:S(2)}) copy-start(s32[4]{0:T(128)} %rc_ref.1) | copy-start | bytes 52
  21.4 3.7 %copy-start.11 = (f32[8]{0:T(128)S(1)}, f32[8]{0:T(128)}, u32[]{:S(2)}) copy-start(f32[8]{0:T(128)} %skip_ref.1) | copy-start | bytes 100
  21.4 3.7 %copy-start.12 = (f32[8]{0:T(128)S(1)}, f32[8]{0:T(128)}, u32[]{:S(2)}) copy-start(f32[8]{0:T(128)} %param.25) | copy-start | bytes 100
  21.4 3.7 %copy-start.13 = (f32[8]{0:T(128)S(1)}, f32[8]{0:T(128)}, u32[]{:S(2)}) copy-start(f32[8]{0:T(128)} %param.26) | copy-start | bytes 100
  45.8 1.2 %collective-permute-start.3 = (f32[8,256]{1,0:T(8,128)S(1)}, f32[8,256]{1,0:T(8,128)S(1)}, u32[]{:S(2)}, u32[]{:S(2)}) collective-permute-start(f32[8,256]{1,0:T(8,128)S(1)} %get-tuple-element.15), channel_id=1, source_target_pairs={{0,1},{1,0},{2,3},{3,2},{4,5},{5,4},{6,7},{7,6},{8,9},{9,8},{10,11... | collective-permute-start | bytes 24584 | tf_op jit(solution)/shard_map/ppermute | solution.py:478
  47.0 3.7 %collective-permute-start.4 = (f32[8,256]{1,0:T(8,128)S(1)}, f32[8,256]{1,0:T(8,128)S(1)}, u32[]{:S(2)}, u32[]{:S(2)}) collective-permute-start(f32[8,256]{1,0:T(8,128)S(1)} %add.15), channel_id=1, source_target_pairs={{0,2},{1,3},{2,0},{3,1},{4,6},{5,7},{6,4},{7,5},{8,10},{9,11},{10,... | collective-permute-start | bytes 24584 | tf_op jit(solution)/shard_map/ppermute | solution.py:478
  50.7 3.7 %collective-permute-start.5 = (f32[8,256]{1,0:T(8,128)S(1)}, f32[8,256]{1,0:T(8,128)S(1)}, u32[]{:S(2)}, u32[]{:S(2)}) collective-permute-start(f32[8,256]{1,0:T(8,128)S(1)} %add.16), channel_id=1, source_target_pairs={{0,4},{4,0},{8,12},{12,8},{16,20},{20,16},{24,28},{28,24},{1,5},{5... | collective-permute-start | bytes 24584 | tf_op jit(solution)/shard_map/ppermute | solution.py:478
  54.4 3.7 %collective-permute-start.6 = (f32[8,256]{1,0:T(8,128)S(1)}, f32[8,256]{1,0:T(8,128)S(1)}, u32[]{:S(2)}, u32[]{:S(2)}) collective-permute-start(f32[8,256]{1,0:T(8,128)S(1)} %add.17), channel_id=1, source_target_pairs={{0,8},{4,12},{8,0},{12,4},{16,24},{20,28},{24,16},{28,20},{1,9},{5... | collective-permute-start | bytes 24584 | tf_op jit(solution)/shard_map/ppermute | solution.py:478
  58.0 4.5 %collective-permute-start.7 = (f32[8,256]{1,0:T(8,128)S(1)}, f32[8,256]{1,0:T(8,128)S(1)}, u32[]{:S(2)}, u32[]{:S(2)}) collective-permute-start(f32[8,256]{1,0:T(8,128)S(1)} %add.18), channel_id=1, source_target_pairs={{0,16},{4,20},{8,24},{12,28},{16,0},{20,4},{24,8},{28,12},{1,17},{... | collective-permute-start | bytes 24584 | tf_op jit(solution)/shard_map/ppermute | solution.py:478
where the time goes:
time: 64.1 us; the launch traced here: 63.7 us
  Pallas kernels  24.3 us (38%)
  waiting for transfers between devices  15.4 us (24%)
  starting transfers between devices  12.8 us (20%)
  local copies, waits for them, and re-layouts  8.93 us (14%)
  other arithmetic  1.48 us (2%)
  between operations  0.8 us (1%)
    pallas_call x1, Pallas kernels, mixer(): pl.pallas_call(functools.partial(mixer_kernel, scale), in_specs=[vmem, sm...  20.7 us
    ppermute x8, waiting for transfers between devices, exchange(): return lax.ppermute(value, axis, [(i, i ^ distance) for i in range(size)])  15.4 us
    ppermute x8, starting transfers between devices, exchange(): return lax.ppermute(value, axis, [(i, i ^ distance) for i in range(size)])  12.8 us
    unnamed x30, local copies, waits for them, and re-layouts  7.82 us
    pallas_call x1, Pallas kernels, tables(): pl.pallas_call(tables_kernel, grid=(steps,), in_specs=[whole(embedding.sh...  3.54 us
    concatenate x3, other arithmetic, on_device(): jnp.concatenate([everyone, exchange(everyone, 'ctx', distance)], axis=0)  1.39 us
  transfers between devices with their start and end apart: 8, of which 7 were waited for; matrix products, arithmetic and copies ran while one was open for 0% of the time, Pallas kernels for 6%

commit v1 on v0

--- a/solution.py
+++ b/solution.py
@@ -44,45 +44,118 @@
     return 1.0 / (1.0 + jnp.exp(-v))
 
 
-def tables_kernel(emb_ref, gain_ref, wv_ref, wg_ref, ws_ref, wt_ref, tv_ref, tz_ref, tbc_ref, dt_ref):
+def windows(pick, table, taps):
+    product = jnp.concatenate([taps[k : k + 1, :] * table for k in range(CONV)], axis=0)
+    p1 = product.astype(bf16)
+    rest = product - p1.astype(f32)
+    p2 = rest.astype(bf16)
+    p3 = (rest - p2.astype(f32)).astype(bf16)
+    return mm(pick, jnp.concatenate([p1, p2, p3, jnp.zeros_like(p1)], axis=0))
+
+
+def tables_kernel(
+    emb_ref,
+    gain_ref,
+    wt_ref,
+    cv_ref,
+    cs_ref,
+    wv_ref,
+    wg_ref,
+    ws_ref,
+    tv_ref,
+    tz_ref,
+    tbc_ref,
+    dt_ref,
+    x_ref,
+    x2_ref,
+    bc_ref,
+    slope_ref,
+    held_v,
+    held_g,
+    held_s,
+    sems,
+):
+    chunks = held_v.shape[0]
+    size = held_v.shape[2]
+    copies = [pltpu.make_async_copy(ws_ref, held_s, sems.at[0])]
+    for i in range(chunks):
+        columns = pl.ds(i * size, size)
+        copies.append(pltpu.make_async_copy(wv_ref.at[:, columns], held_v.at[i], sems.at[1 + i]))
+    for i in range(chunks):
+        columns = pl.ds(i * size, size)
+        copies.append(pltpu.make_async_copy(wg_ref.at[:, columns], held_g.at[i], sems.at[1 + chunks + i]))
+    for copy in copies:
+        copy.start()
     embedded = emb_ref[...].astype(f32)
     mean = jnp.mean(embedded * embedded, axis=1, keepdims=True)
     normed = (embedded * lax.rsqrt(mean + EPSILON) * gain_ref[...]).astype(bf16)
-    for out, weights in ((tv_ref, wv_ref), (tz_ref, wg_ref), (tbc_ref, ws_ref)):
-        out[0:IDS, :] = mm(normed, weights[...])
-        out[IDS:, :] = jnp.zeros((8 - IDS, out.shape[1]), f32)
     dt_ref[...] = mm(wt_ref[...], normed, NT)
-
-
-def tables(embedding, norm_gain, w_values, w_gates, w_states, w_steps):
+    lane = iota((WINDOWS, 128), 1)
+    digit = (iota((WINDOWS, 128), 0) >> (2 * ((lane >> 3) & 3))) & 3
+    pick = ((digit == (lane & 7)) & (lane < 96)).astype(f32).astype(bf16)
+
+    def rows(weights):
+        product = mm(normed, weights)
+        return jnp.concatenate([product, jnp.zeros((8 - IDS, product.shape[1]), f32)], axis=0)
+
+    copies[0].wait()
+    table = rows(held_s[...])
+    tbc_ref[...] = table
+    summed = windows(pick, table, cs_ref[...])
+    sig = sigmoid(summed)
+    bc_ref[...] = summed * sig
+    slope_ref[...] = sig * (1.0 + summed * (1.0 - sig))
+    for i in range(chunks):
+        copies[1 + i].wait()
+        columns = slice(i * size, (i + 1) * size)
+        table = rows(held_v[i])
+        tv_ref[:, columns] = table
+        summed = windows(pick, table, cv_ref[:, columns])
+        x = summed * sigmoid(summed)
+        x_ref[:, columns] = x
+        high, low = split(x)
+        for h in range(size // HEAD):
+            at = (i * (size // HEAD) + h) * 2 * HEAD
+            own = slice(h * HEAD, (h + 1) * HEAD)
+            x2_ref[:, at : at + HEAD] = high[:, own]
+            x2_ref[:, at + HEAD : at + 2 * HEAD] = low[:, own]
+    for i in range(chunks):
+        copies[1 + chunks + i].wait()
+        table = rows(held_g[i])
+        tz_ref[:, i * size : (i + 1) * size] = table * sigmoid(table)
+
+
+def tables(embedding, norm_gain, w_values, w_gates, w_states, w_steps, conv_values, conv_states):
     depth, width = w_values.shape
     heads = w_steps.shape[1]
-    steps = width // 256
-    state_blocks = w_states.shape[1] // 128
-    whole = lambda shape: pl.BlockSpec(shape, lambda i: (0, 0))
-    columns = lambda rows, size: pl.BlockSpec((rows, size), lambda i: (0, i))
-    states = lambda rows: pl.BlockSpec((rows, 128), lambda i: (0, jnp.minimum(i, state_blocks - 1)))
+    size = 256
+    chunks = width // size
+    vmem = pl.BlockSpec(memory_space=pltpu.VMEM)
+    hbm = pl.BlockSpec(memory_space=pl.ANY)
+    shapes = [
+        ((8, width), f32),
+        ((8, width), f32),
+        ((8, 2 * STATE), f32),
+        ((heads, IDS), f32),
+        ((WINDOWS, width), f32),
+        ((WINDOWS, 2 * width), bf16),
+        ((WINDOWS, 2 * STATE), f32),
+        ((WINDOWS, 2 * STATE), f32),
+    ]
     return pl.pallas_call(
         tables_kernel,
-        grid=(steps,),
-        in_specs=[
-            whole(embedding.shape),
-            whole((1, depth)),
-            columns(depth, 256),
-            columns(depth, 256),
-            states(depth),
-            whole((heads, depth)),
+        in_specs=[vmem] * 5 + [hbm] * 3,
+        out_specs=[vmem] * len(shapes),
+        out_shape=[jax.ShapeDtypeStruct(shape, kind) for shape, kind in shapes],
+        scratch_shapes=[
+            pltpu.VMEM((chunks, depth, size), bf16),
+            pltpu.VMEM((chunks, depth, size), bf16),
+            pltpu.VMEM((depth, 2 * STATE), bf16),
+            pltpu.SemaphoreType.DMA((1 + 2 * chunks,)),
         ],
-        out_specs=[columns(8, 256), columns(8, 256), states(8), whole((heads, IDS))],
-        out_shape=[
-            jax.ShapeDtypeStruct((8, width), f32),
-            jax.ShapeDtypeStruct((8, width), f32),
-            jax.ShapeDtypeStruct((8, w_states.shape[1]), f32),
-            jax.ShapeDtypeStruct((heads, IDS), f32),
-        ],
-        compiler_params=pltpu.CompilerParams(vmem_limit_bytes=24 * 2**20),
+        compiler_params=pltpu.CompilerParams(vmem_limit_bytes=56 * 2**20),
         name="tables",
-    )(embedding, norm_gain.reshape(1, depth), w_values, w_gates, w_states, w_steps.T)
+    )(embedding, norm_gain.reshape(1, depth), w_steps.T, conv_values, conv_states, w_values, w_gates, w_states)
 
 
 def mixer_kernel(
@@ -95,6 +168,10 @@
     tbc_ref,
     tz_ref,
     dt_ref,
+    xw_ref,
+    x2w_ref,
+    bc_ref,
+    slope_ref,
     cv_ref,
     cs_ref,
     bias_ref,
@@ -108,13 +185,11 @@
     count_s,
     onehot_s,
     weight_s,
-    x_s,
-    xh_s,
-    xl_s,
+    edge_s,
     wh_s,
     wl_s,
-    lh_s,
-    ll_s,
+    x_s,
+    x2_s,
     far_s,
     dh_s,
     dl_s,
@@ -233,9 +308,6 @@
     weights = mm(onehot_s[...], weight_s[...], NT)
     weights = weights + pltpu.roll(weights, 64, 1)
 
-    lane_w = iota((WINDOWS, 128), 1)
-    tap_w = (lane_w >> 3) & 3
-    digit = (iota((WINDOWS, 128), 0) >> (2 * tap_w)) & 3
     lane_e = iota((16, 128), 1)
     row_e = iota((16, 128), 0)
     tap_e = (lane_e >> 3) & 3
@@ -249,27 +321,20 @@
                 rtok[devices - 1 : devices, count - 1 - at : count - at],
                 edge,
             )
-    chosen = jnp.concatenate([digit, edge], axis=0)
-    lane_r = iota((ROWS, 128), 1)
-    pick = ((chosen == (lane_r & 7)) & (lane_r < 96)).astype(f32).astype(bf16)
-
-    def windows(table, taps_ref):
-        product = jnp.concatenate([taps_ref[k : k + 1, :] * table for k in range(CONV)], axis=0)
-        p1 = product.astype(bf16)
-        rest = product - p1.astype(f32)
-        p2 = rest.astype(bf16)
-        p3 = (rest - p2.astype(f32)).astype(bf16)
-        return mm(pick, jnp.concatenate([p1, p2, p3, jnp.zeros_like(p1)], axis=0))
-
-    summed = windows(tv_ref[...], cv_ref)
-    x_all = summed * sigmoid(summed)
-    x_s[...] = x_all
-    xh_s[...], xl_s[...] = split(x_all)
+    edge_pick = ((edge == (lane_e & 7)) & (lane_e < 96)).astype(f32).astype(bf16)
+    summed = windows(edge_pick, tv_ref[...], cv_ref[...])
+    edge_x = summed * sigmoid(summed)
+    edge_s[...] = edge_x
+    edge_high, edge_low = split(edge_x)
+    edge_x2 = []
+    for h in range(heads):
+        edge_x2 += [edge_high[:, h * HEAD : (h + 1) * HEAD], edge_low[:, h * HEAD : (h + 1) * HEAD]]
+    edge_x2 = jnp.concatenate(edge_x2, axis=1)
     table_bc = tbc_ref[...]
-    summed = windows(table_bc, cs_ref)
+    summed = windows(edge_pick, table_bc, cs_ref[...])
     sig = sigmoid(summed)
-    bc_all = summed * sig
-    bc_slope = sig * (1.0 + summed * (1.0 - sig))
+    bc_all = jnp.concatenate([bc_ref[...], summed * sig], axis=0)
+    bc_slope = jnp.concatenate([slope_ref[...], sig * (1.0 + summed * (1.0 - sig))], axis=0)
     bc = split(bc_all)
     b_all = (bc[0][:, :STATE], bc[1][:, :STATE])
 
@@ -303,7 +368,6 @@
     base = 4 * heads
     tcol_s[...] = jnp.broadcast_to(turned[:, base + 2 : base + 3], (count, 128))
     gates = tz_ref[...]
-    gates = gates * sigmoid(gates)
     gate_s[0] = gates
     for t in range(IDS):
         picked = gates[0:1, :]
@@ -318,61 +382,104 @@
     for s in range(2):
         picks = (lane_k == turned[:, base + s : base + s + 1]).astype(f32).astype(bf16)
         own_onehot.append((window_rows == own_ids[s]).astype(f32).astype(bf16))
-        lh_s[s] = mm(picks, xh_s[...]).astype(bf16)
-        ll_s[s] = mm(picks, xl_s[...]).astype(bf16)
-        own_bc.append((mm(picks, bc[0]).astype(bf16), mm(picks, bc[1]).astype(bf16)))
+        ends = slice(0, 16) if s == 0 else slice(count - 16, count)
+        pieces = []
+        for table, extra in ((x2w_ref[...], edge_x2), (bc[0][:WINDOWS], bc[0][WINDOWS:]), (bc[1][:WINDOWS], bc[1][WINDOWS:])):
+            got = mm(picks[:, :WINDOWS], table)
+            more = mm(picks[ends, WINDOWS:], extra)
+            if s == 0:
+                got = jnp.concatenate([got[:16] + more, got[16:]], axis=0)
+            else:
+                got = jnp.concatenate([got[: count - 16], got[count - 16 :] + more], axis=0)
+            pieces.append(got)
+        x2_s[s] = pieces[0].astype(bf16)
+        for h in range(heads):
+            at = 2 * h * HEAD
+            x_s[s, :, h * HEAD : (h + 1) * HEAD] = pieces[0][:, at : at + HEAD] + pieces[0][:, at + HEAD : at + 2 * HEAD]
+        own_bc.append((pieces[1].astype(bf16), pieces[2].astype(bf16)))
         own_b = tuple(part[:, :STATE] for part in own_bc[s])
         own_c = tuple(part[:, STATE:] for part in own_bc[s])
-        score_s[s] = mm3(own_c, own_b, NT)
+        twice_c = jnp.concatenate([own_c[0], own_c[0]], axis=1)
+        score_s[s] = mm(twice_c, jnp.concatenate(own_b, axis=1), NT) + mm(own_c[1], own_b[0], NT)
         for h in range(heads):
             at = 3 * s * heads + h
             columns = slice(h * HEAD, (h + 1) * HEAD)
-            weighted = split(x_s[:, columns] * weights[:, at : at + 1])
-            wh_s[s, :, columns], wl_s[s, :, columns] = weighted
-        states.append(split(mm3(b_all, (wh_s[s], wl_s[s]), TN)))
-        far_s[s] = mm3(own_c, states[s])
+            weighted = split(xw_ref[:, columns] * weights[:WINDOWS, at : at + 1])
+            wh_s[s, :WINDOWS, columns], wl_s[s, :WINDOWS, columns] = weighted
+            weighted = split(edge_s[:, columns] * weights[WINDOWS:, at : at + 1])
+            wh_s[s, WINDOWS:, columns], wl_s[s, WINDOWS:, columns] = weighted
+        regular, edges = slice(0, WINDOWS), slice(WINDOWS, ROWS)
+        state = mm3(tuple(part[regular] for part in b_all), (wh_s[s, regular], wl_s[s, regular]), TN)
+        state = state + mm(
+            jnp.concatenate([b_all[0][edges], b_all[0][edges], b_all[1][edges]], axis=0),
+            jnp.concatenate([wh_s[s, edges], wl_s[s, edges], wh_s[s, edges]], axis=0),
+            TN,
+        )
+        states.append(jnp.concatenate(split(state), axis=0))
+        far_s[s] = mm(twice_c, states[s]) + mm(own_c[1], states[s][:STATE])
 
     q_s[...] = jnp.zeros_like(q_s)
-    sub = iota((count, count), 0)
-    lan = iota((count, count), 1)
+    tiles = count // 128
+    triangle = [iota((128, 128), 0) >= iota((128, 128), 1), iota((128, 128), 0) <= iota((128, 128), 1)]
 
     def one_head(h, _):
         columns = pl.ds(pl.multiple_of(h * HEAD, HEAD), HEAD)
+        columns2 = pl.ds(pl.multiple_of(h * 2 * HEAD, 2 * HEAD), 2 * HEAD)
         gain = gain_ref[:, columns]
-        cot = cot_ref[:, columns].astype(f32) * scale * gain
-        tcol = tcol_s[...]
-        total_out = jnp.zeros((count, HEAD), f32)
+        skip = skip_ref[h]
+        outs = [None] * tiles
         rate_row = jnp.zeros((1, 128), f32)
         bias_row = jnp.zeros((1, 128), f32)
         for s in range(2):
-            lcol = lcol_s[s, h]
+            column_sums = [jnp.zeros((1, 128), f32) for _ in range(tiles)]
+            part = lambda j: slice(j * 128, (j + 1) * 128)
             log_row = row_s[s, 0, pl.ds(h, 1), :]
             step_row = row_s[s, 1, pl.ds(h, 1), :]
             mixed_row = row_s[s, 2, pl.ds(h, 1), :]
-            causal = (sub >= lan) if s == 0 else (sub <= lan)
-            wide = jnp.concatenate([lcol] * (count // 128), axis=1)
-            factor = jnp.exp(jnp.where(causal, wide - log_row, -1e30)) * step_row
-            mixing = score_s[s] * factor
-            x = (lh_s[s, :, columns], ll_s[s, :, columns])
-            grown = jnp.exp(lcol)
-            y = mm3(split(mixing), x) + grown * far_s[s, :, columns]
-            gate = gate_s[s, 0:1, columns]
-            for t in range(1, IDS):
-                gate = jnp.where(tcol == t, gate_s[s, t : t + 1, columns], gate)
-            gated = (y + skip_ref[h] * (x[0].astype(f32) + x[1].astype(f32))) * gate
-            inverse = lax.rsqrt(jnp.mean(gated * gated, axis=1, keepdims=True) + EPSILON)
-            total_out = total_out + gated * inverse * gain
-            shared = jnp.mean(cot * gated, axis=1, keepdims=True) * (inverse * inverse)
-            dy = (cot - gated * shared) * inverse * gate
-            e = mm3(split(dy), x, NT)
-            q_s[s] += e * factor
-            column_sum = jnp.sum(e * mixing, axis=0, keepdims=True)
-            row_terms = dy * y
-            fold = lambda v: sum(v[:, i * 128 : (i + 1) * 128] for i in range(count // 128))
-            rate_row += jnp.sum(lcol * row_terms, axis=0, keepdims=True) - fold(log_row * column_sum)
-            bias_row += jnp.sum(acol_s[s, h] * row_terms, axis=0, keepdims=True) + fold(mixed_row * column_sum)
-            dh_s[s, :, columns], dl_s[s, :, columns] = split(grown * dy)
-        enc_ref[:, columns] = total_out.astype(enc_ref.dtype)
+            for i in range(tiles):
+                near = range(0, i + 1) if s == 0 else range(i, tiles)
+                span = slice(near[0] * 128, (near[-1] + 1) * 128)
+                lcol = lcol_s[s, h, part(i), :]
+                factors = []
+                for j in near:
+                    gap = lcol - log_row[:, part(j)]
+                    if j == i:
+                        gap = jnp.where(triangle[s], gap, -1e30)
+                    factors.append(jnp.exp(gap) * step_row[:, part(j)])
+                factor = jnp.concatenate(factors, axis=1)
+                high, low = split(score_s[s, part(i), span] * factor)
+                x2 = x2_s[s, span, columns2]
+                y = mm(high, x2)
+                y = y[:, :HEAD] + (y[:, HEAD:] + mm(low, x2[:, :HEAD]))
+                grown = jnp.exp(lcol)
+                y = y + grown * far_s[s, part(i), columns]
+                tcol = tcol_s[part(i), :]
+                gate = gate_s[s, 0:1, columns]
+                for t in range(1, IDS):
+                    gate = jnp.where(tcol == t, gate_s[s, t : t + 1, columns], gate)
+                gated = (y + skip * x_s[s, part(i), columns]) * gate
+                inverse = lax.rsqrt(jnp.mean(gated * gated, axis=1, keepdims=True) + EPSILON)
+                normal = gated * inverse
+                outs[i] = normal if outs[i] is None else outs[i] + normal
+                cot = cot_ref[part(i), columns].astype(f32) * gain
+                shared = jnp.mean(cot * normal, axis=1, keepdims=True)
+                dy = (cot - normal * shared) * (inverse * gate)
+                high, low = split(dy)
+                e = mm(jnp.concatenate([high, high], axis=1), x2, NT) + mm(low, x2[:, :HEAD], NT)
+                e = e * factor
+                q_s[s, part(i), span] += e
+                e = e * score_s[s, part(i), span]
+                for n, j in enumerate(near):
+                    column_sums[j] = column_sums[j] + jnp.sum(e[:, part(n)], axis=0, keepdims=True)
+                row_terms = dy * y
+                rate_row += jnp.sum(lcol * row_terms, axis=0, keepdims=True)
+                bias_row += jnp.sum(acol_s[s, h, part(i), :] * row_terms, axis=0, keepdims=True)
+                dh_s[s, part(i), columns], dl_s[s, part(i), columns] = split(grown * dy)
+            for j in range(tiles):
+                rate_row -= log_row[:, part(j)] * column_sums[j]
+                bias_row += mixed_row[:, part(j)] * column_sums[j]
+        for i in range(tiles):
+            enc_ref[i * 128 : (i + 1) * 128, columns] = (outs[i] * gain).astype(enc_ref.dtype)
         acc_s[0, pl.ds(h, 1), :] = rate_row
         acc_s[1, pl.ds(h, 1), :] = bias_row
         return 0
@@ -381,34 +488,43 @@
 
     db_all = jnp.zeros((ROWS, STATE), f32)
     dc_all = jnp.zeros((ROWS, STATE), f32)
+    twice_b = jnp.concatenate([b_all[0], b_all[0]], axis=1)
     for s in range(2):
         own_b = tuple(part[:, :STATE] for part in own_bc[s])
         own_c = tuple(part[:, STATE:] for part in own_bc[s])
         q = split(q_s[s])
         grown = (dh_s[s], dl_s[s])
-        dc_own = split(mm3(q, own_b) + mm3(grown, states[s], NT))
+        far = mm(grown[0], states[s], NT)
+        far = far[:, :STATE] + (far[:, STATE:] + mm(grown[1], states[s][:STATE], NT))
+        dc_own = split(mm3(q, own_b) + far)
         db_own = split(mm3(q, own_c, TN))
-        back = split(mm3(own_c, grown, TN))
+        back = jnp.concatenate(split(mm3(own_c, grown, TN)), axis=0)
         dc_all = dc_all + (mm(own_onehot[s], dc_own[0]) + mm(own_onehot[s], dc_own[1]))
         db_all = db_all + (mm(own_onehot[s], db_own[0]) + mm(own_onehot[s], db_own[1]))
-        db_all = db_all + mm3((wh_s[s], wl_s[s]), back, NT)
-        reach = mm3(b_all, back)
+        far = mm(wh_s[s], back, NT)
+        db_all = db_all + (far[:, :STATE] + (far[:, STATE:] + mm(wl_s[s], back[:STATE], NT)))
+        reach = mm(twice_b, back) + mm(b_all[1], back[:STATE])
         for h in range(heads):
             at = 3 * s * heads + heads + h
             columns = slice(h * HEAD, (h + 1) * HEAD)
-            terms = reach[:, columns] * x_s[:, columns]
+            x = jnp.concatenate([xw_ref[:, columns], edge_s[:, columns]], axis=0)
+            terms = reach[:, columns] * x
             acc_s[0, h : h + 1, :] += jnp.sum(terms * weights[:, at : at + 1], axis=0, keepdims=True)
             acc_s[1, h : h + 1, :] += jnp.sum(
                 terms * weights[:, at + heads : at + heads + 1], axis=0, keepdims=True
             )
     d_summed = split(jnp.concatenate([db_all, dc_all], axis=1) * bc_slope)
+    lane_w = iota((WINDOWS, 128), 1)
+    digit = (iota((WINDOWS, 128), 0) >> (2 * ((lane_w >> 3) & 3))) & 3
+    pick = ((digit == (lane_w & 7)) & (lane_w < 32)).astype(f32).astype(bf16)
+    pick = jnp.concatenate([pick, edge_pick], axis=0)
     by_tap = mm(pick, d_summed[0], TN) + mm(pick, d_summed[1], TN)
     grad_ref[...] = jnp.zeros_like(grad_ref)
     for k in range(CONV):
-        grad_ref[k : k + 1, :] = jnp.sum(by_tap[8 * k : 8 * k + 8, :] * table_bc, axis=0, keepdims=True)
+        grad_ref[k : k + 1, :] = scale * jnp.sum(by_tap[8 * k : 8 * k + 8, :] * table_bc, axis=0, keepdims=True)
     place = iota((heads, 128), 1) == iota((heads, 128), 0) + tp_place * heads
     for i in range(2):
-        sums = jnp.sum(acc_s[i], axis=1, keepdims=True)
+        sums = scale * jnp.sum(acc_s[i], axis=1, keepdims=True)
         grad_ref[CONV + i : CONV + i + 1, 0:128] = jnp.sum(jnp.where(place, sums, 0.0), axis=0, keepdims=True)
 
 
@@ -416,7 +532,7 @@
     devices, count = tokens.shape
     width = conv_values.shape[1]
     heads = width // HEAD
-    tv, tz, tbc, dt = tabs
+    tv, tz, tbc, dt, x, x2, bc, slope = tabs
     vmem = pl.BlockSpec(memory_space=pltpu.VMEM)
     smem = pl.BlockSpec(memory_space=pltpu.SMEM)
     scratch = [
@@ -425,13 +541,11 @@
         ((IDS, devices, count), f32),
         ((ROWS, devices * count), bf16),
         ((128, devices * count), bf16),
-        ((ROWS, width), f32),
-        ((ROWS, width), bf16),
-        ((ROWS, width), bf16),
+        ((16, width), f32),
         ((2, ROWS, width), bf16),
         ((2, ROWS, width), bf16),
-        ((2, count, width), bf16),
-        ((2, count, width), bf16),
+        ((2, count, width), f32),
+        ((2, count, 2 * width), bf16),
         ((2, count, width), f32),
         ((2, count, width), bf16),
         ((2, count, width), bf16),
@@ -446,7 +560,7 @@
     ]
     return pl.pallas_call(
         functools.partial(mixer_kernel, scale),
-        in_specs=[vmem, smem, smem, smem] + [vmem] * 10,
+        in_specs=[vmem, smem, smem, smem] + [vmem] * 14,
         out_specs=[vmem, vmem],
         out_shape=[
             jax.ShapeDtypeStruct((count, width), bf16),
@@ -464,6 +578,10 @@
         tbc,
         tz,
         dt,
+        x,
+        x2,
+        bc,
+        slope,
         conv_values,
         conv_states,
         bias.reshape(1, heads),
@@ -497,12 +615,12 @@
 ):
     devices = lax.axis_size("ctx")
     count = tokens.shape[0]
-    everyone = tokens.reshape(1, count)
+    everyone = jnp.minimum(tokens, IDS - 1).reshape(1, count)
     distance = 1
     while distance < devices:
         everyone = jnp.concatenate([everyone, exchange(everyone, "ctx", distance)], axis=0)
         distance *= 2
-    tabs = tables(embedding, norm_gain, w_values, w_gates, w_states, w_steps)
+    tabs = tables(embedding, norm_gain, w_values, w_gates, w_states, w_steps, conv_values, conv_states)
     place = jnp.stack([lax.axis_index("ctx"), lax.axis_index("tp")]).astype(jnp.int32)
     scale = 1.0 / math.sqrt(count * devices * HEAD)
     encoded, grads = mixer(

time: 64.1 us -> 63.8 us (level)
  Pallas kernels: 24.3 us -> 27.9 us
  local copies, waits for them, and re-layouts: 8.93 us -> 5.95 us
  other arithmetic: 1.48 us -> 0.8 us
    pallas_call x1, Pallas kernels: 3.54 us -> 7.92 us  [tables(): pl.pallas_call(tables_kernel, in_specs=[vmem] * 5 + [hbm] * 3, out_specs=...]
    unnamed x30 -> x28, local copies, waits for them, and re-layouts: 7.82 us -> 4.83 us
    concatenate x3, other arithmetic: 1.39 us -> 0.03 us  [on_device(): jnp.concatenate([everyone, exchange(everyone, 'ctx', distance)], axis=0)]
    pallas_call x1, Pallas kernels: 20.7 us -> 19.9 us  [mixer(): pl.pallas_call(functools.partial(mixer_kernel, scale), in_specs=[vmem, sm...]
    min x0 -> x1, other arithmetic: none -> 0.68 us  [on_device(): everyone = jnp.minimum(tokens, IDS - 1).reshape(1, count)]
  transfers between devices with their start and end apart: 8 -> 8, of which waited for: 7 -> 7; matrix products, arithmetic and copies ran while one was open for 0% -> 0% of each run, Pallas kernels for 6% -> 12%
where the time goes in v1:
time: 63.8 us; the launch traced here: 63.4 us
  Pallas kernels  27.9 us (44%)
  waiting for transfers between devices  15.2 us (24%)
  starting transfers between devices  12.8 us (20%)
  local copies, waits for them, and re-layouts  5.95 us (9%)
  other arithmetic  0.8 us (1%)
  between operations  0.79 us (1%)
    pallas_call x1, Pallas kernels, mixer(): pl.pallas_call(functools.partial(mixer_kernel, scale), in_specs=[vmem, sm...  19.9 us
    ppermute x8, waiting for transfers between devices, exchange(): return lax.ppermute(value, axis, [(i, i ^ distance) for i in range(size)])  15.2 us
    ppermute x8, starting transfers between devices, exchange(): return lax.ppermute(value, axis, [(i, i ^ distance) for i in range(size)])  12.8 us
    pallas_call x1, Pallas kernels, tables(): pl.pallas_call(tables_kernel, in_specs=[vmem] * 5 + [hbm] * 3, out_specs=...  7.92 us
    unnamed x28, local copies, waits for them, and re-layouts  4.83 us
  transfers between devices with their start and end apart: 8, of which 7 were waited for; matrix products, arithmetic and copies ran while one was open for 0% of the time, Pallas kernels for 12%

profile of v1, /device:TPU:0, one launch (start us, length us, event | category | flops | bytes accessed | tf_op | source)
XLA Modules:
  0.0 63.4 jit_solution(17257214775846998090)
XLA Ops:
  0.6 0.7 %broadcast_minimum_fusion = s32[256]{0:T(256)S(1)} fusion(s32[256]{0:T(256)} %param.15), kind=kLoop, calls=%fused_computation.6 | loop fusion | flops 256 | bytes 2048 | tf_op jit(solution)/shard_map/min | solution.py:618
  1.3 2.9 %collective-permute-start = (s32[1,256]{1,0:T(1,128)S(1)}, s32[1,256]{1,0:T(1,128)S(1)}, u32[]{:S(2)}, u32[]{:S(2)}) collective-permute-start(s32[1,256]{1,0:T(1,128)S(1)} %bitcast.16), channel_id=1, source_target_pairs={{0,4},{4,0},{8,12},{12,8},{16,20},{20,16},{24,28},{28,24},{1,5},{5... | collective-permute-start | bytes 3080 | tf_op jit(solution)/shard_map/ppermute | solution.py:596
  4.3 1.5 %collective-permute-done = s32[1,256]{1,0:T(1,128)S(1)} collective-permute-done((s32[1,256]{1,0:T(1,128)S(1)}, s32[1,256]{1,0:T(1,128)S(1)}, u32[]{:S(2)}, u32[]{:S(2)}) %collective-permute-start) | collective-permute-done | bytes 1056 | tf_op jit(solution)/shard_map/ppermute | solution.py:596
  5.8 2.1 %collective-permute-start.1 = (s32[2,256]{1,0:T(2,128)S(1)}, s32[2,256]{1,0:T(2,128)S(1)}, u32[]{:S(2)}, u32[]{:S(2)}) collective-permute-start(s32[2,256]{1,0:T(2,128)S(1)} %pad_add_fusion.2), channel_id=1, source_target_pairs={{0,8},{4,12},{8,0},{12,4},{16,24},{20,28},{24,16},{28,20},{1,9},{5... | collective-permute-start | bytes 6152 | tf_op jit(solution)/shard_map/ppermute | solution.py:596
  7.9 1.6 %collective-permute-done.1 = s32[2,256]{1,0:T(2,128)S(1)} collective-permute-done((s32[2,256]{1,0:T(2,128)S(1)}, s32[2,256]{1,0:T(2,128)S(1)}, u32[]{:S(2)}, u32[]{:S(2)}) %collective-permute-start.1) | collective-permute-done | bytes 2080 | tf_op jit(solution)/shard_map/ppermute | solution.py:596
  9.5 3.1 %collective-permute-start.2 = (s32[4,256]{1,0:T(4,128)S(1)}, s32[4,256]{1,0:T(4,128)S(1)}, u32[]{:S(2)}, u32[]{:S(2)}) collective-permute-start(s32[4,256]{1,0:T(4,128)S(1)} %pad_add_fusion.1), channel_id=1, source_target_pairs={{0,16},{4,20},{8,24},{12,28},{16,0},{20,4},{24,8},{28,12},{1,17},{... | collective-permute-start | bytes 12296 | tf_op jit(solution)/shard_map/ppermute | solution.py:596
  12.6 0.1 pad_add_fusion.3.place_ref
  12.7 0.0 copy-start
  12.7 0.0 copy-start.3
  12.7 0.0 copy-start.6
  12.7 0.0 copy-start.8
  12.7 0.0 copy-start.10
  12.7 0.0 copy-start.11
  12.7 0.0 copy-start.12
  12.7 0.0 copy-start.13
  12.7 7.9 %tables.1 = (f32[8,1024]{1,0:T(8,128)}, f32[8,1024]{1,0:T(8,128)}, f32[8,256]{1,0:T(8,128)}, f32[8,4]{1,0:T(8,128)}, f32[256,1024]{1,0:T(8,128)}, /*index=5*/bf1...) custom-call(bf16[4,2048]{1,0:T(4,128)(2,1)} %emb_ref.1, f32[1,2048]{1,0:T(1,128)} %bitcast.20, ...), custom_call_target="tpu_custom_call" | custom-call | tf_op jit(solution)/shard_map/tables/pallas_call | solution.py:145
  20.6 0.0 collective-permute-done.2
  20.7 0.0 copy-done
  20.7 0.0 copy-done.3
  20.7 0.0 copy-done.6
  20.7 0.0 copy-done.8
  20.7 0.0 copy-done.10
  20.7 0.0 copy-done.11
  20.7 0.0 copy-done.12
  20.7 0.0 copy-done.13
  20.8 0.0 copy-start.1
  20.8 0.9 %copy-done.1 = f32[256,256]{1,0:T(8,128)S(1)} copy-done((f32[256,256]{1,0:T(8,128)S(1)}, f32[256,256]{1,0:T(8,128)}, u32[]{:S(2)}) %copy-start.1) | copy-done | bytes 262168
  21.7 0.0 copy-start.2
  21.7 0.9 %copy-done.2 = f32[256,256]{1,0:T(8,128)S(1)} copy-done((f32[256,256]{1,0:T(8,128)S(1)}, f32[256,256]{1,0:T(8,128)}, u32[]{:S(2)}) %copy-start.2) | copy-done | bytes 262168
  22.7 0.0 copy-start.4
  22.7 0.8 %copy-done.4 = f32[8,1024]{1,0:T(8,128)S(1)} copy-done((f32[8,1024]{1,0:T(8,128)S(1)}, f32[8,1024]{1,0:T(8,128)}, u32[]{:S(2)}) %copy-start.4) | copy-done | bytes 32792
  23.4 0.0 copy-start.5
  23.4 0.8 %copy-done.5 = f32[8,1024]{1,0:T(8,128)S(1)} copy-done((f32[8,1024]{1,0:T(8,128)S(1)}, f32[8,1024]{1,0:T(8,128)}, u32[]{:S(2)}) %copy-start.5) | copy-done | bytes 32792
  24.2 0.7 %copy-done.7 = f32[8,256]{1,0:T(8,128)S(1)} copy-done((f32[8,256]{1,0:T(8,128)S(1)}, f32[8,256]{1,0:T(8,128)}, u32[]{:S(2)}) %copy-start.7) | copy-done | bytes 8216
  24.9 0.7 %copy-done.9 = f32[8,4]{1,0:T(8,128)S(1)} copy-done((f32[8,4]{1,0:T(8,128)S(1)}, f32[8,4]{1,0:T(8,128)}, u32[]{:S(2)}) %copy-start.9) | copy-done | bytes 152
  25.6 19.9 %mixer.1 = (bf16[256,1024]{1,0:T(8,128)(2,1)}, f32[8,256]{1,0:T(8,128)S(1)}) custom-call(s32[8,256]{1,0:T(8,128)S(1)} %pad_add_fusion.tok_ref, s32[4]{0:T(128)S(1)} %copy-done.10, s32[2]{0:T(128)S(1)} %pad_add_fusion.3.place_ref, f32[8]{0:T(128)S(1)} %copy-done.11, f32[8,1024]{1,0:T(8,128)S(1)} %copy-done.4, f32[8,256]{1,0:T(8,128)S(1)} %copy-done.7, ...), custom_call_target="tpu_custom_call" | custom-call | tf_op jit(solution)/shard_map/mixer/pallas_call | solution.py:561
  45.5 0.1 collective-permute-start.3
  45.6 1.2 %collective-permute-done.3 = f32[8,256]{1,0:T(8,128)S(1)} collective-permute-done((f32[8,256]{1,0:T(8,128)S(1)}, f32[8,256]{1,0:T(8,128)S(1)}, u32[]{:S(2)}, u32[]{:S(2)}) %collective-permute-start.3) | collective-permute-done | bytes 8224 | tf_op jit(solution)/shard_map/ppermute | solution.py:596
  46.7 1.5 %collective-permute-start.4 = (f32[8,256]{1,0:T(8,128)S(1)}, f32[8,256]{1,0:T(8,128)S(1)}, u32[]{:S(2)}, u32[]{:S(2)}) collective-permute-start(f32[8,256]{1,0:T(8,128)S(1)} %add.15), channel_id=1, source_target_pairs={{0,2},{1,3},{2,0},{3,1},{4,6},{5,7},{6,4},{7,5},{8,10},{9,11},{10,... | collective-permute-start | bytes 24584 | tf_op jit(solution)/shard_map/ppermute | solution.py:596
  48.3 2.1 %collective-permute-done.4 = f32[8,256]{1,0:T(8,128)S(1)} collective-permute-done((f32[8,256]{1,0:T(8,128)S(1)}, f32[8,256]{1,0:T(8,128)S(1)}, u32[]{:S(2)}, u32[]{:S(2)}) %collective-permute-start.4) | collective-permute-done | bytes 8224 | tf_op jit(solution)/shard_map/ppermute | solution.py:596
  50.4 1.5 %collective-permute-start.5 = (f32[8,256]{1,0:T(8,128)S(1)}, f32[8,256]{1,0:T(8,128)S(1)}, u32[]{:S(2)}, u32[]{:S(2)}) collective-permute-start(f32[8,256]{1,0:T(8,128)S(1)} %add.16), channel_id=1, source_target_pairs={{0,4},{4,0},{8,12},{12,8},{16,20},{20,16},{24,28},{28,24},{1,5},{5... | collective-permute-start | bytes 24584 | tf_op jit(solution)/shard_map/ppermute | solution.py:596
  51.9 2.2 %collective-permute-done.5 = f32[8,256]{1,0:T(8,128)S(1)} collective-permute-done((f32[8,256]{1,0:T(8,128)S(1)}, f32[8,256]{1,0:T(8,128)S(1)}, u32[]{:S(2)}, u32[]{:S(2)}) %collective-permute-start.5) | collective-permute-done | bytes 8224 | tf_op jit(solution)/shard_map/ppermute | solution.py:596
  54.1 1.6 %collective-permute-start.6 = (f32[8,256]{1,0:T(8,128)S(1)}, f32[8,256]{1,0:T(8,128)S(1)}, u32[]{:S(2)}, u32[]{:S(2)}) collective-permute-start(f32[8,256]{1,0:T(8,128)S(1)} %add.17), channel_id=1, source_target_pairs={{0,8},{4,12},{8,0},{12,4},{16,24},{20,28},{24,16},{28,20},{1,9},{5... | collective-permute-start | bytes 24584 | tf_op jit(solution)/shard_map/ppermute | solution.py:596
  55.6 2.1 %collective-permute-done.6 = f32[8,256]{1,0:T(8,128)S(1)} collective-permute-done((f32[8,256]{1,0:T(8,128)S(1)}, f32[8,256]{1,0:T(8,128)S(1)}, u32[]{:S(2)}, u32[]{:S(2)}) %collective-permute-start.6) | collective-permute-done | bytes 8224 | tf_op jit(solution)/shard_map/ppermute | solution.py:596
  57.7 0.0 collective-permute-start.7
  57.7 4.5 %collective-permute-done.7 = f32[8,256]{1,0:T(8,128)S(1)} collective-permute-done((f32[8,256]{1,0:T(8,128)S(1)}, f32[8,256]{1,0:T(8,128)S(1)}, u32[]{:S(2)}, u32[]{:S(2)}) %collective-permute-start.7) | collective-permute-done | bytes 8224 | tf_op jit(solution)/shard_map/ppermute | solution.py:596
  62.3 0.5 slice_bitcast_fusion
  62.8 0.6 slice.14
  (10 shorter events, 0.0 us)
Async XLA Ops:
  1.3 4.5 %collective-permute-start = (s32[1,256]{1,0:T(1,128)S(1)}, s32[1,256]{1,0:T(1,128)S(1)}, u32[]{:S(2)}, u32[]{:S(2)}) collective-permute-start(s32[1,256]{1,0:T(1,128)S(1)} %bitcast.16), channel_id=1, source_target_pairs={{0,4},{4,0},{8,12},{12,8},{16,20},{20,16},{24,28},{28,24},{1,5},{5... | collective-permute-start | bytes 3080 | tf_op jit(solution)/shard_map/ppermute | solution.py:596
  5.8 3.7 %collective-permute-start.1 = (s32[2,256]{1,0:T(2,128)S(1)}, s32[2,256]{1,0:T(2,128)S(1)}, u32[]{:S(2)}, u32[]{:S(2)}) collective-permute-start(s32[2,256]{1,0:T(2,128)S(1)} %pad_add_fusion.2), channel_id=1, source_target_pairs={{0,8},{4,12},{8,0},{12,4},{16,24},{20,28},{24,16},{28,20},{1,9},{5... | collective-permute-start | bytes 6152 | tf_op jit(solution)/shard_map/ppermute | solution.py:596
  9.5 11.2 %collective-permute-start.2 = (s32[4,256]{1,0:T(4,128)S(1)}, s32[4,256]{1,0:T(4,128)S(1)}, u32[]{:S(2)}, u32[]{:S(2)}) collective-permute-start(s32[4,256]{1,0:T(4,128)S(1)} %pad_add_fusion.1), channel_id=1, source_target_pairs={{0,16},{4,20},{8,24},{12,28},{16,0},{20,4},{24,8},{28,12},{1,17},{... | collective-permute-start | bytes 12296 | tf_op jit(solution)/shard_map/ppermute | solution.py:596
  12.7 8.0 %copy-start = (bf16[256,1024]{1,0:T(8,128)(2,1)S(1)}, bf16[256,1024]{1,0:T(8,128)(2,1)}, u32[]{:S(2)}) copy-start(bf16[256,1024]{1,0:T(8,128)(2,1)} %cot_ref.1) | copy-start | bytes 1572868
  12.7 8.0 %copy-start.3 = (f32[4,1024]{1,0:T(4,128)S(1)}, f32[4,1024]{1,0:T(4,128)}, u32[]{:S(2)}) copy-start(f32[4,1024]{1,0:T(4,128)} %cv_ref.3) | copy-start | bytes 49156
  12.7 8.0 %copy-start.6 = (f32[4,256]{1,0:T(4,128)S(1)}, f32[4,256]{1,0:T(4,128)}, u32[]{:S(2)}) copy-start(f32[4,256]{1,0:T(4,128)} %cs_ref.3) | copy-start | bytes 12292
  12.7 8.0 %copy-start.8 = (f32[1024]{0:T(1024)S(1)}, f32[1024]{0:T(1024)}, u32[]{:S(2)}) copy-start(f32[1024]{0:T(1024)} %param.28) | copy-start | bytes 12292
  12.7 8.1 %copy-start.10 = (s32[4]{0:T(128)S(1)}, s32[4]{0:T(128)}, u32[]{:S(2)}) copy-start(s32[4]{0:T(128)} %rc_ref.1) | copy-start | bytes 52
  12.7 8.0 %copy-start.11 = (f32[8]{0:T(128)S(1)}, f32[8]{0:T(128)}, u32[]{:S(2)}) copy-start(f32[8]{0:T(128)} %skip_ref.1) | copy-start | bytes 100
  12.7 8.0 %copy-start.12 = (f32[8]{0:T(128)S(1)}, f32[8]{0:T(128)}, u32[]{:S(2)}) copy-start(f32[8]{0:T(128)} %param.25) | copy-start | bytes 100
  12.7 8.0 %copy-start.13 = (f32[8]{0:T(128)S(1)}, f32[8]{0:T(128)}, u32[]{:S(2)}) copy-start(f32[8]{0:T(128)} %param.26) | copy-start | bytes 100
  20.8 1.0 %copy-start.1 = (f32[256,256]{1,0:T(8,128)S(1)}, f32[256,256]{1,0:T(8,128)}, u32[]{:S(2)}) copy-start(f32[256,256]{1,0:T(8,128)} %get-tuple-element.20.bc_ref) | copy-start | bytes 786436
  21.7 0.9 %copy-start.2 = (f32[256,256]{1,0:T(8,128)S(1)}, f32[256,256]{1,0:T(8,128)}, u32[]{:S(2)}) copy-start(f32[256,256]{1,0:T(8,128)} %get-tuple-element.21.slope_ref) | copy-start | bytes 786436
  22.7 0.8 %copy-start.4 = (f32[8,1024]{1,0:T(8,128)S(1)}, f32[8,1024]{1,0:T(8,128)}, u32[]{:S(2)}) copy-start(f32[8,1024]{1,0:T(8,128)} %get-tuple-element.14.tv_ref) | copy-start | bytes 98308
  23.4 0.8 %copy-start.5 = (f32[8,1024]{1,0:T(8,128)S(1)}, f32[8,1024]{1,0:T(8,128)}, u32[]{:S(2)}) copy-start(f32[8,1024]{1,0:T(8,128)} %get-tuple-element.16.tz_ref) | copy-start | bytes 98308
  24.2 0.7 %copy-start.7 = (f32[8,256]{1,0:T(8,128)S(1)}, f32[8,256]{1,0:T(8,128)}, u32[]{:S(2)}) copy-start(f32[8,256]{1,0:T(8,128)} %get-tuple-element.15.tbc_ref) | copy-start | bytes 24580
  24.9 0.7 %copy-start.9 = (f32[8,4]{1,0:T(8,128)S(1)}, f32[8,4]{1,0:T(8,128)}, u32[]{:S(2)}) copy-start(f32[8,4]{1,0:T(8,128)} %get-tuple-element.17.dt_ref) | copy-start | bytes 388
  45.5 1.2 %collective-permute-start.3 = (f32[8,256]{1,0:T(8,128)S(1)}, f32[8,256]{1,0:T(8,128)S(1)}, u32[]{:S(2)}, u32[]{:S(2)}) collective-permute-start(f32[8,256]{1,0:T(8,128)S(1)} %get-tuple-element.23), channel_id=1, source_target_pairs={{0,1},{1,0},{2,3},{3,2},{4,5},{5,4},{6,7},{7,6},{8,9},{9,8},{10,11... | collective-permute-start | bytes 24584 | tf_op jit(solution)/shard_map/ppermute | solution.py:596
  46.7 3.7 %collective-permute-start.4 = (f32[8,256]{1,0:T(8,128)S(1)}, f32[8,256]{1,0:T(8,128)S(1)}, u32[]{:S(2)}, u32[]{:S(2)}) collective-permute-start(f32[8,256]{1,0:T(8,128)S(1)} %add.15), channel_id=1, source_target_pairs={{0,2},{1,3},{2,0},{3,1},{4,6},{5,7},{6,4},{7,5},{8,10},{9,11},{10,... | collective-permute-start | bytes 24584 | tf_op jit(solution)/shard_map/ppermute | solution.py:596
  50.4 3.7 %collective-permute-start.5 = (f32[8,256]{1,0:T(8,128)S(1)}, f32[8,256]{1,0:T(8,128)S(1)}, u32[]{:S(2)}, u32[]{:S(2)}) collective-permute-start(f32[8,256]{1,0:T(8,128)S(1)} %add.16), channel_id=1, source_target_pairs={{0,4},{4,0},{8,12},{12,8},{16,20},{20,16},{24,28},{28,24},{1,5},{5... | collective-permute-start | bytes 24584 | tf_op jit(solution)/shard_map/ppermute | solution.py:596
  54.1 3.7 %collective-permute-start.6 = (f32[8,256]{1,0:T(8,128)S(1)}, f32[8,256]{1,0:T(8,128)S(1)}, u32[]{:S(2)}, u32[]{:S(2)}) collective-permute-start(f32[8,256]{1,0:T(8,128)S(1)} %add.17), channel_id=1, source_target_pairs={{0,8},{4,12},{8,0},{12,4},{16,24},{20,28},{24,16},{28,20},{1,9},{5... | collective-permute-start | bytes 24584 | tf_op jit(solution)/shard_map/ppermute | solution.py:596
  57.7 4.5 %collective-permute-start.7 = (f32[8,256]{1,0:T(8,128)S(1)}, f32[8,256]{1,0:T(8,128)S(1)}, u32[]{:S(2)}, u32[]{:S(2)}) collective-permute-start(f32[8,256]{1,0:T(8,128)S(1)} %add.18), channel_id=1, source_target_pairs={{0,16},{4,20},{8,24},{12,28},{16,0},{20,4},{24,8},{28,12},{1,17},{... | collective-permute-start | bytes 24584 | tf_op jit(solution)/shard_map/ppermute | solution.py:596

commit v2 on v0

v2 whole, which is shorter than its diff:
```python
import functools
import math

import jax
import jax.numpy as jnp
from jax import lax
from jax.experimental import pallas as pl
from jax.experimental.pallas import tpu as pltpu
from jax.sharding import PartitionSpec as P

HEAD = 128
STATE = 128
CONV = 4
IDS = 4
WINDOWS = IDS**CONV
ROWS = WINDOWS + 16
UNROLL = 2
EPSILON = 1e-05

f32 = jnp.float32
bf16 = jnp.bfloat16
NN = (((1,), (0,)), ((), ()))
NT = (((1,), (1,)), ((), ()))
TN = (((0,), (0,)), ((), ()))


def iota(shape, dim):
    return lax.broadcasted_iota(jnp.int32, shape, dim)


def mm(a, b, dims=NN):
    return lax.dot_general(a, b, dims, preferred_element_type=f32)


def split(x):
    high = x.astype(bf16)
    return high, (x - high.astype(f32)).astype(bf16)


def mm3(a, b, dims=NN):
    return mm(a[0], b[0], dims) + (mm(a[0], b[1], dims) + mm(a[1], b[0], dims))


def rows_of(parts):
    return jnp.concatenate(parts, axis=0)


def lanes_of(parts):
    return jnp.concatenate(parts, axis=1)


def stacked(a, b2, dims=NN):
    count = a[0].shape[0]
    both = mm(rows_of([lanes_of([a[0], a[0]]), lanes_of([a[1], a[1]])]), b2, dims)
    return both[:count] + both[count:]


def stacked_out(a, b2, width, dims=NN):
    count = a[0].shape[0]
    both = mm(rows_of([a[0], a[1]]), b2, dims)
    both = both[:count] + both[count:]
    return both[:, :width] + both[:, width:]


def sigmoid(v):
    return 1.0 / (1.0 + jnp.exp(-v))


def tap_parts(table, taps):
    product = rows_of([taps[k : k + 1, :] * table for k in range(CONV)])
    p1 = product.astype(bf16)
    rest = product - p1.astype(f32)
    p2 = rest.astype(bf16)
    p3 = (rest - p2.astype(f32)).astype(bf16)
    return rows_of([p1, p2, p3, jnp.zeros_like(p1)])


def mixer_kernel(
    scale,
    near_ref,
    far_ref,
    rc_ref,
    skip_ref,
    emb_ref,
    norm_gain_ref,
    wt_ref,
    cv_ref,
    cs_ref,
    bias_ref,
    rate_ref,
    gain_ref,
    wv_hbm,
    wg_hbm,
    ws_hbm,
    cot_hbm,
    enc_hbm,
    grad_ref,
    held_v,
    held_g,
    held_s,
    sems,
    enc_ref,
    enc_sem,
    tok_s,
    ids_s,
    count_s,
    onehot_s,
    weight_s,
    cot_s,
    cot_sem,
    xw_s,
    x2w_s,
    edge_s,
    wh_s,
    wl_s,
    x_s,
    x2_s,
    far_s,
    dh_s,
    dl_s,
    row_s,
    lcol_s,
    acol_s,
    tcol_s,
    gate_s,
    score_s,
    q_s,
    acc_s,
):
    devices, count = tok_s.shape
    width = cv_ref.shape[1]
    heads = width // HEAD
    here = lax.axis_index("ctx")
    tp_place = lax.axis_index("tp")
    chunks, size, _ = held_v.shape
    rows_at = lambda i: pl.ds(i * size, size)
    copies = [pltpu.make_async_copy(ws_hbm, held_s, sems.at[0])]
    for i in range(chunks):
        copies.append(pltpu.make_async_copy(wv_hbm.at[rows_at(i), :], held_v.at[i], sems.at[1 + i]))
    for i in range(chunks):
        copies.append(pltpu.make_async_copy(wg_hbm.at[rows_at(i), :], held_g.at[i], sems.at[1 + chunks + i]))
    for copy in copies:
        copy.start()

    cot_copy = pltpu.make_async_copy(cot_hbm, cot_s, cot_sem)
    cot_copy.start()

    half = near_ref.shape[0]
    for r in range(devices):
        own = near_ref[r : r + 1, :] if r < half else far_ref[r - half : r - half + 1, :]
        tok_s[pl.ds(jnp.bitwise_xor(here, r), 1), :] = own
    tok = tok_s[...]
    rc = [rc_ref[t] for t in range(IDS)]
    rtok = jnp.zeros_like(tok)
    for t in range(IDS):
        rtok = jnp.where(tok == t, rc[t], rtok)
    lane = iota((devices, count), 1)
    row = iota((devices, count), 0)

    def before(ids, shift):
        turned = pltpu.roll(ids, shift, 1)
        return jnp.where(lane < shift, pltpu.roll(turned, 1, 0), turned)

    def after(ids, shift):
        turned = pltpu.roll(ids, count - shift, 1)
        return jnp.where(lane >= count - shift, pltpu.roll(turned, devices - 1, 0), turned)

    kf = before(tok, 3) + IDS * before(tok, 2) + IDS**2 * before(tok, 1) + IDS**3 * tok
    kr = after(rtok, 3) + IDS * after(rtok, 2) + IDS**2 * after(rtok, 1) + IDS**3 * rtok
    first = row * count + lane
    last = devices * count - 1 - first
    kf = jnp.where(first < CONV - 1, WINDOWS + first, kf)
    kr = jnp.where(last < CONV - 1, WINDOWS + CONV - 1 + last, kr)
    ids_s[0] = kf
    ids_s[1] = kr

    embedded = emb_ref[...].astype(f32)
    mean = jnp.mean(embedded * embedded, axis=1, keepdims=True)
    normed = (embedded * lax.rsqrt(mean + EPSILON) * norm_gain_ref[...]).astype(bf16)
    eye = iota((heads, heads), 0) == iota((heads, heads), 1)
    column = lambda ref: jnp.sum(jnp.where(eye, ref[...], 0.0), axis=1, keepdims=True)
    raw = mm(wt_ref[...], normed, NT) + column(bias_ref)
    rate = jnp.exp(column(rate_ref))
    step = jnp.maximum(raw, 0.0) + jnp.log1p(jnp.exp(-jnp.abs(raw)))
    slope = sigmoid(raw)
    ratio = jnp.where(step > 1e-37, slope / jnp.maximum(step, 1e-37), 1.0)

    def per_strand(table):
        own = [table[:, t : t + 1] for t in range(IDS)]
        mapped = []
        for t in range(IDS):
            picked = own[0]
            for other in range(1, IDS):
                picked = jnp.where(rc[t] == other, own[other], picked)
            mapped.append(picked)
        return own, mapped

    step_of, slope_of, ratio_of = per_strand(step), per_strand(slope), per_strand(ratio)
    log_of, alog_of = per_strand(-rate * step), per_strand(-rate * slope)

    masks = [(tok == t).astype(f32) for t in range(IDS)]
    upper = (iota((count, count), 0) <= iota((count, count), 1)).astype(bf16)
    for t in range(IDS):
        count_s[t] = mm(masks[t].astype(bf16), upper)
    totals = [jnp.sum(m, axis=1, keepdims=True) for m in masks]
    row1 = iota((devices, 1), 0)
    far_counts = []
    for t in range(IDS):
        between = jnp.zeros((devices, 1), f32)
        for j in range(devices):
            inside = ((row1 < j) & (j < here)) | ((row1 > j) & (j > here))
            between = between + jnp.where(inside, totals[t][j : j + 1, :], 0.0)
        inclusive = count_s[t]
        far_counts.append(
            jnp.where(row < here, totals[t] - inclusive, inclusive - masks[t]) + between
        )

    window_rows = iota((ROWS, count), 0)
    def earlier(j):
        forward = j < here
        reverse = j > here
        choose = lambda pair, t: jnp.where(forward, pair[0][t], pair[1][t])
        tok_j = tok[j : j + 1, :]
        log_sum = jnp.zeros((heads, count), f32)
        alog_sum = jnp.zeros((heads, count), f32)
        step_j = jnp.zeros((heads, count), f32)
        slope_j = jnp.zeros((heads, count), f32)
        for t in range(IDS):
            number = far_counts[t][j : j + 1, :]
            log_sum = log_sum + choose(log_of, t) * number
            alog_sum = alog_sum + choose(alog_of, t) * number
            step_j = jnp.where(tok_j == t, choose(step_of, t), step_j)
            slope_j = jnp.where(tok_j == t, choose(slope_of, t), slope_j)
        decay = jnp.exp(log_sum)
        weight = decay * step_j
        terms = jnp.concatenate([weight, weight * log_sum, decay * (slope_j + step_j * alog_sum)], axis=0)
        both = jnp.concatenate(
            [
                jnp.where(forward, terms, 0.0),
                jnp.where(reverse, terms, 0.0),
                jnp.zeros((64 - 6 * heads, count), f32),
            ],
            axis=0,
        )
        high, low = split(both)
        weight_s[0:64, j * count : (j + 1) * count] = high
        weight_s[64:128, j * count : (j + 1) * count] = low
        window_j = jnp.where(forward, kf[j : j + 1, :], kr[j : j + 1, :])
        onehot_s[:, j * count : (j + 1) * count] = (window_rows == window_j).astype(bf16)

    blank = lambda size: jnp.zeros((8 - IDS, size), f32)
    copies[0].wait()
    product = mm(normed, held_s[...])
    table_bc = rows_of([product, blank(product.shape[1])])
    product = None
    for i in range(chunks):
        copies[1 + i].wait()
        term = mm(normed[:, i * size : (i + 1) * size], held_v[i])
        product = term if product is None else product + term
        for j in range(i * devices // chunks, (i + 1) * devices // chunks):
            earlier(j)
    taps_v = tap_parts(rows_of([product, blank(width)]), cv_ref[...])
    taps_s = tap_parts(table_bc, cs_ref[...])
    product = None
    for i in range(chunks):
        copies[1 + chunks + i].wait()
        term = mm(normed[:, i * size : (i + 1) * size], held_g[i])
        product = term if product is None else product + term
    gates = rows_of([product, blank(width)])
    gates = gates * sigmoid(gates)

    weights = mm(onehot_s[...], weight_s[...], NT)
    weights = weights + pltpu.roll(weights, 64, 1)

    lane_w = iota((WINDOWS, 128), 1)
    digit = (iota((WINDOWS, 128), 0) >> (2 * ((lane_w >> 3) & 3))) & 3
    pick = ((digit == (lane_w & 7)) & (lane_w < 96)).astype(f32).astype(bf16)
    for h in range(0, heads, 2):
        columns = slice(h * HEAD, (h + 2) * HEAD)
        summed = mm(pick, taps_v[:, columns])
        x = summed * sigmoid(summed)
        xw_s[:, columns] = x
        high, low = split(x)
        for i in range(2):
            at = 2 * (h + i) * HEAD
            own = slice(i * HEAD, (i + 1) * HEAD)
            x2w_s[:, at : at + HEAD] = high[:, own]
            x2w_s[:, at + HEAD : at + 2 * HEAD] = low[:, own]

    lane_e = iota((16, 128), 1)
    row_e = iota((16, 128), 0)
    tap_e = (lane_e >> 3) & 3
    edge = jnp.full((16, 128), IDS, jnp.int32)
    for u in range(CONV - 1):
        for k in range(CONV - 1 - u, CONV):
            at = u - (CONV - 1) + k
            edge = jnp.where((row_e == u) & (tap_e == k), tok[0:1, at : at + 1], edge)
            edge = jnp.where(
                (row_e == CONV - 1 + u) & (tap_e == k),
                rtok[devices - 1 : devices, count - 1 - at : count - at],
                edge,
            )
    edge_pick = ((edge == (lane_e & 7)) & (lane_e < 96)).astype(f32).astype(bf16)
    summed = mm(edge_pick, taps_v)
    edge_x = summed * sigmoid(summed)
    edge_s[...] = edge_x
    edge_high, edge_low = split(edge_x)
    edge_x2 = []
    for h in range(heads):
        edge_x2 += [edge_high[:, h * HEAD : (h + 1) * HEAD], edge_low[:, h * HEAD : (h + 1) * HEAD]]
    edge_x2 = jnp.concatenate(edge_x2, axis=1)
    pick = rows_of([pick, edge_pick])
    summed = mm(pick, taps_s)
    sig = sigmoid(summed)
    bc_all = summed * sig
    bc_slope = sig * (1.0 + summed * (1.0 - sig))
    bc = split(bc_all)
    b_all = (bc[0][:, :STATE], bc[1][:, :STATE])

    own_tok = tok_s[pl.ds(here, 1), :]
    own_masks = [(own_tok == t).astype(f32) for t in range(IDS)]
    own_counts = [[], []]
    for t in range(IDS):
        inclusive = count_s[t, pl.ds(here, 1), :]
        total = jnp.sum(own_masks[t], axis=1, keepdims=True)
        own_counts[0].append(inclusive)
        own_counts[1].append(total - inclusive + own_masks[t])
    turned = []
    for s in range(2):
        logs = sum(log_of[s][t] * own_counts[s][t] for t in range(IDS))
        alogs = sum(alog_of[s][t] * own_counts[s][t] for t in range(IDS))
        row_s[s, 0] = logs
        row_s[s, 1] = sum(step_of[s][t] * own_masks[t] for t in range(IDS))
        row_s[s, 2] = sum(ratio_of[s][t] * own_masks[t] for t in range(IDS)) - alogs
        turned += [logs, alogs]
    own_ids = [ids_s[s, pl.ds(here, 1), :] for s in range(2)]
    extra = jnp.concatenate(
        [own_ids[0].astype(f32), own_ids[1].astype(f32), own_tok.astype(f32), jnp.zeros((5, count), f32)],
        axis=0,
    )
    turned = jnp.concatenate(turned + [extra, jnp.zeros((120 - 4 * heads, count), f32)], axis=0).T
    for s in range(2):
        for h in range(heads):
            at = 2 * s * heads + h
            lcol_s[s, h] = jnp.broadcast_to(turned[:, at : at + 1], (count, 128))
            acol_s[s, h] = jnp.broadcast_to(turned[:, at + heads : at + heads + 1], (count, 128))
    base = 4 * heads
    tcol_s[...] = jnp.broadcast_to(turned[:, base + 2 : base + 3], (count, 128))
    gate_s[0] = gates
    for t in range(IDS):
        picked = gates[0:1, :]
        for other in range(1, IDS):
            picked = jnp.where(rc[t] == other, gates[other : other + 1, :], picked)
        gate_s[1, t : t + 1, :] = picked

    own_onehot = []
    lane_k = iota((count, ROWS), 1).astype(f32)
    picks = []
    for s in range(2):
        picks.append((lane_k == turned[:, base + s : base + s + 1]).astype(f32).astype(bf16))
        own_onehot.append((window_rows == own_ids[s]).astype(f32).astype(bf16))
    regular, edges = slice(0, WINDOWS), slice(WINDOWS, ROWS)
    both_picks = rows_of([picks[0][:, regular], picks[1][:, regular]])
    edge_picks = rows_of([picks[0][:16, edges], picks[1][count - 16 :, edges]])

    def gather(table, extra):
        got = mm(both_picks, table)
        more = mm(edge_picks, extra)
        return [
            rows_of([got[:16] + more[:16], got[16:count]]),
            rows_of([got[count : 2 * count - 16], got[2 * count - 16 :] + more[16:]]),
        ]

    for h in range(heads):
        columns = slice(2 * h * HEAD, 2 * (h + 1) * HEAD)
        for s, got in enumerate(gather(x2w_s[:, columns], edge_x2[:, columns])):
            x2_s[s, :, columns] = got.astype(bf16)
            x_s[s, :, h * HEAD : (h + 1) * HEAD] = got[:, :HEAD] + got[:, HEAD:]
    bc_high = gather(bc[0][regular], bc[0][edges])
    bc_low = gather(bc[1][regular], bc[1][edges])
    own_b, own_c, states = [], [], []
    for s in range(2):
        high, low = bc_high[s].astype(bf16), bc_low[s].astype(bf16)
        own_b.append((high[:, :STATE], low[:, :STATE]))
        own_c.append((high[:, STATE:], low[:, STATE:]))
        score_s[s] = stacked(own_c[s], lanes_of(own_b[s]), NT)
        for h in range(heads):
            at = 3 * s * heads + h
            columns = slice(h * HEAD, (h + 1) * HEAD)
            weighted = split(xw_s[:, columns] * weights[:WINDOWS, at : at + 1])
            wh_s[s, :WINDOWS, columns], wl_s[s, :WINDOWS, columns] = weighted
            weighted = split(edge_s[:, columns] * weights[WINDOWS:, at : at + 1])
            wh_s[s, WINDOWS:, columns], wl_s[s, WINDOWS:, columns] = weighted
        b2 = lanes_of([part[regular] for part in b_all])
        state = mm(b2, wh_s[s, regular], TN)
        state = state[:STATE] + state[STATE:] + mm(b2[:, :STATE], wl_s[s, regular], TN)
        state = state + mm(
            rows_of([b_all[0][edges], b_all[0][edges], b_all[1][edges]]),
            rows_of([wh_s[s, edges], wl_s[s, edges], wh_s[s, edges]]),
            TN,
        )
        states.append(rows_of(split(state)))
        far_s[s] = stacked(own_c[s], states[s])

    cot_copy.wait()
    q_s[...] = jnp.zeros_like(q_s)
    tiles = count // 128
    triangle = [iota((128, 128), 0) >= iota((128, 128), 1), iota((128, 128), 0) <= iota((128, 128), 1)]

    nothing = jnp.zeros((128, 128), bf16)
    part = lambda j: slice(j * 128, (j + 1) * 128)

    def one_head(h, _):
        columns = pl.ds(pl.multiple_of(h * HEAD, HEAD), HEAD)
        columns2 = pl.ds(pl.multiple_of(h * 2 * HEAD, 2 * HEAD), 2 * HEAD)
        gain = gain_ref[:, columns]
        skip = skip_ref[h]
        outs = [None] * tiles
        rate_row = jnp.zeros((1, 128), f32)
        bias_row = jnp.zeros((1, 128), f32)
        factors, ys = [], []
        for s in range(2):
            log_row = row_s[s, 0, pl.ds(h, 1), :]
            step_row = row_s[s, 1, pl.ds(h, 1), :]
            highs, lows, own = [], [], {}
            for i in range(tiles):
                lcol = lcol_s[s, h, part(i), :]
                high_row, low_row = [], []
                for j in range(tiles):
                    if (j > i) if s == 0 else (j < i):
                        high, low = nothing, nothing
                    else:
                        gap = lcol - log_row[:, part(j)]
                        if j == i:
                            gap = jnp.where(triangle[s], gap, -1e30)
                        own[i, j] = jnp.exp(gap) * step_row[:, part(j)]
                        high, low = split(score_s[s, part(i), part(j)] * own[i, j])
                    high_row.append(high)
                    low_row.append(low)
                highs.append(lanes_of(high_row))
                lows.append(lanes_of(low_row))
            factors.append(own)
            both = mm(rows_of(highs + lows), x2_s[s, :, columns2])
            both = both[:count] + both[count:]
            ys.append(both[:, :HEAD] + both[:, HEAD:])
        for s in range(2):
            column_sums = [jnp.zeros((1, 128), f32) for _ in range(tiles)]
            log_row = row_s[s, 0, pl.ds(h, 1), :]
            mixed_row = row_s[s, 2, pl.ds(h, 1), :]
            highs, lows = [], []
            for i in range(tiles):
                lcol = lcol_s[s, h, part(i), :]
                grown = jnp.exp(lcol)
                y = ys[s][part(i)] + grown * far_s[s, part(i), columns]
                tcol = tcol_s[part(i), :]
                gate = gate_s[s, 0:1, columns]
                for t in range(1, IDS):
                    gate = jnp.where(tcol == t, gate_s[s, t : t + 1, columns], gate)
                gated = (y + skip * x_s[s, part(i), columns]) * gate
                inverse = lax.rsqrt(jnp.mean(gated * gated, axis=1, keepdims=True) + EPSILON)
                normal = gated * inverse
                outs[i] = normal if outs[i] is None else outs[i] + normal
                cot = cot_s[part(i), columns].astype(f32) * gain
                shared = jnp.mean(cot * normal, axis=1, keepdims=True)
                dy = (cot - normal * shared) * (inverse * gate)
                high, low = split(dy)
                highs.append(lanes_of([high, high]))
                lows.append(lanes_of([low, low]))
                row_terms = dy * y
                rate_row += jnp.sum(lcol * row_terms, axis=0, keepdims=True)
                bias_row += jnp.sum(acol_s[s, h, part(i), :] * row_terms, axis=0, keepdims=True)
                dh_s[s, part(i), columns], dl_s[s, part(i), columns] = split(grown * dy)
            both = mm(rows_of(highs + lows), x2_s[s, :, columns2], NT)
            for i, j in factors[s]:
                e = both[part(i), part(j)] + both[part(tiles + i), part(j)]
                e = e * factors[s][i, j]
                q_s[s, part(i), part(j)] += e
                column_sums[j] = column_sums[j] + jnp.sum(e * score_s[s, part(i), part(j)], axis=0, keepdims=True)
            for j in range(tiles):
                rate_row -= log_row[:, part(j)] * column_sums[j]
                bias_row += mixed_row[:, part(j)] * column_sums[j]
        for i in range(tiles):
            enc_ref[i * 128 : (i + 1) * 128, columns] = (outs[i] * gain).astype(enc_ref.dtype)
        acc_s[0, pl.ds(h, 1), :] = rate_row
        acc_s[1, pl.ds(h, 1), :] = bias_row

    def some_heads(g, _):
        for i in range(UNROLL):
            one_head(g * UNROLL + i, 0)
        return 0

    lax.fori_loop(0, heads // UNROLL, some_heads, 0)

    enc_copy = pltpu.make_async_copy(enc_ref, enc_hbm, enc_sem)
    enc_copy.start()

    db_all = jnp.zeros((ROWS, STATE), f32)
    dc_all = jnp.zeros((ROWS, STATE), f32)
    for s in range(2):
        q = split(q_s[s])
        grown = (dh_s[s], dl_s[s])
        far = stacked_out(grown, states[s], STATE, NT)
        dc_own = split(stacked_out(q, lanes_of(own_b[s]), STATE) + far)
        db_own = split(mm3(q, own_c[s], TN))
        c2 = lanes_of(own_c[s])
        back = mm(c2, grown[0], TN)
        back = back[:STATE] + back[STATE:] + mm(own_c[s][0], grown[1], TN)
        back = rows_of(split(back))
        both = mm(own_onehot[s], lanes_of([db_own[0], dc_own[0]])) + mm(own_onehot[s], lanes_of([db_own[1], dc_own[1]]))
        dc_all = dc_all + both[:, STATE:]
        db_all = db_all + both[:, :STATE] + stacked_out((wh_s[s], wl_s[s]), back, STATE, NT)
        reach = stacked(b_all, back)
        for h in range(heads):
            at = 3 * s * heads + heads + h
            columns = slice(h * HEAD, (h + 1) * HEAD)
            x = rows_of([xw_s[:, columns], edge_s[:, columns]])
            terms = reach[:, columns] * x
            acc_s[0, h : h + 1, :] += jnp.sum(terms * weights[:, at : at + 1], axis=0, keepdims=True)
            acc_s[1, h : h + 1, :] += jnp.sum(
                terms * weights[:, at + heads : at + heads + 1], axis=0, keepdims=True
            )
    d_summed = split(jnp.concatenate([db_all, dc_all], axis=1) * bc_slope)
    by_tap = mm(pick, d_summed[0], TN) + mm(pick, d_summed[1], TN)
    grad_ref[...] = jnp.zeros_like(grad_ref)
    for k in range(CONV):
        grad_ref[k : k + 1, :] = scale * jnp.sum(by_tap[8 * k : 8 * k + 8, :] * table_bc, axis=0, keepdims=True)
    place = iota((heads, 128), 1) == iota((heads, 128), 0) + tp_place * heads
    for i in range(2):
        sums = scale * jnp.sum(acc_s[i], axis=1, keepdims=True)
        grad_ref[CONV + i : CONV + i + 1, 0:128] = jnp.sum(jnp.where(place, sums, 0.0), axis=0, keepdims=True)
    enc_copy.wait()


def mixer(near, far, rc_map, skip, small, large, scale):
    devices, count = near.shape[0] + far.shape[0], near.shape[1]
    depth, width = large[0].shape
    heads = width // HEAD
    chunks = 4
    vmem = pl.BlockSpec(memory_space=pltpu.VMEM)
    smem = pl.BlockSpec(memory_space=pltpu.SMEM)
    hbm = pl.BlockSpec(memory_space=pl.ANY)
    scratch = [
        ((chunks, depth // chunks, width), bf16),
        ((chunks, depth // chunks, width), bf16),
        ((depth, 2 * STATE), bf16),
        1 + 2 * chunks,
        ((count, width), bf16),
        None,
        ((devices, count), jnp.int32),
        ((2, devices, count), jnp.int32),
        ((IDS, devices, count), f32),
        ((ROWS, devices * count), bf16),
        ((128, devices * count), bf16),
        ((count, width), bf16),
        None,
        ((WINDOWS, width), f32),
        ((WINDOWS, 2 * width), bf16),
        ((16, width), f32),
        ((2, ROWS, width), bf16),
        ((2, ROWS, width), bf16),
        ((2, count, width), f32),
        ((2, count, 2 * width), bf16),
        ((2, count, width), f32),
        ((2, count, width), bf16),
        ((2, count, width), bf16),
        ((2, 3, heads, count), f32),
        ((2, heads, count, 128), f32),
        ((2, heads, count, 128), f32),
        ((count, 128), f32),
        ((2, 8, width), f32),
        ((2, count, count), f32),
        ((2, count, count), f32),
        ((2, heads, 128), f32),
    ]

    def space(item):
        if isinstance(item, tuple):
            return pltpu.VMEM(*item)
        return pltpu.SemaphoreType.DMA((item,)) if item else pltpu.SemaphoreType.DMA

    return pl.pallas_call(
        functools.partial(mixer_kernel, scale),
        in_specs=[vmem, vmem, smem, smem] + [vmem] * len(small) + [hbm] * len(large),
        out_specs=[hbm, vmem],
        out_shape=[
            jax.ShapeDtypeStruct((count, width), bf16),
            jax.ShapeDtypeStruct((8, 2 * STATE), f32),
        ],
        scratch_shapes=[space(item) for item in scratch],
        compiler_params=pltpu.CompilerParams(vmem_limit_bytes=56 * 2**20),
        name="mixer",
    )(
        near,
        far,
        rc_map,
        skip,
        *small,
        *large,
    )


def exchange(value, axis, distance):
    size = lax.axis_size(axis)
    return lax.ppermute(value, axis, [(i, i ^ distance) for i in range(size)])


def on_device(
    tokens,
    rc_map,
    embedding,
    norm_gain,
    w_values,
    w_gates,
    w_states,
    w_steps,
    conv_values,
    conv_states,
    step_bias,
    log_rate,
    skip_gain,
    head_gain,
    cotangent,
):
    devices = lax.axis_size("ctx")
    count = tokens.shape[0]
    near = jnp.minimum(tokens, IDS - 1).reshape(1, count)
    far = exchange(near, "ctx", 1)
    distance = 2
    while distance < devices:
        near = jnp.concatenate([near, far], axis=0)
        far = exchange(near, "ctx", distance)
        distance *= 2
    scale = 1.0 / math.sqrt(count * devices * HEAD)
    small = [
        embedding,
        norm_gain.reshape(1, -1),
        w_steps.T,
        conv_values,
        conv_states,
        step_bias.reshape(1, -1),
        log_rate.reshape(1, -1),
        head_gain.reshape(1, -1),
    ]
    large = [w_values, w_gates, w_states, cotangent]
    encoded, grads = mixer(near, far, rc_map, skip_gain, small, large, scale)
    for axis in ("tp", "ctx"):
        distance = 1
        while distance < lax.axis_size(axis):
            grads = grads + exchange(grads, axis, distance)
            distance *= 2
    head_total = log_rate.shape[0] * lax.axis_size("tp")
    return (encoded, grads[CONV, :head_total], grads[CONV + 1, :head_total], grads[:CONV])


def solution(mesh):
    placed = (
        P("ctx"),
        P(),
        P(),
        P(),
        P(None, "tp"),
        P(None, "tp"),
        P(),
        P(None, "tp"),
        P(None, "tp"),
        P(),
        P("tp"),
        P("tp"),
        P("tp"),
        P("tp"),
        P("ctx", "tp"),
    )
    return jax.shard_map(
        on_device,
        mesh=mesh,
        in_specs=placed,
        out_specs=(P("ctx", "tp"), P(), P(), P()),
        check_vma=False,
    )
```

time: 64.1 us -> 52.8 us (0.82)
  local copies, waits for them, and re-layouts: 8.93 us -> 1.7 us
  Pallas kernels: 24.3 us -> 19 us
  starting transfers between devices: 12.8 us -> 16.7 us
  waiting for transfers between devices: 15.4 us -> 13.1 us
    unnamed x30 -> x4, local copies, waits for them, and re-layouts: 7.82 us -> 0.59 us
    pallas_call x2 -> x1, Pallas kernels: 24.3 us -> 19 us  [mixer(): pl.pallas_call(functools.partial(mixer_kernel, scale), in_specs=[vmem, vm...]
    ppermute x8, starting transfers between devices: 12.8 us -> 16.7 us  [exchange(): return lax.ppermute(value, axis, [(i, i ^ distance) for i in range(size)])]
    ppermute x8, waiting for transfers between devices: 15.4 us -> 13.1 us  [exchange(): return lax.ppermute(value, axis, [(i, i ^ distance) for i in range(size)])]
    concatenate x3 -> x2, other arithmetic: 1.39 us -> 0.02 us  [on_device(): near = jnp.concatenate([near, far], axis=0)]
    add x5, other arithmetic: 0.02 us -> 0.71 us  [on_device(): grads = grads + exchange(grads, axis, distance)]
    min x0 -> x1, other arithmetic: none -> 0.68 us  [on_device(): near = jnp.minimum(tokens, IDS - 1).reshape(1, count)]
  transfers between devices with their start and end apart: 8 -> 8, of which waited for: 7 -> 8; matrix products, arithmetic and copies ran while one was open for 0% -> 0% of each run, Pallas kernels for 6% -> 0%
where the time goes in v2:
time: 52.8 us; the launch traced here: 52.6 us
  Pallas kernels  19 us (36%)
  starting transfers between devices  16.7 us (32%)
  waiting for transfers between devices  13.1 us (25%)
  local copies, waits for them, and re-layouts  1.7 us (3%)
  other arithmetic  1.41 us (3%)
  between operations  0.66 us (1%)
    pallas_call x1, Pallas kernels, mixer(): pl.pallas_call(functools.partial(mixer_kernel, scale), in_specs=[vmem, vm...  19 us
    ppermute x8, starting transfers between devices, exchange(): return lax.ppermute(value, axis, [(i, i ^ distance) for i in range(size)])  16.7 us
    ppermute x8, waiting for transfers between devices, exchange(): return lax.ppermute(value, axis, [(i, i ^ distance) for i in range(size)])  13.1 us
  transfers between devices with their start and end apart: 8, of which 8 were waited for; matrix products, arithmetic and copies ran while one was open for 0% of the time, Pallas kernels for 0%

profile of v2, /device:TPU:0, one launch (start us, length us, event | category | flops | bytes accessed | tf_op | source)
XLA Modules:
  0.0 52.6 jit_solution(18006934450369258960)
XLA Ops:
  0.6 0.7 %broadcast_minimum_fusion = s32[256]{0:T(256)S(1)} fusion(s32[256]{0:T(256)} %param.15), kind=kLoop, calls=%fused_computation.4 | loop fusion | flops 256 | bytes 2048 | tf_op jit(solution)/shard_map/min | solution.py:626
  1.3 2.9 %collective-permute-start = (s32[1,256]{1,0:T(1,128)S(1)}, s32[1,256]{1,0:T(1,128)S(1)}, u32[]{:S(2)}, u32[]{:S(2)}) collective-permute-start(s32[1,256]{1,0:T(1,128)S(1)} %bitcast.11), channel_id=1, source_target_pairs={{0,4},{4,0},{8,12},{12,8},{16,20},{20,16},{24,28},{28,24},{1,5},{5... | collective-permute-start | bytes 3080 | tf_op jit(solution)/shard_map/ppermute | solution.py:604
  4.3 1.5 %collective-permute-done = s32[1,256]{1,0:T(1,128)S(1)} collective-permute-done((s32[1,256]{1,0:T(1,128)S(1)}, s32[1,256]{1,0:T(1,128)S(1)}, u32[]{:S(2)}, u32[]{:S(2)}) %collective-permute-start) | collective-permute-done | bytes 1056 | tf_op jit(solution)/shard_map/ppermute | solution.py:604
  5.8 2.1 %collective-permute-start.1 = (s32[2,256]{1,0:T(2,128)S(1)}, s32[2,256]{1,0:T(2,128)S(1)}, u32[]{:S(2)}, u32[]{:S(2)}) collective-permute-start(s32[2,256]{1,0:T(2,128)S(1)} %pad_add_fusion.1), channel_id=1, source_target_pairs={{0,8},{4,12},{8,0},{12,4},{16,24},{20,28},{24,16},{28,20},{1,9},{5... | collective-permute-start | bytes 6152 | tf_op jit(solution)/shard_map/ppermute | solution.py:604
  7.9 1.6 %collective-permute-done.1 = s32[2,256]{1,0:T(2,128)S(1)} collective-permute-done((s32[2,256]{1,0:T(2,128)S(1)}, s32[2,256]{1,0:T(2,128)S(1)}, u32[]{:S(2)}, u32[]{:S(2)}) %collective-permute-start.1) | collective-permute-done | bytes 2080 | tf_op jit(solution)/shard_map/ppermute | solution.py:604
  9.5 0.0 copy-start
  9.5 3.1 %collective-permute-start.2 = (s32[4,256]{1,0:T(4,128)S(1)}, s32[4,256]{1,0:T(4,128)S(1)}, u32[]{:S(2)}, u32[]{:S(2)}) collective-permute-start(s32[4,256]{1,0:T(4,128)S(1)} %pad_add_fusion.near_ref), channel_id=1, source_target_pairs={{0,16},{4,20},{8,24},{12,28},{16,0},{20,4},{24,8},{28,12},{1,17},{... | collective-permute-start | bytes 12296 | tf_op jit(solution)/shard_map/ppermute | solution.py:604
  12.6 1.6 %collective-permute-done.2.far_ref = s32[4,256]{1,0:T(4,128)S(1)} collective-permute-done((s32[4,256]{1,0:T(4,128)S(1)}, s32[4,256]{1,0:T(4,128)S(1)}, u32[]{:S(2)}, u32[]{:S(2)}) %collective-permute-start.2) | collective-permute-done | bytes 4128 | tf_op jit(solution)/shard_map/ppermute | solution.py:604
  14.2 0.0 copy-start.1
  14.2 0.0 copy-done
  14.2 0.6 %copy-done.1 = s32[4,256]{1,0:T(4,128)} copy-done((s32[4,256]{1,0:T(4,128)}, s32[4,256]{1,0:T(4,128)S(1)}, u32[]{:S(2)}) %copy-start.1) | copy-done | bytes 4120
  14.8 19.0 %mixer.1 = (bf16[256,1024]{1,0:T(8,128)(2,1)}, f32[8,256]{1,0:T(8,128)}) custom-call(s32[4,256]{1,0:T(4,128)} %copy-done, s32[4,256]{1,0:T(4,128)} %copy-done.1, s32[4]{0:T(128)} %rc_ref.1, f32[8]{0:T(128)} %skip_ref.1, bf16[4,2048]{1,0:T(4,128)(2,1)} %emb_ref.1, f32[1,2048]{1,0:T(1,128)} %bitcast.14, bf16[8,2048]{1,0:T(8,128)(2,1)} %bitcast.10, ...), custom_call_target="tpu_custom_call" | custom-call | tf_op jit(solution)/shard_map/mixer/pallas_call | solution.py:581
  33.8 0.1 collective-permute-start.3
  33.9 1.4 %collective-permute-done.3 = f32[8,256]{1,0:T(8,128)S(1)} collective-permute-done((f32[8,256]{1,0:T(8,128)}, f32[8,256]{1,0:T(8,128)S(1)}, u32[]{:S(2)}, u32[]{:S(2)}) %collective-permute-start.3) | collective-permute-done | bytes 8224 | tf_op jit(solution)/shard_map/ppermute | solution.py:604
  35.2 0.7 %add.15 = f32[8,256]{1,0:T(8,128)S(1)} add(f32[8,256]{1,0:T(8,128)} %get-tuple-element.7, f32[8,256]{1,0:T(8,128)S(1)} %collective-permute-done.3) | non-fusion elementwise | flops 2048 | bytes 24576 | tf_op jit(solution)/shard_map/add | solution.py:649
  35.9 1.8 %collective-permute-start.4 = (f32[8,256]{1,0:T(8,128)S(1)}, f32[8,256]{1,0:T(8,128)S(1)}, u32[]{:S(2)}, u32[]{:S(2)}) collective-permute-start(f32[8,256]{1,0:T(8,128)S(1)} %add.15), channel_id=1, source_target_pairs={{0,2},{1,3},{2,0},{3,1},{4,6},{5,7},{6,4},{7,5},{8,10},{9,11},{10,... | collective-permute-start | bytes 24584 | tf_op jit(solution)/shard_map/ppermute | solution.py:604
  37.8 1.8 %collective-permute-done.4 = f32[8,256]{1,0:T(8,128)S(1)} collective-permute-done((f32[8,256]{1,0:T(8,128)S(1)}, f32[8,256]{1,0:T(8,128)S(1)}, u32[]{:S(2)}, u32[]{:S(2)}) %collective-permute-start.4) | collective-permute-done | bytes 8224 | tf_op jit(solution)/shard_map/ppermute | solution.py:604
  39.6 1.8 %collective-permute-start.5 = (f32[8,256]{1,0:T(8,128)S(1)}, f32[8,256]{1,0:T(8,128)S(1)}, u32[]{:S(2)}, u32[]{:S(2)}) collective-permute-start(f32[8,256]{1,0:T(8,128)S(1)} %add.16), channel_id=1, source_target_pairs={{0,4},{4,0},{8,12},{12,8},{16,20},{20,16},{24,28},{28,24},{1,5},{5... | collective-permute-start | bytes 24584 | tf_op jit(solution)/shard_map/ppermute | solution.py:604
  41.4 1.8 %collective-permute-done.5 = f32[8,256]{1,0:T(8,128)S(1)} collective-permute-done((f32[8,256]{1,0:T(8,128)S(1)}, f32[8,256]{1,0:T(8,128)S(1)}, u32[]{:S(2)}, u32[]{:S(2)}) %collective-permute-start.5) | collective-permute-done | bytes 8224 | tf_op jit(solution)/shard_map/ppermute | solution.py:604
  43.2 1.9 %collective-permute-start.6 = (f32[8,256]{1,0:T(8,128)S(1)}, f32[8,256]{1,0:T(8,128)S(1)}, u32[]{:S(2)}, u32[]{:S(2)}) collective-permute-start(f32[8,256]{1,0:T(8,128)S(1)} %add.17), channel_id=1, source_target_pairs={{0,8},{4,12},{8,0},{12,4},{16,24},{20,28},{24,16},{28,20},{1,9},{5... | collective-permute-start | bytes 24584 | tf_op jit(solution)/shard_map/ppermute | solution.py:604
  45.1 1.7 %collective-permute-done.6 = f32[8,256]{1,0:T(8,128)S(1)} collective-permute-done((f32[8,256]{1,0:T(8,128)S(1)}, f32[8,256]{1,0:T(8,128)S(1)}, u32[]{:S(2)}, u32[]{:S(2)}) %collective-permute-start.6) | collective-permute-done | bytes 8224 | tf_op jit(solution)/shard_map/ppermute | solution.py:604
  46.9 2.9 %collective-permute-start.7 = (f32[8,256]{1,0:T(8,128)S(1)}, f32[8,256]{1,0:T(8,128)S(1)}, u32[]{:S(2)}, u32[]{:S(2)}) collective-permute-start(f32[8,256]{1,0:T(8,128)S(1)} %add.18), channel_id=1, source_target_pairs={{0,16},{4,20},{8,24},{12,28},{16,0},{20,4},{24,8},{28,12},{1,17},{... | collective-permute-start | bytes 24584 | tf_op jit(solution)/shard_map/ppermute | solution.py:604
  49.8 1.6 %collective-permute-done.7 = f32[8,256]{1,0:T(8,128)S(1)} collective-permute-done((f32[8,256]{1,0:T(8,128)S(1)}, f32[8,256]{1,0:T(8,128)S(1)}, u32[]{:S(2)}, u32[]{:S(2)}) %collective-permute-start.7) | collective-permute-done | bytes 8224 | tf_op jit(solution)/shard_map/ppermute | solution.py:604
  51.4 0.5 slice_bitcast_fusion
  52.0 0.6 %slice.14 = f32[4,256]{1,0:T(4,128)} slice(f32[8,256]{1,0:T(8,128)S(1)} %add.19), slice={[0:4], [0:256]} | slice | bytes 8192 | tf_op jit(solution)/shard_map/slice | solution.py:652
  (6 shorter events, 0.0 us)
Async XLA Ops:
  1.3 4.5 %collective-permute-start = (s32[1,256]{1,0:T(1,128)S(1)}, s32[1,256]{1,0:T(1,128)S(1)}, u32[]{:S(2)}, u32[]{:S(2)}) collective-permute-start(s32[1,256]{1,0:T(1,128)S(1)} %bitcast.11), channel_id=1, source_target_pairs={{0,4},{4,0},{8,12},{12,8},{16,20},{20,16},{24,28},{28,24},{1,5},{5... | collective-permute-start | bytes 3080 | tf_op jit(solution)/shard_map/ppermute | solution.py:604
  5.8 3.7 %collective-permute-start.1 = (s32[2,256]{1,0:T(2,128)S(1)}, s32[2,256]{1,0:T(2,128)S(1)}, u32[]{:S(2)}, u32[]{:S(2)}) collective-permute-start(s32[2,256]{1,0:T(2,128)S(1)} %pad_add_fusion.1), channel_id=1, source_target_pairs={{0,8},{4,12},{8,0},{12,4},{16,24},{20,28},{24,16},{28,20},{1,9},{5... | collective-permute-start | bytes 6152 | tf_op jit(solution)/shard_map/ppermute | solution.py:604
  9.5 4.7 %copy-start = (s32[4,256]{1,0:T(4,128)}, s32[4,256]{1,0:T(4,128)S(1)}, u32[]{:S(2)}) copy-start(s32[4,256]{1,0:T(4,128)S(1)} %pad_add_fusion.near_ref) | copy-start | bytes 12292
  9.5 4.7 %collective-permute-start.2 = (s32[4,256]{1,0:T(4,128)S(1)}, s32[4,256]{1,0:T(4,128)S(1)}, u32[]{:S(2)}, u32[]{:S(2)}) collective-permute-start(s32[4,256]{1,0:T(4,128)S(1)} %pad_add_fusion.near_ref), channel_id=1, source_target_pairs={{0,16},{4,20},{8,24},{12,28},{16,0},{20,4},{24,8},{28,12},{1,17},{... | collective-permute-start | bytes 12296 | tf_op jit(solution)/shard_map/ppermute | solution.py:604
  14.2 0.6 %copy-start.1 = (s32[4,256]{1,0:T(4,128)}, s32[4,256]{1,0:T(4,128)S(1)}, u32[]{:S(2)}) copy-start(s32[4,256]{1,0:T(4,128)S(1)} %collective-permute-done.2.far_ref) | copy-start | bytes 12292
  33.8 1.4 %collective-permute-start.3 = (f32[8,256]{1,0:T(8,128)}, f32[8,256]{1,0:T(8,128)S(1)}, u32[]{:S(2)}, u32[]{:S(2)}) collective-permute-start(f32[8,256]{1,0:T(8,128)} %get-tuple-element.7), channel_id=1, source_target_pairs={{0,1},{1,0},{2,3},{3,2},{4,5},{5,4},{6,7},{7,6},{8,9},{9,8},{10,11... | collective-permute-start | bytes 24584 | tf_op jit(solution)/shard_map/ppermute | solution.py:604
  35.9 3.7 %collective-permute-start.4 = (f32[8,256]{1,0:T(8,128)S(1)}, f32[8,256]{1,0:T(8,128)S(1)}, u32[]{:S(2)}, u32[]{:S(2)}) collective-permute-start(f32[8,256]{1,0:T(8,128)S(1)} %add.15), channel_id=1, source_target_pairs={{0,2},{1,3},{2,0},{3,1},{4,6},{5,7},{6,4},{7,5},{8,10},{9,11},{10,... | collective-permute-start | bytes 24584 | tf_op jit(solution)/shard_map/ppermute | solution.py:604
  39.6 3.7 %collective-permute-start.5 = (f32[8,256]{1,0:T(8,128)S(1)}, f32[8,256]{1,0:T(8,128)S(1)}, u32[]{:S(2)}, u32[]{:S(2)}) collective-permute-start(f32[8,256]{1,0:T(8,128)S(1)} %add.16), channel_id=1, source_target_pairs={{0,4},{4,0},{8,12},{12,8},{16,20},{20,16},{24,28},{28,24},{1,5},{5... | collective-permute-start | bytes 24584 | tf_op jit(solution)/shard_map/ppermute | solution.py:604
  43.2 3.7 %collective-permute-start.6 = (f32[8,256]{1,0:T(8,128)S(1)}, f32[8,256]{1,0:T(8,128)S(1)}, u32[]{:S(2)}, u32[]{:S(2)}) collective-permute-start(f32[8,256]{1,0:T(8,128)S(1)} %add.17), channel_id=1, source_target_pairs={{0,8},{4,12},{8,0},{12,4},{16,24},{20,28},{24,16},{28,20},{1,9},{5... | collective-permute-start | bytes 24584 | tf_op jit(solution)/shard_map/ppermute | solution.py:604
  46.9 4.5 %collective-permute-start.7 = (f32[8,256]{1,0:T(8,128)S(1)}, f32[8,256]{1,0:T(8,128)S(1)}, u32[]{:S(2)}, u32[]{:S(2)}) collective-permute-start(f32[8,256]{1,0:T(8,128)S(1)} %add.18), channel_id=1, source_target_pairs={{0,16},{4,20},{8,24},{12,28},{16,0},{20,4},{24,8},{28,12},{1,17},{... | collective-permute-start | bytes 24584 | tf_op jit(solution)/shard_map/ppermute | solution.py:604

commit v3 on v2

--- a/solution.py
+++ b/solution.py
@@ -15,6 +15,8 @@
 WINDOWS = IDS**CONV
 ROWS = WINDOWS + 16
 UNROLL = 2
+TABLES_VMEM = 53 * 2**20
+MIXER_VMEM = 53 * 2**20
 EPSILON = 1e-05
 
 f32 = jnp.float32
@@ -75,29 +77,69 @@
     return rows_of([p1, p2, p3, jnp.zeros_like(p1)])
 
 
+def tables_kernel(normed_ref, wv_hbm, ws_hbm, tv_ref, ts_ref, held_v, held_s, sems):
+    chunks, size, _ = held_v.shape
+    copies = [pltpu.make_async_copy(ws_hbm, held_s, sems.at[chunks])]
+    for i in range(chunks):
+        copies.append(pltpu.make_async_copy(wv_hbm.at[pl.ds(i * size, size), :], held_v.at[i], sems.at[i]))
+    for copy in copies:
+        copy.start()
+    normed = normed_ref[...]
+    copies[0].wait()
+    ts_ref[0:IDS, :] = mm(normed, held_s[...])
+    ts_ref[IDS:, :] = jnp.zeros((8 - IDS, ts_ref.shape[1]), f32)
+    product = None
+    for i in range(chunks):
+        copies[1 + i].wait()
+        term = mm(normed[:, i * size : (i + 1) * size], held_v[i])
+        product = term if product is None else product + term
+    tv_ref[0:IDS, :] = product
+    tv_ref[IDS:, :] = jnp.zeros((8 - IDS, tv_ref.shape[1]), f32)
+
+
+def tables(normed, w_values, w_states):
+    depth, width = w_values.shape
+    chunks = 4
+    vmem = pl.BlockSpec(memory_space=pltpu.VMEM)
+    hbm = pl.BlockSpec(memory_space=pl.ANY)
+    return pl.pallas_call(
+        tables_kernel,
+        in_specs=[vmem, hbm, hbm],
+        out_specs=[vmem, vmem],
+        out_shape=[
+            jax.ShapeDtypeStruct((8, width), f32),
+            jax.ShapeDtypeStruct((8, w_states.shape[1]), f32),
+        ],
+        scratch_shapes=[
+            pltpu.VMEM((chunks, depth // chunks, width), bf16),
+            pltpu.VMEM(w_states.shape, bf16),
+            pltpu.SemaphoreType.DMA((1 + chunks,)),
+        ],
+        compiler_params=pltpu.CompilerParams(vmem_limit_bytes=TABLES_VMEM),
+        name="tables",
+    )(normed, w_values, w_states)
+
+
 def mixer_kernel(
     scale,
     near_ref,
     far_ref,
     rc_ref,
     skip_ref,
-    emb_ref,
-    norm_gain_ref,
-    wt_ref,
+    normed_ref,
+    tv_ref,
+    tbc_ref,
+    dt_ref,
     cv_ref,
     cs_ref,
     bias_ref,
     rate_ref,
     gain_ref,
-    wv_hbm,
+    cot_ref,
     wg_hbm,
-    ws_hbm,
-    cot_hbm,
     enc_hbm,
     grad_ref,
-    held_v,
     held_g,
-    held_s,
     sems,
     enc_ref,
     enc_sem,
@@ -106,8 +148,6 @@
     count_s,
     onehot_s,
     weight_s,
-    cot_s,
-    cot_sem,
     xw_s,
     x2w_s,
     edge_s,
@@ -132,18 +172,12 @@
     heads = width // HEAD
     here = lax.axis_index("ctx")
     tp_place = lax.axis_index("tp")
-    chunks, size, _ = held_v.shape
-    rows_at = lambda i: pl.ds(i * size, size)
-    copies = [pltpu.make_async_copy(ws_hbm, held_s, sems.at[0])]
+    chunks, size, _ = held_g.shape
+    copies = []
     for i in range(chunks):
-        copies.append(pltpu.make_async_copy(wv_hbm.at[rows_at(i), :], held_v.at[i], sems.at[1 + i]))
-    for i in range(chunks):
-        copies.append(pltpu.make_async_copy(wg_hbm.at[rows_at(i), :], held_g.at[i], sems.at[1 + chunks + i]))
+        copies.append(pltpu.make_async_copy(wg_hbm.at[pl.ds(i * size, size), :], held_g.at[i], sems.at[i]))
     for copy in copies:
         copy.start()
-
-    cot_copy = pltpu.make_async_copy(cot_hbm, cot_s, cot_sem)
-    cot_copy.start()
 
     half = near_ref.shape[0]
     for r in range(devices):
@@ -174,12 +208,9 @@
     ids_s[0] = kf
     ids_s[1] = kr
 
-    embedded = emb_ref[...].astype(f32)
-    mean = jnp.mean(embedded * embedded, axis=1, keepdims=True)
-    normed = (embedded * lax.rsqrt(mean + EPSILON) * norm_gain_ref[...]).astype(bf16)
     eye = iota((heads, heads), 0) == iota((heads, heads), 1)
     column = lambda ref: jnp.sum(jnp.where(eye, ref[...], 0.0), axis=1, keepdims=True)
-    raw = mm(wt_ref[...], normed, NT) + column(bias_ref)
+    raw = dt_ref[...] + column(bias_ref)
     rate = jnp.exp(column(rate_ref))
     step = jnp.maximum(raw, 0.0) + jnp.log1p(jnp.exp(-jnp.abs(raw)))
     slope = sigmoid(raw)
@@ -248,25 +279,18 @@
         window_j = jnp.where(forward, kf[j : j + 1, :], kr[j : j + 1, :])
         onehot_s[:, j * count : (j + 1) * count] = (window_rows == window_j).astype(bf16)
 
-    blank = lambda size: jnp.zeros((8 - IDS, size), f32)
-    copies[0].wait()
-    product = mm(normed, held_s[...])
-    table_bc = rows_of([product, blank(product.shape[1])])
-    product = None
-    for i in range(chunks):
-        copies[1 + i].wait()
-        term = mm(normed[:, i * size : (i + 1) * size], held_v[i])
-        product = term if product is None else product + term
-        for j in range(i * devices // chunks, (i + 1) * devices // chunks):
-            earlier(j)
-    taps_v = tap_parts(rows_of([product, blank(width)]), cv_ref[...])
+    for j in range(devices):
+        earlier(j)
+
+    table_bc = tbc_ref[...]
+    taps_v = tap_parts(tv_ref[...], cv_ref[...])
     taps_s = tap_parts(table_bc, cs_ref[...])
     product = None
     for i in range(chunks):
-        copies[1 + chunks + i].wait()
-        term = mm(normed[:, i * size : (i + 1) * size], held_g[i])
+        copies[i].wait()
+        term = mm(normed_ref[:, i * size : (i + 1) * size], held_g[i])
         product = term if product is None else product + term
-    gates = rows_of([product, blank(width)])
+    gates = rows_of([product, jnp.zeros((8 - IDS, width), f32)])
     gates = gates * sigmoid(gates)
 
     weights = mm(onehot_s[...], weight_s[...], NT)
@@ -402,7 +426,6 @@
         states.append(rows_of(split(state)))
         far_s[s] = stacked(own_c[s], states[s])
 
-    cot_copy.wait()
     q_s[...] = jnp.zeros_like(q_s)
     tiles = count // 128
     triangle = [iota((128, 128), 0) >= iota((128, 128), 1), iota((128, 128), 0) <= iota((128, 128), 1)]
@@ -460,7 +483,7 @@
                 inverse = lax.rsqrt(jnp.mean(gated * gated, axis=1, keepdims=True) + EPSILON)
                 normal = gated * inverse
                 outs[i] = normal if outs[i] is None else outs[i] + normal
-                cot = cot_s[part(i), columns].astype(f32) * gain
+                cot = cot_ref[part(i), columns].astype(f32) * gain
                 shared = jnp.mean(cot * normal, axis=1, keepdims=True)
                 dy = (cot - normal * shared) * (inverse * gate)
                 high, low = split(dy)
@@ -531,9 +554,9 @@
     enc_copy.wait()
 
 
-def mixer(near, far, rc_map, skip, small, large, scale):
+def mixer(near, far, rc_map, skip, small, w_gates, scale):
     devices, count = near.shape[0] + far.shape[0], near.shape[1]
-    depth, width = large[0].shape
+    depth, width = w_gates.shape
     heads = width // HEAD
     chunks = 4
     vmem = pl.BlockSpec(memory_space=pltpu.VMEM)
@@ -541,9 +564,7 @@
     hbm = pl.BlockSpec(memory_space=pl.ANY)
     scratch = [
         ((chunks, depth // chunks, width), bf16),
-        ((chunks, depth // chunks, width), bf16),
-        ((depth, 2 * STATE), bf16),
-        1 + 2 * chunks,
+        chunks,
         ((count, width), bf16),
         None,
         ((devices, count), jnp.int32),
@@ -551,8 +572,6 @@
         ((IDS, devices, count), f32),
         ((ROWS, devices * count), bf16),
         ((128, devices * count), bf16),
-        ((count, width), bf16),
-        None,
         ((WINDOWS, width), f32),
         ((WINDOWS, 2 * width), bf16),
         ((16, width), f32),
@@ -580,14 +599,14 @@
 
     return pl.pallas_call(
         functools.partial(mixer_kernel, scale),
-        in_specs=[vmem, vmem, smem, smem] + [vmem] * len(small) + [hbm] * len(large),
+        in_specs=[vmem, vmem, smem, smem] + [vmem] * len(small) + [hbm],
         out_specs=[hbm, vmem],
         out_shape=[
             jax.ShapeDtypeStruct((count, width), bf16),
             jax.ShapeDtypeStruct((8, 2 * STATE), f32),
         ],
         scratch_shapes=[space(item) for item in scratch],
-        compiler_params=pltpu.CompilerParams(vmem_limit_bytes=56 * 2**20),
+        compiler_params=pltpu.CompilerParams(vmem_limit_bytes=MIXER_VMEM),
         name="mixer",
     )(
         near,
@@ -595,7 +614,7 @@
         rc_map,
         skip,
         *small,
-        *large,
+        w_gates,
     )
 
 
@@ -631,18 +650,24 @@
         far = exchange(near, "ctx", distance)
         distance *= 2
     scale = 1.0 / math.sqrt(count * devices * HEAD)
+    embedded = embedding.astype(f32)
+    mean = jnp.mean(embedded * embedded, axis=1, keepdims=True)
+    normed = (embedded * lax.rsqrt(mean + EPSILON) * norm_gain).astype(bf16)
+    tv, tbc = tables(normed, w_values, w_states)
+    dt = lax.dot_general(w_steps, normed, (((0,), (1,)), ((), ())), preferred_element_type=f32)
     small = [
-        embedding,
-        norm_gain.reshape(1, -1),
-        w_steps.T,
+        normed,
+        tv,
+        tbc,
+        dt,
         conv_values,
         conv_states,
         step_bias.reshape(1, -1),
         log_rate.reshape(1, -1),
         head_gain.reshape(1, -1),
+        cotangent,
     ]
-    large = [w_values, w_gates, w_states, cotangent]
-    encoded, grads = mixer(near, far, rc_map, skip_gain, small, large, scale)
+    encoded, grads = mixer(near, far, rc_map, skip_gain, small, w_gates, scale)
     for axis in ("tp", "ctx"):
         distance = 1
         while distance < lax.axis_size(axis):

time: 52.8 us -> 50.8 us (0.962)
  starting transfers between devices: 16.7 us -> 14 us
  other arithmetic: 1.41 us -> 2.41 us
  waiting for transfers between devices: 13.1 us -> 12.3 us
  local copies, waits for them, and re-layouts: 1.7 us -> 1.16 us
    pallas_call x0 -> x1, Pallas kernels: none -> 3.09 us  [tables(): pl.pallas_call(tables_kernel, in_specs=[vmem, hbm, hbm], out_specs=[vmem,...]
    ppermute x8, starting transfers between devices: 16.7 us -> 14 us  [exchange(): return lax.ppermute(value, axis, [(i, i ^ distance) for i in range(size)])]
    pallas_call x1, Pallas kernels: 19 us -> 16.4 us  [mixer(): pl.pallas_call(functools.partial(mixer_kernel, scale), in_specs=[vmem, vm...]
    reduce_sum x0 -> x1, other arithmetic: none -> 0.85 us  [on_device(): mean = jnp.mean(embedded * embedded, axis=1, keepdims=True)]
    convert_element_type x0 -> x1, other arithmetic: none -> 0.8 us  [on_device(): normed = (embedded * lax.rsqrt(mean + EPSILON) * norm_gain).astype(bf16)]
    ppermute x8, waiting for transfers between devices: 13.1 us -> 12.3 us  [exchange(): return lax.ppermute(value, axis, [(i, i ^ distance) for i in range(size)])]
    add x5, other arithmetic: 0.71 us -> 0.02 us  [on_device(): grads = grads + exchange(grads, axis, distance)]
    unnamed x4 -> x18, local copies, waits for them, and re-layouts: 0.59 us -> 0.04 us
  transfers between devices with their start and end apart: 8 -> 8, of which waited for: 8 -> 7; matrix products, arithmetic and copies ran while one was open for 0% -> 4% of each run, Pallas kernels for 0% -> 6%
where the time goes in v3:
time: 50.8 us; the launch traced here: 50.3 us
  Pallas kernels  19.5 us (38%)
  starting transfers between devices  14 us (28%)
  waiting for transfers between devices  12.3 us (24%)
  other arithmetic  2.41 us (5%)
  local copies, waits for them, and re-layouts  1.16 us (2%)
  between operations  0.82 us (2%)
    pallas_call x1, Pallas kernels, mixer(): pl.pallas_call(functools.partial(mixer_kernel, scale), in_specs=[vmem, vm...  16.4 us
    ppermute x8, starting transfers between devices, exchange(): return lax.ppermute(value, axis, [(i, i ^ distance) for i in range(size)])  14 us
    ppermute x8, waiting for transfers between devices, exchange(): return lax.ppermute(value, axis, [(i, i ^ distance) for i in range(size)])  12.3 us
    pallas_call x1, Pallas kernels, tables(): pl.pallas_call(tables_kernel, in_specs=[vmem, hbm, hbm], out_specs=[vmem,...  3.09 us
  transfers between devices with their start and end apart: 8, of which 7 were waited for; matrix products, arithmetic and copies ran while one was open for 4% of the time, Pallas kernels for 6%

profile of v3, /device:TPU:0, one launch (start us, length us, event | category | flops | bytes accessed | tf_op | source)
XLA Modules:
  0.0 50.3 jit_solution(5674529581465365583)
XLA Ops:
  0.6 0.0 copy-start
  0.6 0.0 copy-start.1
  0.7 0.0 copy-start.4
  0.7 0.0 copy-start.6
  0.7 0.0 copy-start.8
  0.7 0.0 copy-start.7
  0.7 0.0 copy-start.3
  0.7 0.0 copy-start.2
  0.7 0.0 copy-start.5
  0.7 0.7 %broadcast_minimum_fusion = s32[256]{0:T(256)S(1)} fusion(s32[256]{0:T(256)} %param.15), kind=kLoop, calls=%fused_computation.11 | loop fusion | flops 256 | bytes 2048 | tf_op jit(solution)/shard_map/min | solution.py:645
  1.5 2.9 %collective-permute-start = (s32[1,256]{1,0:T(1,128)S(1)}, s32[1,256]{1,0:T(1,128)S(1)}, u32[]{:S(2)}, u32[]{:S(2)}) collective-permute-start(s32[1,256]{1,0:T(1,128)S(1)} %bitcast.15), channel_id=1, source_target_pairs={{0,4},{4,0},{8,12},{12,8},{16,20},{20,16},{24,28},{28,24},{1,5},{5... | collective-permute-start | bytes 3080 | tf_op jit(solution)/shard_map/ppermute | solution.py:623
  4.4 0.8 %fusion = f32[4]{0:T(128)S(1)} fusion(bf16[4,2048]{1,0:T(4,128)(2,1)} %param.17), kind=kLoop, calls=%fused_computation.3 | loop fusion | flops 24572 | bytes 16400 | tf_op jit(solution)/shard_map/reduce_sum | solution.py:654
  5.3 0.7 %collective-permute-done = s32[1,256]{1,0:T(1,128)S(1)} collective-permute-done((s32[1,256]{1,0:T(1,128)S(1)}, s32[1,256]{1,0:T(1,128)S(1)}, u32[]{:S(2)}, u32[]{:S(2)}) %collective-permute-start) | collective-permute-done | bytes 1056 | tf_op jit(solution)/shard_map/ppermute | solution.py:623
  6.0 2.1 %collective-permute-start.1 = (s32[2,256]{1,0:T(2,128)S(1)}, s32[2,256]{1,0:T(2,128)S(1)}, u32[]{:S(2)}, u32[]{:S(2)}) collective-permute-start(s32[2,256]{1,0:T(2,128)S(1)} %pad_add_fusion.1), channel_id=1, source_target_pairs={{0,8},{4,12},{8,0},{12,4},{16,24},{20,28},{24,16},{28,20},{1,9},{5... | collective-permute-start | bytes 6152 | tf_op jit(solution)/shard_map/ppermute | solution.py:623
  8.1 0.8 %fusion.2.normed_ref = bf16[4,2048]{1,0:T(4,128)(2,1)S(1)} fusion(bf16[4,2048]{1,0:T(4,128)(2,1)} %param.17, f32[2048]{0:T(1024)} %param.18, f32[4]{0:T(128)S(1)} %add_rsqrt_fusion), kind=kLoop, calls=%fused_computation.5 | loop fusion | flops 32768 | bytes 40976 | tf_op jit(solution)/shard_map/convert_element_type | solution.py:655
  8.9 0.8 %collective-permute-done.1 = s32[2,256]{1,0:T(2,128)S(1)} collective-permute-done((s32[2,256]{1,0:T(2,128)S(1)}, s32[2,256]{1,0:T(2,128)S(1)}, u32[]{:S(2)}, u32[]{:S(2)}) %collective-permute-start.1) | collective-permute-done | bytes 2080 | tf_op jit(solution)/shard_map/ppermute | solution.py:623
  9.6 3.1 %collective-permute-start.2 = (s32[4,256]{1,0:T(4,128)S(1)}, s32[4,256]{1,0:T(4,128)S(1)}, u32[]{:S(2)}, u32[]{:S(2)}) collective-permute-start(s32[4,256]{1,0:T(4,128)S(1)} %pad_add_fusion.near_ref), channel_id=1, source_target_pairs={{0,16},{4,20},{8,24},{12,28},{16,0},{20,4},{24,8},{28,12},{1,17},{... | collective-permute-start | bytes 12296 | tf_op jit(solution)/shard_map/ppermute | solution.py:623
  12.7 0.0 copy-done
  12.7 0.1 convolution_bitcast_fusion.dt_ref
  12.9 3.1 %tables.1 = (f32[8,1024]{1,0:T(8,128)S(1)}, f32[8,256]{1,0:T(8,128)S(1)}) custom-call(bf16[4,2048]{1,0:T(4,128)(2,1)S(1)} %fusion.2.normed_ref, bf16[2048,1024]{1,0:T(8,128)(2,1)} %wv_hbm.1, bf16[2048,256]{1,0:T(8,128)(2,1)} %ws_hbm.1), custom_call_target="tpu_custom_call" | custom-call | tf_op jit(solution)/shard_map/tables/pallas_call | solution.py:105
  16.0 0.0 collective-permute-done.2.far_ref
  16.0 0.0 copy-done.1
  16.0 0.0 copy-done.4
  16.0 0.0 copy-done.6
  16.0 0.0 copy-done.8
  16.0 0.0 copy-done.7
  16.0 0.0 copy-done.3
  16.0 0.0 copy-done.2
  16.0 0.0 copy-done.5
  16.0 16.4 %mixer.1 = (bf16[256,1024]{1,0:T(8,128)(2,1)}, f32[8,256]{1,0:T(8,128)S(1)}) custom-call(s32[4,256]{1,0:T(4,128)S(1)} %pad_add_fusion.near_ref, s32[4,256]{1,0:T(4,128)S(1)} %collective-permute-done.2.far_ref, s32[4]{0:T(128)S(1)} %copy-done.5, f32[8]{0:T(128)S(1)} %copy-done.6, bf16[4,2048]{1,0:T(4,128)(2,1)S(1)} %fusion.2.normed_ref, ...), custom_call_target="tpu_custom_call" | custom-call | tf_op jit(solution)/shard_map/mixer/pallas_call | solution.py:600
  32.5 0.1 collective-permute-start.3
  32.5 1.2 %collective-permute-done.3 = f32[8,256]{1,0:T(8,128)S(1)} collective-permute-done((f32[8,256]{1,0:T(8,128)S(1)}, f32[8,256]{1,0:T(8,128)S(1)}, u32[]{:S(2)}, u32[]{:S(2)}) %collective-permute-start.3) | collective-permute-done | bytes 8224 | tf_op jit(solution)/shard_map/ppermute | solution.py:623
  33.7 1.5 %collective-permute-start.4 = (f32[8,256]{1,0:T(8,128)S(1)}, f32[8,256]{1,0:T(8,128)S(1)}, u32[]{:S(2)}, u32[]{:S(2)}) collective-permute-start(f32[8,256]{1,0:T(8,128)S(1)} %add.24), channel_id=1, source_target_pairs={{0,2},{1,3},{2,0},{3,1},{4,6},{5,7},{6,4},{7,5},{8,10},{9,11},{10,... | collective-permute-start | bytes 24584 | tf_op jit(solution)/shard_map/ppermute | solution.py:623
  35.2 2.1 %collective-permute-done.4 = f32[8,256]{1,0:T(8,128)S(1)} collective-permute-done((f32[8,256]{1,0:T(8,128)S(1)}, f32[8,256]{1,0:T(8,128)S(1)}, u32[]{:S(2)}, u32[]{:S(2)}) %collective-permute-start.4) | collective-permute-done | bytes 8224 | tf_op jit(solution)/shard_map/ppermute | solution.py:623
  37.4 1.5 %collective-permute-start.5 = (f32[8,256]{1,0:T(8,128)S(1)}, f32[8,256]{1,0:T(8,128)S(1)}, u32[]{:S(2)}, u32[]{:S(2)}) collective-permute-start(f32[8,256]{1,0:T(8,128)S(1)} %add.25), channel_id=1, source_target_pairs={{0,4},{4,0},{8,12},{12,8},{16,20},{20,16},{24,28},{28,24},{1,5},{5... | collective-permute-start | bytes 24584 | tf_op jit(solution)/shard_map/ppermute | solution.py:623
  38.9 2.2 %collective-permute-done.5 = f32[8,256]{1,0:T(8,128)S(1)} collective-permute-done((f32[8,256]{1,0:T(8,128)S(1)}, f32[8,256]{1,0:T(8,128)S(1)}, u32[]{:S(2)}, u32[]{:S(2)}) %collective-permute-start.5) | collective-permute-done | bytes 8224 | tf_op jit(solution)/shard_map/ppermute | solution.py:623
  41.0 1.6 %collective-permute-start.6 = (f32[8,256]{1,0:T(8,128)S(1)}, f32[8,256]{1,0:T(8,128)S(1)}, u32[]{:S(2)}, u32[]{:S(2)}) collective-permute-start(f32[8,256]{1,0:T(8,128)S(1)} %add.26), channel_id=1, source_target_pairs={{0,8},{4,12},{8,0},{12,4},{16,24},{20,28},{24,16},{28,20},{1,9},{5... | collective-permute-start | bytes 24584 | tf_op jit(solution)/shard_map/ppermute | solution.py:623
  42.6 2.1 %collective-permute-done.6 = f32[8,256]{1,0:T(8,128)S(1)} collective-permute-done((f32[8,256]{1,0:T(8,128)S(1)}, f32[8,256]{1,0:T(8,128)S(1)}, u32[]{:S(2)}, u32[]{:S(2)}) %collective-permute-start.6) | collective-permute-done | bytes 8224 | tf_op jit(solution)/shard_map/ppermute | solution.py:623
  44.7 1.2 %collective-permute-start.7 = (f32[8,256]{1,0:T(8,128)S(1)}, f32[8,256]{1,0:T(8,128)S(1)}, u32[]{:S(2)}, u32[]{:S(2)}) collective-permute-start(f32[8,256]{1,0:T(8,128)S(1)} %add.27), channel_id=1, source_target_pairs={{0,16},{4,20},{8,24},{12,28},{16,0},{20,4},{24,8},{28,12},{1,17},{... | collective-permute-start | bytes 24584 | tf_op jit(solution)/shard_map/ppermute | solution.py:623
  45.9 3.3 %collective-permute-done.7 = f32[8,256]{1,0:T(8,128)S(1)} collective-permute-done((f32[8,256]{1,0:T(8,128)S(1)}, f32[8,256]{1,0:T(8,128)S(1)}, u32[]{:S(2)}, u32[]{:S(2)}) %collective-permute-start.7) | collective-permute-done | bytes 8224 | tf_op jit(solution)/shard_map/ppermute | solution.py:623
  49.2 0.5 %slice_bitcast_fusion = (f32[32]{0:T(128)}, f32[32]{0:T(128)}) fusion(f32[8,256]{1,0:T(8,128)S(1)} %add.28), kind=kLoop, calls=%fused_computation.8 | loop fusion | bytes 512 | tf_op jit(solution)/shard_map/squeeze | solution.py:677
  49.8 0.6 %slice.14 = f32[4,256]{1,0:T(4,128)} slice(f32[8,256]{1,0:T(8,128)S(1)} %add.28), slice={[0:4], [0:256]} | slice | bytes 8192 | tf_op jit(solution)/shard_map/slice | solution.py:677
  (8 shorter events, 0.0 us)
Async XLA Ops:
  0.6 12.1 %copy-start = (bf16[2048,8]{0,1:T(8,128)(2,1)S(1)}, bf16[2048,8]{0,1:T(8,128)(2,1)}, u32[]{:S(2)}) copy-start(bf16[2048,8]{0,1:T(8,128)(2,1)} %param.22) | copy-start | bytes 98308
  0.6 15.3 %copy-start.1 = (bf16[256,1024]{1,0:T(8,128)(2,1)S(1)}, bf16[256,1024]{1,0:T(8,128)(2,1)}, u32[]{:S(2)}) copy-start(bf16[256,1024]{1,0:T(8,128)(2,1)} %cot_ref.1) | copy-start | bytes 1572868
  0.7 15.3 %copy-start.4 = (f32[1024]{0:T(1024)S(1)}, f32[1024]{0:T(1024)}, u32[]{:S(2)}) copy-start(f32[1024]{0:T(1024)} %param.28) | copy-start | bytes 12292
  0.7 15.3 %copy-start.6 = (f32[8]{0:T(128)S(1)}, f32[8]{0:T(128)}, u32[]{:S(2)}) copy-start(f32[8]{0:T(128)} %skip_ref.1) | copy-start | bytes 100
  0.7 15.3 %copy-start.8 = (f32[8]{0:T(128)S(1)}, f32[8]{0:T(128)}, u32[]{:S(2)}) copy-start(f32[8]{0:T(128)} %param.26) | copy-start | bytes 100
  0.7 15.3 %copy-start.7 = (f32[8]{0:T(128)S(1)}, f32[8]{0:T(128)}, u32[]{:S(2)}) copy-start(f32[8]{0:T(128)} %param.25) | copy-start | bytes 100
  0.7 15.3 %copy-start.3 = (f32[4,256]{1,0:T(4,128)S(1)}, f32[4,256]{1,0:T(4,128)}, u32[]{:S(2)}) copy-start(f32[4,256]{1,0:T(4,128)} %cs_ref.1) | copy-start | bytes 12292
  0.7 15.3 %copy-start.2 = (f32[4,1024]{1,0:T(4,128)S(1)}, f32[4,1024]{1,0:T(4,128)}, u32[]{:S(2)}) copy-start(f32[4,1024]{1,0:T(4,128)} %cv_ref.1) | copy-start | bytes 49156
  0.7 15.3 %copy-start.5 = (s32[4]{0:T(128)S(1)}, s32[4]{0:T(128)}, u32[]{:S(2)}) copy-start(s32[4]{0:T(128)} %rc_ref.1) | copy-start | bytes 52
  1.5 4.5 %collective-permute-start = (s32[1,256]{1,0:T(1,128)S(1)}, s32[1,256]{1,0:T(1,128)S(1)}, u32[]{:S(2)}, u32[]{:S(2)}) collective-permute-start(s32[1,256]{1,0:T(1,128)S(1)} %bitcast.15), channel_id=1, source_target_pairs={{0,4},{4,0},{8,12},{12,8},{16,20},{20,16},{24,28},{28,24},{1,5},{5... | collective-permute-start | bytes 3080 | tf_op jit(solution)/shard_map/ppermute | solution.py:623
  6.0 3.7 %collective-permute-start.1 = (s32[2,256]{1,0:T(2,128)S(1)}, s32[2,256]{1,0:T(2,128)S(1)}, u32[]{:S(2)}, u32[]{:S(2)}) collective-permute-start(s32[2,256]{1,0:T(2,128)S(1)} %pad_add_fusion.1), channel_id=1, source_target_pairs={{0,8},{4,12},{8,0},{12,4},{16,24},{20,28},{24,16},{28,20},{1,9},{5... | collective-permute-start | bytes 6152 | tf_op jit(solution)/shard_map/ppermute | solution.py:623
  9.6 6.3 %collective-permute-start.2 = (s32[4,256]{1,0:T(4,128)S(1)}, s32[4,256]{1,0:T(4,128)S(1)}, u32[]{:S(2)}, u32[]{:S(2)}) collective-permute-start(s32[4,256]{1,0:T(4,128)S(1)} %pad_add_fusion.near_ref), channel_id=1, source_target_pairs={{0,16},{4,20},{8,24},{12,28},{16,0},{20,4},{24,8},{28,12},{1,17},{... | collective-permute-start | bytes 12296 | tf_op jit(solution)/shard_map/ppermute | solution.py:623
  32.5 1.2 %collective-permute-start.3 = (f32[8,256]{1,0:T(8,128)S(1)}, f32[8,256]{1,0:T(8,128)S(1)}, u32[]{:S(2)}, u32[]{:S(2)}) collective-permute-start(f32[8,256]{1,0:T(8,128)S(1)} %get-tuple-element.11), channel_id=1, source_target_pairs={{0,1},{1,0},{2,3},{3,2},{4,5},{5,4},{6,7},{7,6},{8,9},{9,8},{10,11... | collective-permute-start | bytes 24584 | tf_op jit(solution)/shard_map/ppermute | solution.py:623
  33.7 3.7 %collective-permute-start.4 = (f32[8,256]{1,0:T(8,128)S(1)}, f32[8,256]{1,0:T(8,128)S(1)}, u32[]{:S(2)}, u32[]{:S(2)}) collective-permute-start(f32[8,256]{1,0:T(8,128)S(1)} %add.24), channel_id=1, source_target_pairs={{0,2},{1,3},{2,0},{3,1},{4,6},{5,7},{6,4},{7,5},{8,10},{9,11},{10,... | collective-permute-start | bytes 24584 | tf_op jit(solution)/shard_map/ppermute | solution.py:623
  37.4 3.7 %collective-permute-start.5 = (f32[8,256]{1,0:T(8,128)S(1)}, f32[8,256]{1,0:T(8,128)S(1)}, u32[]{:S(2)}, u32[]{:S(2)}) collective-permute-start(f32[8,256]{1,0:T(8,128)S(1)} %add.25), channel_id=1, source_target_pairs={{0,4},{4,0},{8,12},{12,8},{16,20},{20,16},{24,28},{28,24},{1,5},{5... | collective-permute-start | bytes 24584 | tf_op jit(solution)/shard_map/ppermute | solution.py:623
  41.0 3.7 %collective-permute-start.6 = (f32[8,256]{1,0:T(8,128)S(1)}, f32[8,256]{1,0:T(8,128)S(1)}, u32[]{:S(2)}, u32[]{:S(2)}) collective-permute-start(f32[8,256]{1,0:T(8,128)S(1)} %add.26), channel_id=1, source_target_pairs={{0,8},{4,12},{8,0},{12,4},{16,24},{20,28},{24,16},{28,20},{1,9},{5... | collective-permute-start | bytes 24584 | tf_op jit(solution)/shard_map/ppermute | solution.py:623
  44.7 4.5 %collective-permute-start.7 = (f32[8,256]{1,0:T(8,128)S(1)}, f32[8,256]{1,0:T(8,128)S(1)}, u32[]{:S(2)}, u32[]{:S(2)}) collective-permute-start(f32[8,256]{1,0:T(8,128)S(1)} %add.27), channel_id=1, source_target_pairs={{0,16},{4,20},{8,24},{12,28},{16,0},{20,4},{24,8},{28,12},{1,17},{... | collective-permute-start | bytes 24584 | tf_op jit(solution)/shard_map/ppermute | solution.py:623

commit v4 on v3

--- a/solution.py
+++ b/solution.py
@@ -14,7 +14,6 @@
 IDS = 4
 WINDOWS = IDS**CONV
 ROWS = WINDOWS + 16
-UNROLL = 2
 TABLES_VMEM = 53 * 2**20
 MIXER_VMEM = 53 * 2**20
 EPSILON = 1e-05
@@ -77,47 +76,46 @@
     return rows_of([p1, p2, p3, jnp.zeros_like(p1)])
 
 
-def tables_kernel(normed_ref, wv_hbm, ws_hbm, tv_ref, ts_ref, held_v, held_s, sems):
-    chunks, size, _ = held_v.shape
-    copies = [pltpu.make_async_copy(ws_hbm, held_s, sems.at[chunks])]
-    for i in range(chunks):
-        copies.append(pltpu.make_async_copy(wv_hbm.at[pl.ds(i * size, size), :], held_v.at[i], sems.at[i]))
+def tables_kernel(count, normed_ref, *refs):
+    weights, outs, held, sems = refs[:count], refs[count : 2 * count], refs[2 * count : 3 * count], refs[-1]
+    copies = []
+    for k in range(count):
+        chunks, size, _ = held[k].shape
+        for i in range(chunks):
+            part = weights[k].at[pl.ds(i * size, size), :]
+            copies.append(pltpu.make_async_copy(part, held[k].at[i], sems.at[len(copies)]))
     for copy in copies:
         copy.start()
     normed = normed_ref[...]
-    copies[0].wait()
-    ts_ref[0:IDS, :] = mm(normed, held_s[...])
-    ts_ref[IDS:, :] = jnp.zeros((8 - IDS, ts_ref.shape[1]), f32)
-    product = None
-    for i in range(chunks):
-        copies[1 + i].wait()
-        term = mm(normed[:, i * size : (i + 1) * size], held_v[i])
-        product = term if product is None else product + term
-    tv_ref[0:IDS, :] = product
-    tv_ref[IDS:, :] = jnp.zeros((8 - IDS, tv_ref.shape[1]), f32)
-
-
-def tables(normed, w_values, w_states):
-    depth, width = w_values.shape
-    chunks = 4
+    done = 0
+    for k in range(count):
+        chunks, size, _ = held[k].shape
+        product = None
+        for i in range(chunks):
+            copies[done].wait()
+            done += 1
+            term = mm(normed[:, i * size : (i + 1) * size], held[k][i])
+            product = term if product is None else product + term
+        outs[k][0:IDS, :] = product
+        outs[k][IDS:, :] = jnp.zeros((8 - IDS, product.shape[1]), f32)
+
+
+def tables(normed, weights, chunks):
     vmem = pl.BlockSpec(memory_space=pltpu.VMEM)
     hbm = pl.BlockSpec(memory_space=pl.ANY)
+    depth = normed.shape[1]
     return pl.pallas_call(
-        tables_kernel,
-        in_specs=[vmem, hbm, hbm],
-        out_specs=[vmem, vmem],
-        out_shape=[
-            jax.ShapeDtypeStruct((8, width), f32),
-            jax.ShapeDtypeStruct((8, w_states.shape[1]), f32),
-        ],
+        functools.partial(tables_kernel, len(weights)),
+        in_specs=[vmem] + [hbm] * len(weights),
+        out_specs=[vmem] * len(weights),
+        out_shape=[jax.ShapeDtypeStruct((8, weight.shape[1]), f32) for weight in weights],
         scratch_shapes=[
-            pltpu.VMEM((chunks, depth // chunks, width), bf16),
-            pltpu.VMEM(w_states.shape, bf16),
-            pltpu.SemaphoreType.DMA((1 + chunks,)),
-        ],
+            pltpu.VMEM((parts, depth // parts, weight.shape[1]), bf16) for weight, parts in zip(weights, chunks)
+        ]
+        + [pltpu.SemaphoreType.DMA((sum(chunks),))],
         compiler_params=pltpu.CompilerParams(vmem_limit_bytes=TABLES_VMEM),
         name="tables",
-    )(normed, w_values, w_states)
+    )(normed, *weights)
 
 
 def mixer_kernel(
@@ -126,9 +124,9 @@
     far_ref,
     rc_ref,
     skip_ref,
-    normed_ref,
     tv_ref,
     tbc_ref,
+    tz_ref,
     dt_ref,
     cv_ref,
     cs_ref,
@@ -136,11 +134,8 @@
     rate_ref,
     gain_ref,
     cot_ref,
-    wg_hbm,
     enc_hbm,
     grad_ref,
-    held_g,
-    sems,
     enc_ref,
     enc_sem,
     tok_s,
@@ -172,19 +167,12 @@
     heads = width // HEAD
     here = lax.axis_index("ctx")
     tp_place = lax.axis_index("tp")
-    chunks, size, _ = held_g.shape
-    copies = []
-    for i in range(chunks):
-        copies.append(pltpu.make_async_copy(wg_hbm.at[pl.ds(i * size, size), :], held_g.at[i], sems.at[i]))
-    for copy in copies:
-        copy.start()
-
     half = near_ref.shape[0]
     for r in range(devices):
         own = near_ref[r : r + 1, :] if r < half else far_ref[r - half : r - half + 1, :]
         tok_s[pl.ds(jnp.bitwise_xor(here, r), 1), :] = own
     tok = tok_s[...]
-    rc = [rc_ref[t] for t in range(IDS)]
+    rc = [rc_ref[:, t : t + 1] for t in range(IDS)]
     rtok = jnp.zeros_like(tok)
     for t in range(IDS):
         rtok = jnp.where(tok == t, rc[t], rtok)
@@ -285,14 +273,6 @@
     table_bc = tbc_ref[...]
     taps_v = tap_parts(tv_ref[...], cv_ref[...])
     taps_s = tap_parts(table_bc, cs_ref[...])
-    product = None
-    for i in range(chunks):
-        copies[i].wait()
-        term = mm(normed_ref[:, i * size : (i + 1) * size], held_g[i])
-        product = term if product is None else product + term
-    gates = rows_of([product, jnp.zeros((8 - IDS, width), f32)])
-    gates = gates * sigmoid(gates)
-
     weights = mm(onehot_s[...], weight_s[...], NT)
     weights = weights + pltpu.roll(weights, 64, 1)
 
@@ -370,13 +350,6 @@
             acol_s[s, h] = jnp.broadcast_to(turned[:, at + heads : at + heads + 1], (count, 128))
     base = 4 * heads
     tcol_s[...] = jnp.broadcast_to(turned[:, base + 2 : base + 3], (count, 128))
-    gate_s[0] = gates
-    for t in range(IDS):
-        picked = gates[0:1, :]
-        for other in range(1, IDS):
-            picked = jnp.where(rc[t] == other, gates[other : other + 1, :], picked)
-        gate_s[1, t : t + 1, :] = picked
-
     own_onehot = []
     lane_k = iota((count, ROWS), 1).astype(f32)
     picks = []
@@ -426,6 +399,17 @@
         states.append(rows_of(split(state)))
         far_s[s] = stacked(own_c[s], states[s])
 
+    gates = tz_ref[...]
+    gates = gates * sigmoid(gates)
+
+    gate_s[0] = gates
+    for t in range(IDS):
+        picked = gates[0:1, :]
+        for other in range(1, IDS):
+            picked = jnp.where(rc[t] == other, gates[other : other + 1, :], picked)
+        gate_s[1, t : t + 1, :] = picked
+
+
     q_s[...] = jnp.zeros_like(q_s)
     tiles = count // 128
     triangle = [iota((128, 128), 0) >= iota((128, 128), 1), iota((128, 128), 0) <= iota((128, 128), 1)]
@@ -433,18 +417,18 @@
     nothing = jnp.zeros((128, 128), bf16)
     part = lambda j: slice(j * 128, (j + 1) * 128)
 
-    def one_head(h, _):
-        columns = pl.ds(pl.multiple_of(h * HEAD, HEAD), HEAD)
-        columns2 = pl.ds(pl.multiple_of(h * 2 * HEAD, 2 * HEAD), 2 * HEAD)
+    def one_head(h):
+        columns = slice(h * HEAD, (h + 1) * HEAD)
+        columns2 = slice(h * 2 * HEAD, (h + 1) * 2 * HEAD)
         gain = gain_ref[:, columns]
-        skip = skip_ref[h]
+        skip = skip_ref[:, h : h + 1]
         outs = [None] * tiles
         rate_row = jnp.zeros((1, 128), f32)
         bias_row = jnp.zeros((1, 128), f32)
         factors, ys = [], []
         for s in range(2):
-            log_row = row_s[s, 0, pl.ds(h, 1), :]
-            step_row = row_s[s, 1, pl.ds(h, 1), :]
+            log_row = row_s[s, 0, h : h + 1, :]
+            step_row = row_s[s, 1, h : h + 1, :]
             highs, lows, own = [], [], {}
             for i in range(tiles):
                 lcol = lcol_s[s, h, part(i), :]
@@ -468,8 +452,8 @@
             ys.append(both[:, :HEAD] + both[:, HEAD:])
         for s in range(2):
             column_sums = [jnp.zeros((1, 128), f32) for _ in range(tiles)]
-            log_row = row_s[s, 0, pl.ds(h, 1), :]
-            mixed_row = row_s[s, 2, pl.ds(h, 1), :]
+            log_row = row_s[s, 0, h : h + 1, :]
+            mixed_row = row_s[s, 2, h : h + 1, :]
             highs, lows = [], []
             for i in range(tiles):
                 lcol = lcol_s[s, h, part(i), :]
@@ -504,15 +488,11 @@
                 bias_row += mixed_row[:, part(j)] * column_sums[j]
         for i in range(tiles):
             enc_ref[i * 128 : (i + 1) * 128, columns] = (outs[i] * gain).astype(enc_ref.dtype)
-        acc_s[0, pl.ds(h, 1), :] = rate_row
-        acc_s[1, pl.ds(h, 1), :] = bias_row
-
-    def some_heads(g, _):
-        for i in range(UNROLL):
-            one_head(g * UNROLL + i, 0)
-        return 0
-
-    lax.fori_loop(0, heads // UNROLL, some_heads, 0)
+        acc_s[0, h : h + 1, :] = rate_row
+        acc_s[1, h : h + 1, :] = bias_row
+
+    for h in range(heads):
+        one_head(h)
 
     enc_copy = pltpu.make_async_copy(enc_ref, enc_hbm, enc_sem)
     enc_copy.start()
@@ -554,17 +534,13 @@
     enc_copy.wait()
 
 
-def mixer(near, far, rc_map, skip, small, w_gates, scale):
+def mixer(near, far, rc_map, skip, small, scale):
     devices, count = near.shape[0] + far.shape[0], near.shape[1]
-    depth, width = w_gates.shape
+    width = small[0].shape[1]
     heads = width // HEAD
-    chunks = 4
     vmem = pl.BlockSpec(memory_space=pltpu.VMEM)
-    smem = pl.BlockSpec(memory_space=pltpu.SMEM)
     hbm = pl.BlockSpec(memory_space=pl.ANY)
     scratch = [
-        ((chunks, depth // chunks, width), bf16),
-        chunks,
         ((count, width), bf16),
         None,
         ((devices, count), jnp.int32),
@@ -599,7 +575,7 @@
 
     return pl.pallas_call(
         functools.partial(mixer_kernel, scale),
-        in_specs=[vmem, vmem, smem, smem] + [vmem] * len(small) + [hbm],
+        in_specs=[vmem] * (4 + len(small)),
         out_specs=[hbm, vmem],
         out_shape=[
             jax.ShapeDtypeStruct((count, width), bf16),
@@ -611,10 +587,9 @@
     )(
         near,
         far,
-        rc_map,
-        skip,
+        rc_map.reshape(1, IDS),
+        skip.reshape(1, heads),
         *small,
-        w_gates,
     )
 
 
@@ -642,23 +617,31 @@
 ):
     devices = lax.axis_size("ctx")
     count = tokens.shape[0]
-    near = jnp.minimum(tokens, IDS - 1).reshape(1, count)
-    far = exchange(near, "ctx", 1)
-    distance = 2
-    while distance < devices:
-        near = jnp.concatenate([near, far], axis=0)
-        far = exchange(near, "ctx", distance)
-        distance *= 2
     scale = 1.0 / math.sqrt(count * devices * HEAD)
     embedded = embedding.astype(f32)
     mean = jnp.mean(embedded * embedded, axis=1, keepdims=True)
     normed = (embedded * lax.rsqrt(mean + EPSILON) * norm_gain).astype(bf16)
-    tv, tbc = tables(normed, w_values, w_states)
+    near = jnp.minimum(tokens, IDS - 1).reshape(1, count)
+    far = exchange(tokens.reshape(1, count), "ctx", 1)
+    tv = tbc = None
+    distance = 2
+    while distance < devices:
+        near = jnp.concatenate([near, far], axis=0)
+        if distance == 2:
+            near, normed = lax.optimization_barrier((near, normed))
+        if distance * 2 >= devices:
+            tbc, tv = tables(normed, [w_states, w_values], [1, 4])
+            near, tbc, tv, normed = lax.optimization_barrier((near, tbc, tv, normed))
+        far = exchange(near, "ctx", distance)
+        distance *= 2
+    if tv is None:
+        tbc, tv = tables(normed, [w_states, w_values], [1, 4])
+    (tz,) = tables(normed, [w_gates], [4])
     dt = lax.dot_general(w_steps, normed, (((0,), (1,)), ((), ())), preferred_element_type=f32)
     small = [
-        normed,
         tv,
         tbc,
+        tz,
         dt,
         conv_values,
         conv_states,
@@ -667,7 +650,7 @@
         head_gain.reshape(1, -1),
         cotangent,
     ]
-    encoded, grads = mixer(near, far, rc_map, skip_gain, small, w_gates, scale)
+    encoded, grads = mixer(near, far, rc_map, skip_gain, small, scale)
     for axis in ("tp", "ctx"):
         distance = 1
         while distance < lax.axis_size(axis):

time: 50.8 us -> 47 us (0.925)
  Pallas kernels: 19.5 us -> 18 us
  starting transfers between devices: 14 us -> 12.6 us
  waiting for transfers between devices: 12.3 us -> 11.4 us
    pallas_call x2 -> x3, Pallas kernels: 19.5 us -> 18 us  [the longest x1 12.5 us: mixer(): pl.pallas_call(functools.partial(mixer_kernel, scale), in_specs=[vmem] *...]
    ppermute x8, starting transfers between devices: 14 us -> 12.6 us  [exchange(): return lax.ppermute(value, axis, [(i, i ^ distance) for i in range(size)])]
    ppermute x8, waiting for transfers between devices: 12.3 us -> 11.4 us  [exchange(): return lax.ppermute(value, axis, [(i, i ^ distance) for i in range(size)])]
  transfers between devices with their start and end apart: 8 -> 8, of which waited for: 7 -> 5; matrix products, arithmetic and copies ran while one was open for 4% -> 5% of each run, Pallas kernels for 6% -> 12%
where the time goes in v4:
time: 47 us; the launch traced here: 46.6 us
  Pallas kernels  18 us (38%)
  starting transfers between devices  12.6 us (27%)
  waiting for transfers between devices  11.4 us (24%)
  other arithmetic  2.37 us (5%)
  local copies, waits for them, and re-layouts  1.17 us (2%)
  between operations  0.84 us (2%)
    ppermute x8, starting transfers between devices, exchange(): return lax.ppermute(value, axis, [(i, i ^ distance) for i in range(size)])  12.6 us
    pallas_call x1, Pallas kernels, mixer(): pl.pallas_call(functools.partial(mixer_kernel, scale), in_specs=[vmem] *...  12.5 us
    ppermute x8, waiting for transfers between devices, exchange(): return lax.ppermute(value, axis, [(i, i ^ distance) for i in range(size)])  11.4 us
    pallas_call x2, Pallas kernels, tables(): pl.pallas_call(functools.partial(tables_kernel, len(weights)), in_specs=[...  5.55 us
  transfers between devices with their start and end apart: 8, of which 5 were waited for; matrix products, arithmetic and copies ran while one was open for 5% of the time, Pallas kernels for 12%

profile of v4, /device:TPU:0, one launch (start us, length us, event | category | flops | bytes accessed | tf_op | source)
XLA Modules:
  0.0 46.6 jit_solution(2825836595069189325)
XLA Ops:
  0.6 0.0 copy-start
  0.6 3.0 %collective-permute-start = (s32[1,256]{1,0:T(1,128)}, s32[1,256]{1,0:T(1,128)S(1)}, u32[]{:S(2)}, u32[]{:S(2)}) collective-permute-start(s32[1,256]{1,0:T(1,128)} %bitcast.21), channel_id=1, source_target_pairs={{0,4},{4,0},{8,12},{12,8},{16,20},{20,16},{24,28},{28,24},{1,5},{5... | collective-permute-start | bytes 3080 | tf_op jit(solution)/shard_map/ppermute | solution.py:598
  3.6 0.8 %fusion = f32[4]{0:T(128)S(1)} fusion(bf16[4,2048]{1,0:T(4,128)(2,1)} %param.17), kind=kLoop, calls=%fused_computation.3 | loop fusion | flops 24572 | bytes 16400 | tf_op jit(solution)/shard_map/reduce_sum | solution.py:622
  4.5 0.8 %fusion.2.normed_ref = bf16[4,2048]{1,0:T(4,128)(2,1)S(1)} fusion(bf16[4,2048]{1,0:T(4,128)(2,1)} %param.17, f32[2048]{0:T(1024)} %param.18, f32[4]{0:T(128)S(1)} %add_rsqrt_fusion), kind=kLoop, calls=%fused_computation.5 | loop fusion | flops 32768 | bytes 40976 | tf_op jit(solution)/shard_map/convert_element_type | solution.py:623
  5.3 0.7 %broadcast_minimum_fusion = s32[256]{0:T(256)S(1)} fusion(s32[256]{0:T(256)} %param.15), kind=kLoop, calls=%fused_computation.11 | loop fusion | flops 256 | bytes 2048 | tf_op jit(solution)/shard_map/min | solution.py:624
  6.0 0.0 collective-permute-done
  6.0 0.0 copy-start.1
  6.0 0.0 copy-start.2
  6.0 0.0 copy-start.3
  6.0 0.0 copy-start.4
  6.1 0.0 copy-start.5
  6.1 0.0 copy-start.6
  6.1 0.0 copy-start.7
  6.1 0.0 copy-start.8
  6.1 1.6 %collective-permute-start.1 = (s32[2,256]{1,0:T(2,128)S(1)}, s32[2,256]{1,0:T(2,128)S(1)}, u32[]{:S(2)}, u32[]{:S(2)}) collective-permute-start(s32[2,256]{1,0:T(2,128)S(1)} %pad_add_fusion.1), channel_id=1, source_target_pairs={{0,8},{4,12},{8,0},{12,4},{16,24},{20,28},{24,16},{28,20},{1,9},{5... | collective-permute-start | bytes 6152 | tf_op jit(solution)/shard_map/ppermute | solution.py:598
  7.7 3.1 %tables.2 = (f32[8,256]{1,0:T(8,128)S(1)}, f32[8,1024]{1,0:T(8,128)S(1)}) custom-call(bf16[4,2048]{1,0:T(4,128)(2,1)S(1)} %fusion.2.normed_ref, bf16[2048,256]{1,0:T(8,128)(2,1)} %refs_0_.2, bf16[2048,1024]{1,0:T(8,128)(2,1)} %refs_1_.1), custom_call_target="tpu_custom_call" | custom-call | tf_op jit(solution)/shard_map/tables/pallas_call | solution.py:107
  10.8 0.0 collective-permute-done.1
  10.9 2.7 %collective-permute-start.2 = (s32[4,256]{1,0:T(4,128)S(1)}, s32[4,256]{1,0:T(4,128)S(1)}, u32[]{:S(2)}, u32[]{:S(2)}) collective-permute-start(s32[4,256]{1,0:T(4,128)S(1)} %pad_add_fusion.near_ref), channel_id=1, source_target_pairs={{0,16},{4,20},{8,24},{12,28},{16,0},{20,4},{24,8},{28,12},{1,17},{... | collective-permute-start | bytes 12296 | tf_op jit(solution)/shard_map/ppermute | solution.py:598
  13.5 0.0 copy-done
  13.5 0.1 convolution_bitcast_fusion.dt_ref
  13.6 2.5 %tables.3.tz_ref = f32[8,1024]{1,0:T(8,128)S(1)} custom-call(bf16[4,2048]{1,0:T(4,128)(2,1)S(1)} %fusion.2.normed_ref, bf16[2048,1024]{1,0:T(8,128)(2,1)} %refs_0_.3), custom_call_target="tpu_custom_call" | custom-call | tf_op jit(solution)/shard_map/tables/pallas_call | solution.py:107
  16.1 0.0 collective-permute-done.2.far_ref
  16.1 0.0 copy-done.1
  16.1 0.0 copy-done.2
  16.2 0.0 copy-done.3
  16.2 0.0 copy-done.4
  16.2 0.0 copy-done.5
  16.2 0.0 copy-done.6
  16.2 0.0 copy-done.7
  16.2 0.0 copy-done.8
  16.2 12.5 %mixer.1 = (bf16[256,1024]{1,0:T(8,128)(2,1)}, f32[8,256]{1,0:T(8,128)S(1)}) custom-call(s32[4,256]{1,0:T(4,128)S(1)} %pad_add_fusion.near_ref, s32[4,256]{1,0:T(4,128)S(1)} %collective-permute-done.2.far_ref, s32[1,4]{1,0:T(1,128)S(1)} %bitcast.16, f32[1,8]{1,0:T(1,128)S(1)} %bitcast.17, f32[8,1024]{1,0:T(8,128)S(1)} %get-tuple-element.19.tv_ref, ...), custom_call_target="tpu_custom_call" | custom-call | tf_op jit(solution)/shard_map/mixer/pallas_call | solution.py:576
  28.7 0.1 collective-permute-start.3
  28.8 1.2 %collective-permute-done.3 = f32[8,256]{1,0:T(8,128)S(1)} collective-permute-done((f32[8,256]{1,0:T(8,128)S(1)}, f32[8,256]{1,0:T(8,128)S(1)}, u32[]{:S(2)}, u32[]{:S(2)}) %collective-permute-start.3) | collective-permute-done | bytes 8224 | tf_op jit(solution)/shard_map/ppermute | solution.py:598
  29.9 1.5 %collective-permute-start.4 = (f32[8,256]{1,0:T(8,128)S(1)}, f32[8,256]{1,0:T(8,128)S(1)}, u32[]{:S(2)}, u32[]{:S(2)}) collective-permute-start(f32[8,256]{1,0:T(8,128)S(1)} %add.24), channel_id=1, source_target_pairs={{0,2},{1,3},{2,0},{3,1},{4,6},{5,7},{6,4},{7,5},{8,10},{9,11},{10,... | collective-permute-start | bytes 24584 | tf_op jit(solution)/shard_map/ppermute | solution.py:598
  31.5 2.1 %collective-permute-done.4 = f32[8,256]{1,0:T(8,128)S(1)} collective-permute-done((f32[8,256]{1,0:T(8,128)S(1)}, f32[8,256]{1,0:T(8,128)S(1)}, u32[]{:S(2)}, u32[]{:S(2)}) %collective-permute-start.4) | collective-permute-done | bytes 8224 | tf_op jit(solution)/shard_map/ppermute | solution.py:598
  33.6 1.4 %collective-permute-start.5 = (f32[8,256]{1,0:T(8,128)S(1)}, f32[8,256]{1,0:T(8,128)S(1)}, u32[]{:S(2)}, u32[]{:S(2)}) collective-permute-start(f32[8,256]{1,0:T(8,128)S(1)} %add.25), channel_id=1, source_target_pairs={{0,4},{4,0},{8,12},{12,8},{16,20},{20,16},{24,28},{28,24},{1,5},{5... | collective-permute-start | bytes 24584 | tf_op jit(solution)/shard_map/ppermute | solution.py:598
  35.0 2.2 %collective-permute-done.5 = f32[8,256]{1,0:T(8,128)S(1)} collective-permute-done((f32[8,256]{1,0:T(8,128)S(1)}, f32[8,256]{1,0:T(8,128)S(1)}, u32[]{:S(2)}, u32[]{:S(2)}) %collective-permute-start.5) | collective-permute-done | bytes 8224 | tf_op jit(solution)/shard_map/ppermute | solution.py:598
  37.3 0.5 collective-permute-start.6
  37.7 3.2 %collective-permute-done.6 = f32[8,256]{1,0:T(8,128)S(1)} collective-permute-done((f32[8,256]{1,0:T(8,128)S(1)}, f32[8,256]{1,0:T(8,128)S(1)}, u32[]{:S(2)}, u32[]{:S(2)}) %collective-permute-start.6) | collective-permute-done | bytes 8224 | tf_op jit(solution)/shard_map/ppermute | solution.py:598
  40.9 1.9 %collective-permute-start.7 = (f32[8,256]{1,0:T(8,128)S(1)}, f32[8,256]{1,0:T(8,128)S(1)}, u32[]{:S(2)}, u32[]{:S(2)}) collective-permute-start(f32[8,256]{1,0:T(8,128)S(1)} %add.27), channel_id=1, source_target_pairs={{0,16},{4,20},{8,24},{12,28},{16,0},{20,4},{24,8},{28,12},{1,17},{... | collective-permute-start | bytes 24584 | tf_op jit(solution)/shard_map/ppermute | solution.py:598
  42.8 2.7 %collective-permute-done.7 = f32[8,256]{1,0:T(8,128)S(1)} collective-permute-done((f32[8,256]{1,0:T(8,128)S(1)}, f32[8,256]{1,0:T(8,128)S(1)}, u32[]{:S(2)}, u32[]{:S(2)}) %collective-permute-start.7) | collective-permute-done | bytes 8224 | tf_op jit(solution)/shard_map/ppermute | solution.py:598
  45.5 0.5 %slice_bitcast_fusion = (f32[32]{0:T(128)}, f32[32]{0:T(128)}) fusion(f32[8,256]{1,0:T(8,128)S(1)} %add.28), kind=kLoop, calls=%fused_computation.8 | loop fusion | bytes 512 | tf_op jit(solution)/shard_map/squeeze | solution.py:660
  46.0 0.6 %slice.14 = f32[4,256]{1,0:T(4,128)} slice(f32[8,256]{1,0:T(8,128)S(1)} %add.28), slice={[0:4], [0:256]} | slice | bytes 8192 | tf_op jit(solution)/shard_map/slice | solution.py:660
  (8 shorter events, 0.0 us)
Async XLA Ops:
  0.6 12.9 %copy-start = (bf16[2048,8]{0,1:T(8,128)(2,1)S(1)}, bf16[2048,8]{0,1:T(8,128)(2,1)}, u32[]{:S(2)}) copy-start(bf16[2048,8]{0,1:T(8,128)(2,1)} %param.22) | copy-start | bytes 98308
  0.6 5.4 %collective-permute-start = (s32[1,256]{1,0:T(1,128)}, s32[1,256]{1,0:T(1,128)S(1)}, u32[]{:S(2)}, u32[]{:S(2)}) collective-permute-start(s32[1,256]{1,0:T(1,128)} %bitcast.21), channel_id=1, source_target_pairs={{0,4},{4,0},{8,12},{12,8},{16,20},{20,16},{24,28},{28,24},{1,5},{5... | collective-permute-start | bytes 3080 | tf_op jit(solution)/shard_map/ppermute | solution.py:598
  6.0 10.1 %copy-start.1 = (bf16[256,1024]{1,0:T(8,128)(2,1)S(1)}, bf16[256,1024]{1,0:T(8,128)(2,1)}, u32[]{:S(2)}) copy-start(bf16[256,1024]{1,0:T(8,128)(2,1)} %cot_ref.1) | copy-start | bytes 1572868
  6.0 10.1 %copy-start.2 = (f32[4,1024]{1,0:T(4,128)S(1)}, f32[4,1024]{1,0:T(4,128)}, u32[]{:S(2)}) copy-start(f32[4,1024]{1,0:T(4,128)} %cv_ref.1) | copy-start | bytes 49156
  6.0 10.1 %copy-start.3 = (f32[4,256]{1,0:T(4,128)S(1)}, f32[4,256]{1,0:T(4,128)}, u32[]{:S(2)}) copy-start(f32[4,256]{1,0:T(4,128)} %cs_ref.1) | copy-start | bytes 12292
  6.0 10.1 %copy-start.4 = (f32[1024]{0:T(1024)S(1)}, f32[1024]{0:T(1024)}, u32[]{:S(2)}) copy-start(f32[1024]{0:T(1024)} %param.28) | copy-start | bytes 12292
  6.1 10.1 %copy-start.5 = (s32[4]{0:T(128)S(1)}, s32[4]{0:T(128)}, u32[]{:S(2)}) copy-start(s32[4]{0:T(128)} %param.16) | copy-start | bytes 52
  6.1 10.1 %copy-start.6 = (f32[8]{0:T(128)S(1)}, f32[8]{0:T(128)}, u32[]{:S(2)}) copy-start(f32[8]{0:T(128)} %param.27) | copy-start | bytes 100
  6.1 10.1 %copy-start.7 = (f32[8]{0:T(128)S(1)}, f32[8]{0:T(128)}, u32[]{:S(2)}) copy-start(f32[8]{0:T(128)} %param.25) | copy-start | bytes 100
  6.1 10.1 %copy-start.8 = (f32[8]{0:T(128)S(1)}, f32[8]{0:T(128)}, u32[]{:S(2)}) copy-start(f32[8]{0:T(128)} %param.26) | copy-start | bytes 100
  6.1 4.7 %collective-permute-start.1 = (s32[2,256]{1,0:T(2,128)S(1)}, s32[2,256]{1,0:T(2,128)S(1)}, u32[]{:S(2)}, u32[]{:S(2)}) collective-permute-start(s32[2,256]{1,0:T(2,128)S(1)} %pad_add_fusion.1), channel_id=1, source_target_pairs={{0,8},{4,12},{8,0},{12,4},{16,24},{20,28},{24,16},{28,20},{1,9},{5... | collective-permute-start | bytes 6152 | tf_op jit(solution)/shard_map/ppermute | solution.py:598
  10.9 5.3 %collective-permute-start.2 = (s32[4,256]{1,0:T(4,128)S(1)}, s32[4,256]{1,0:T(4,128)S(1)}, u32[]{:S(2)}, u32[]{:S(2)}) collective-permute-start(s32[4,256]{1,0:T(4,128)S(1)} %pad_add_fusion.near_ref), channel_id=1, source_target_pairs={{0,16},{4,20},{8,24},{12,28},{16,0},{20,4},{24,8},{28,12},{1,17},{... | collective-permute-start | bytes 12296 | tf_op jit(solution)/shard_map/ppermute | solution.py:598
  28.7 1.2 %collective-permute-start.3 = (f32[8,256]{1,0:T(8,128)S(1)}, f32[8,256]{1,0:T(8,128)S(1)}, u32[]{:S(2)}, u32[]{:S(2)}) collective-permute-start(f32[8,256]{1,0:T(8,128)S(1)} %get-tuple-element.23), channel_id=1, source_target_pairs={{0,1},{1,0},{2,3},{3,2},{4,5},{5,4},{6,7},{7,6},{8,9},{9,8},{10,11... | collective-permute-start | bytes 24584 | tf_op jit(solution)/shard_map/ppermute | solution.py:598
  29.9 3.7 %collective-permute-start.4 = (f32[8,256]{1,0:T(8,128)S(1)}, f32[8,256]{1,0:T(8,128)S(1)}, u32[]{:S(2)}, u32[]{:S(2)}) collective-permute-start(f32[8,256]{1,0:T(8,128)S(1)} %add.24), channel_id=1, source_target_pairs={{0,2},{1,3},{2,0},{3,1},{4,6},{5,7},{6,4},{7,5},{8,10},{9,11},{10,... | collective-permute-start | bytes 24584 | tf_op jit(solution)/shard_map/ppermute | solution.py:598
  33.6 3.7 %collective-permute-start.5 = (f32[8,256]{1,0:T(8,128)S(1)}, f32[8,256]{1,0:T(8,128)S(1)}, u32[]{:S(2)}, u32[]{:S(2)}) collective-permute-start(f32[8,256]{1,0:T(8,128)S(1)} %add.25), channel_id=1, source_target_pairs={{0,4},{4,0},{8,12},{12,8},{16,20},{20,16},{24,28},{28,24},{1,5},{5... | collective-permute-start | bytes 24584 | tf_op jit(solution)/shard_map/ppermute | solution.py:598
  37.3 3.7 %collective-permute-start.6 = (f32[8,256]{1,0:T(8,128)S(1)}, f32[8,256]{1,0:T(8,128)S(1)}, u32[]{:S(2)}, u32[]{:S(2)}) collective-permute-start(f32[8,256]{1,0:T(8,128)S(1)} %add.26), channel_id=1, source_target_pairs={{0,8},{4,12},{8,0},{12,4},{16,24},{20,28},{24,16},{28,20},{1,9},{5... | collective-permute-start | bytes 24584 | tf_op jit(solution)/shard_map/ppermute | solution.py:598
  40.9 4.5 %collective-permute-start.7 = (f32[8,256]{1,0:T(8,128)S(1)}, f32[8,256]{1,0:T(8,128)S(1)}, u32[]{:S(2)}, u32[]{:S(2)}) collective-permute-start(f32[8,256]{1,0:T(8,128)S(1)} %add.27), channel_id=1, source_target_pairs={{0,16},{4,20},{8,24},{12,28},{16,0},{20,4},{24,8},{28,12},{1,17},{... | collective-permute-start | bytes 24584 | tf_op jit(solution)/shard_map/ppermute | solution.py:598

commit v5 on v4

--- a/solution.py
+++ b/solution.py
@@ -161,6 +161,7 @@
     score_s,
     q_s,
     acc_s,
+    back_s,
 ):
     devices, count = tok_s.shape
     width = cv_ref.shape[1]
@@ -375,12 +376,24 @@
             x_s[s, :, h * HEAD : (h + 1) * HEAD] = got[:, :HEAD] + got[:, HEAD:]
     bc_high = gather(bc[0][regular], bc[0][edges])
     bc_low = gather(bc[1][regular], bc[1][edges])
-    own_b, own_c, states = [], [], []
+    gates = tz_ref[...]
+    gates = gates * sigmoid(gates)
+
+    gate_s[0] = gates
+    for t in range(IDS):
+        picked = gates[0:1, :]
+        for other in range(1, IDS):
+            picked = jnp.where(rc[t] == other, gates[other : other + 1, :], picked)
+        gate_s[1, t : t + 1, :] = picked
+    own_b, own_c, states = [], [], [None, None]
     for s in range(2):
         high, low = bc_high[s].astype(bf16), bc_low[s].astype(bf16)
         own_b.append((high[:, :STATE], low[:, :STATE]))
         own_c.append((high[:, STATE:], low[:, STATE:]))
         score_s[s] = stacked(own_c[s], lanes_of(own_b[s]), NT)
+    b2 = lanes_of([part[regular] for part in b_all])
+
+    def enter(s):
         for h in range(heads):
             at = 3 * s * heads + h
             columns = slice(h * HEAD, (h + 1) * HEAD)
@@ -388,7 +401,6 @@
             wh_s[s, :WINDOWS, columns], wl_s[s, :WINDOWS, columns] = weighted
             weighted = split(edge_s[:, columns] * weights[WINDOWS:, at : at + 1])
             wh_s[s, WINDOWS:, columns], wl_s[s, WINDOWS:, columns] = weighted
-        b2 = lanes_of([part[regular] for part in b_all])
         state = mm(b2, wh_s[s, regular], TN)
         state = state[:STATE] + state[STATE:] + mm(b2[:, :STATE], wl_s[s, regular], TN)
         state = state + mm(
@@ -396,19 +408,8 @@
             rows_of([wh_s[s, edges], wl_s[s, edges], wh_s[s, edges]]),
             TN,
         )
-        states.append(rows_of(split(state)))
+        states[s] = rows_of(split(state))
         far_s[s] = stacked(own_c[s], states[s])
-
-    gates = tz_ref[...]
-    gates = gates * sigmoid(gates)
-
-    gate_s[0] = gates
-    for t in range(IDS):
-        picked = gates[0:1, :]
-        for other in range(1, IDS):
-            picked = jnp.where(rc[t] == other, gates[other : other + 1, :], picked)
-        gate_s[1, t : t + 1, :] = picked
-
 
     q_s[...] = jnp.zeros_like(q_s)
     tiles = count // 128
@@ -417,14 +418,8 @@
     nothing = jnp.zeros((128, 128), bf16)
     part = lambda j: slice(j * 128, (j + 1) * 128)
 
-    def one_head(h):
-        columns = slice(h * HEAD, (h + 1) * HEAD)
+    def mix(h):
         columns2 = slice(h * 2 * HEAD, (h + 1) * 2 * HEAD)
-        gain = gain_ref[:, columns]
-        skip = skip_ref[:, h : h + 1]
-        outs = [None] * tiles
-        rate_row = jnp.zeros((1, 128), f32)
-        bias_row = jnp.zeros((1, 128), f32)
         factors, ys = [], []
         for s in range(2):
             log_row = row_s[s, 0, h : h + 1, :]
@@ -450,10 +445,18 @@
             both = mm(rows_of(highs + lows), x2_s[s, :, columns2])
             both = both[:count] + both[count:]
             ys.append(both[:, :HEAD] + both[:, HEAD:])
+        return factors, ys
+
+    def gate_rows(h, ys):
+        columns = slice(h * HEAD, (h + 1) * HEAD)
+        columns2 = slice(h * 2 * HEAD, (h + 1) * 2 * HEAD)
+        gain = gain_ref[:, columns]
+        skip = skip_ref[:, h : h + 1]
+        outs = [None] * tiles
+        rate_row = jnp.zeros((1, 128), f32)
+        bias_row = jnp.zeros((1, 128), f32)
+        pairs = []
         for s in range(2):
-            column_sums = [jnp.zeros((1, 128), f32) for _ in range(tiles)]
-            log_row = row_s[s, 0, h : h + 1, :]
-            mixed_row = row_s[s, 2, h : h + 1, :]
             highs, lows = [], []
             for i in range(tiles):
                 lcol = lcol_s[s, h, part(i), :]
@@ -477,22 +480,56 @@
                 rate_row += jnp.sum(lcol * row_terms, axis=0, keepdims=True)
                 bias_row += jnp.sum(acol_s[s, h, part(i), :] * row_terms, axis=0, keepdims=True)
                 dh_s[s, part(i), columns], dl_s[s, part(i), columns] = split(grown * dy)
-            both = mm(rows_of(highs + lows), x2_s[s, :, columns2], NT)
+            pairs.append(mm(rows_of(highs + lows), x2_s[s, :, columns2], NT))
+        for i in range(tiles):
+            enc_ref[i * 128 : (i + 1) * 128, columns] = (outs[i] * gain).astype(enc_ref.dtype)
+        return pairs, rate_row, bias_row
+
+    def settle(h, factors, pairs, rate_row, bias_row):
+        for s in range(2):
+            column_sums = [jnp.zeros((1, 128), f32) for _ in range(tiles)]
+            log_row = row_s[s, 0, h : h + 1, :]
+            mixed_row = row_s[s, 2, h : h + 1, :]
             for i, j in factors[s]:
-                e = both[part(i), part(j)] + both[part(tiles + i), part(j)]
+                e = pairs[s][part(i), part(j)] + pairs[s][part(tiles + i), part(j)]
                 e = e * factors[s][i, j]
                 q_s[s, part(i), part(j)] += e
                 column_sums[j] = column_sums[j] + jnp.sum(e * score_s[s, part(i), part(j)], axis=0, keepdims=True)
             for j in range(tiles):
                 rate_row -= log_row[:, part(j)] * column_sums[j]
                 bias_row += mixed_row[:, part(j)] * column_sums[j]
-        for i in range(tiles):
-            enc_ref[i * 128 : (i + 1) * 128, columns] = (outs[i] * gain).astype(enc_ref.dtype)
         acc_s[0, h : h + 1, :] = rate_row
         acc_s[1, h : h + 1, :] = bias_row
 
+    def reach_back(first):
+        columns = slice(first * HEAD, (first + 2) * HEAD)
+        for s in range(2):
+            back = mm(lanes_of(own_c[s]), dh_s[s, :, columns], TN)
+            back = back[:STATE] + back[STATE:] + mm(own_c[s][0], dl_s[s, :, columns], TN)
+            back = rows_of(split(back))
+            back_s[s, :, columns] = back
+            reach = stacked(b_all, back)
+            for h in (first, first + 1):
+                at = 3 * s * heads + heads + h
+                own = slice((h - first) * HEAD, (h - first + 1) * HEAD)
+                whole = slice(h * HEAD, (h + 1) * HEAD)
+                terms = reach[:, own] * rows_of([xw_s[:, whole], edge_s[:, whole]])
+                acc_s[0, h : h + 1, :] += jnp.sum(terms * weights[:, at : at + 1], axis=0, keepdims=True)
+                acc_s[1, h : h + 1, :] += jnp.sum(
+                    terms * weights[:, at + heads : at + heads + 1], axis=0, keepdims=True
+                )
+
+    mixed = {0: mix(0)}
+    enter(0)
+    mixed[1] = mix(1)
+    enter(1)
     for h in range(heads):
-        one_head(h)
+        if 1 <= h < heads - 1:
+            mixed[h + 1] = mix(h + 1)
+        factors, ys = mixed.pop(h)
+        settle(h, factors, *gate_rows(h, ys))
+        if h % 2 == 1:
+            reach_back(h - 1)
 
     enc_copy = pltpu.make_async_copy(enc_ref, enc_hbm, enc_sem)
     enc_copy.start()
@@ -505,23 +542,9 @@
         far = stacked_out(grown, states[s], STATE, NT)
         dc_own = split(stacked_out(q, lanes_of(own_b[s]), STATE) + far)
         db_own = split(mm3(q, own_c[s], TN))
-        c2 = lanes_of(own_c[s])
-        back = mm(c2, grown[0], TN)
-        back = back[:STATE] + back[STATE:] + mm(own_c[s][0], grown[1], TN)
-        back = rows_of(split(back))
         both = mm(own_onehot[s], lanes_of([db_own[0], dc_own[0]])) + mm(own_onehot[s], lanes_of([db_own[1], dc_own[1]]))
         dc_all = dc_all + both[:, STATE:]
-        db_all = db_all + both[:, :STATE] + stacked_out((wh_s[s], wl_s[s]), back, STATE, NT)
-        reach = stacked(b_all, back)
-        for h in range(heads):
-            at = 3 * s * heads + heads + h
-            columns = slice(h * HEAD, (h + 1) * HEAD)
-            x = rows_of([xw_s[:, columns], edge_s[:, columns]])
-            terms = reach[:, columns] * x
-            acc_s[0, h : h + 1, :] += jnp.sum(terms * weights[:, at : at + 1], axis=0, keepdims=True)
-            acc_s[1, h : h + 1, :] += jnp.sum(
-                terms * weights[:, at + heads : at + heads + 1], axis=0, keepdims=True
-            )
+        db_all = db_all + both[:, :STATE] + stacked_out((wh_s[s], wl_s[s]), back_s[s], STATE, NT)
     d_summed = split(jnp.concatenate([db_all, dc_all], axis=1) * bc_slope)
     by_tap = mm(pick, d_summed[0], TN) + mm(pick, d_summed[1], TN)
     grad_ref[...] = jnp.zeros_like(grad_ref)
@@ -566,6 +589,7 @@
         ((2, count, count), f32),
         ((2, count, count), f32),
         ((2, heads, 128), f32),
+        ((2, 2 * STATE, width), bf16),
     ]
 
     def space(item):

time: 47 us -> 45.8 us (0.974)
  Pallas kernels: 18 us -> 16.8 us
    pallas_call x1, Pallas kernels: 12.5 us -> 11.2 us  [mixer(): pl.pallas_call(functools.partial(mixer_kernel, scale), in_specs=[vmem] *...]
where the time goes in v5:
time: 45.8 us; the launch traced here: 45.3 us
  Pallas kernels  16.8 us (37%)
  starting transfers between devices  12.6 us (28%)
  waiting for transfers between devices  11.4 us (25%)
  other arithmetic  2.37 us (5%)
  local copies, waits for them, and re-layouts  1.17 us (3%)
  between operations  0.84 us (2%)
    ppermute x8, starting transfers between devices, exchange(): return lax.ppermute(value, axis, [(i, i ^ distance) for i in range(size)])  12.6 us
    ppermute x8, waiting for transfers between devices, exchange(): return lax.ppermute(value, axis, [(i, i ^ distance) for i in range(size)])  11.4 us
    pallas_call x1, Pallas kernels, mixer(): pl.pallas_call(functools.partial(mixer_kernel, scale), in_specs=[vmem] *...  11.2 us
    pallas_call x2, Pallas kernels, tables(): pl.pallas_call(functools.partial(tables_kernel, len(weights)), in_specs=[...  5.55 us
  transfers between devices with their start and end apart: 8, of which 5 were waited for; matrix products, arithmetic and copies ran while one was open for 5% of the time, Pallas kernels for 12%

profile of v5, /device:TPU:0, one launch (start us, length us, event | category | flops | bytes accessed | tf_op | source)
XLA Modules:
  0.0 45.3 jit_solution(2338020670630627592)
XLA Ops:
  0.6 0.0 copy-start
  0.6 3.0 %collective-permute-start = (s32[1,256]{1,0:T(1,128)}, s32[1,256]{1,0:T(1,128)S(1)}, u32[]{:S(2)}, u32[]{:S(2)}) collective-permute-start(s32[1,256]{1,0:T(1,128)} %bitcast.21), channel_id=1, source_target_pairs={{0,4},{4,0},{8,12},{12,8},{16,20},{20,16},{24,28},{28,24},{1,5},{5... | collective-permute-start | bytes 3080 | tf_op jit(solution)/shard_map/ppermute | solution.py:622
  3.6 0.8 %fusion = f32[4]{0:T(128)S(1)} fusion(bf16[4,2048]{1,0:T(4,128)(2,1)} %param.17), kind=kLoop, calls=%fused_computation.3 | loop fusion | flops 24572 | bytes 16400 | tf_op jit(solution)/shard_map/reduce_sum | solution.py:646
  4.5 0.8 %fusion.2.normed_ref = bf16[4,2048]{1,0:T(4,128)(2,1)S(1)} fusion(bf16[4,2048]{1,0:T(4,128)(2,1)} %param.17, f32[2048]{0:T(1024)} %param.18, f32[4]{0:T(128)S(1)} %add_rsqrt_fusion), kind=kLoop, calls=%fused_computation.5 | loop fusion | flops 32768 | bytes 40976 | tf_op jit(solution)/shard_map/convert_element_type | solution.py:647
  5.3 0.7 %broadcast_minimum_fusion = s32[256]{0:T(256)S(1)} fusion(s32[256]{0:T(256)} %param.15), kind=kLoop, calls=%fused_computation.11 | loop fusion | flops 256 | bytes 2048 | tf_op jit(solution)/shard_map/min | solution.py:648
  6.0 0.0 collective-permute-done
  6.0 0.0 copy-start.1
  6.0 0.0 copy-start.2
  6.0 0.0 copy-start.3
  6.0 0.0 copy-start.4
  6.1 0.0 copy-start.5
  6.1 0.0 copy-start.6
  6.1 0.0 copy-start.7
  6.1 0.0 copy-start.8
  6.1 1.6 %collective-permute-start.1 = (s32[2,256]{1,0:T(2,128)S(1)}, s32[2,256]{1,0:T(2,128)S(1)}, u32[]{:S(2)}, u32[]{:S(2)}) collective-permute-start(s32[2,256]{1,0:T(2,128)S(1)} %pad_add_fusion.1), channel_id=1, source_target_pairs={{0,8},{4,12},{8,0},{12,4},{16,24},{20,28},{24,16},{28,20},{1,9},{5... | collective-permute-start | bytes 6152 | tf_op jit(solution)/shard_map/ppermute | solution.py:622
  7.7 3.1 %tables.2 = (f32[8,256]{1,0:T(8,128)S(1)}, f32[8,1024]{1,0:T(8,128)S(1)}) custom-call(bf16[4,2048]{1,0:T(4,128)(2,1)S(1)} %fusion.2.normed_ref, bf16[2048,256]{1,0:T(8,128)(2,1)} %refs_0_.2, bf16[2048,1024]{1,0:T(8,128)(2,1)} %refs_1_.1), custom_call_target="tpu_custom_call" | custom-call | tf_op jit(solution)/shard_map/tables/pallas_call | solution.py:107
  10.8 0.0 collective-permute-done.1
  10.9 2.7 %collective-permute-start.2 = (s32[4,256]{1,0:T(4,128)S(1)}, s32[4,256]{1,0:T(4,128)S(1)}, u32[]{:S(2)}, u32[]{:S(2)}) collective-permute-start(s32[4,256]{1,0:T(4,128)S(1)} %pad_add_fusion.near_ref), channel_id=1, source_target_pairs={{0,16},{4,20},{8,24},{12,28},{16,0},{20,4},{24,8},{28,12},{1,17},{... | collective-permute-start | bytes 12296 | tf_op jit(solution)/shard_map/ppermute | solution.py:622
  13.5 0.0 copy-done
  13.5 0.1 convolution_bitcast_fusion.dt_ref
  13.6 2.5 %tables.3.tz_ref = f32[8,1024]{1,0:T(8,128)S(1)} custom-call(bf16[4,2048]{1,0:T(4,128)(2,1)S(1)} %fusion.2.normed_ref, bf16[2048,1024]{1,0:T(8,128)(2,1)} %refs_0_.3), custom_call_target="tpu_custom_call" | custom-call | tf_op jit(solution)/shard_map/tables/pallas_call | solution.py:107
  16.1 0.0 collective-permute-done.2.far_ref
  16.1 0.0 copy-done.1
  16.1 0.0 copy-done.2
  16.2 0.0 copy-done.3
  16.2 0.0 copy-done.4
  16.2 0.0 copy-done.5
  16.2 0.0 copy-done.6
  16.2 0.0 copy-done.7
  16.2 0.0 copy-done.8
  16.2 11.2 %mixer.1 = (bf16[256,1024]{1,0:T(8,128)(2,1)}, f32[8,256]{1,0:T(8,128)S(1)}) custom-call(s32[4,256]{1,0:T(4,128)S(1)} %pad_add_fusion.near_ref, s32[4,256]{1,0:T(4,128)S(1)} %collective-permute-done.2.far_ref, s32[1,4]{1,0:T(1,128)S(1)} %bitcast.16, f32[1,8]{1,0:T(1,128)S(1)} %bitcast.17, f32[8,1024]{1,0:T(8,128)S(1)} %get-tuple-element.19.tv_ref, ...), custom_call_target="tpu_custom_call" | custom-call | tf_op jit(solution)/shard_map/mixer/pallas_call | solution.py:600
  27.4 0.1 collective-permute-start.3
  27.5 1.2 %collective-permute-done.3 = f32[8,256]{1,0:T(8,128)S(1)} collective-permute-done((f32[8,256]{1,0:T(8,128)S(1)}, f32[8,256]{1,0:T(8,128)S(1)}, u32[]{:S(2)}, u32[]{:S(2)}) %collective-permute-start.3) | collective-permute-done | bytes 8224 | tf_op jit(solution)/shard_map/ppermute | solution.py:622
  28.7 1.5 %collective-permute-start.4 = (f32[8,256]{1,0:T(8,128)S(1)}, f32[8,256]{1,0:T(8,128)S(1)}, u32[]{:S(2)}, u32[]{:S(2)}) collective-permute-start(f32[8,256]{1,0:T(8,128)S(1)} %add.24), channel_id=1, source_target_pairs={{0,2},{1,3},{2,0},{3,1},{4,6},{5,7},{6,4},{7,5},{8,10},{9,11},{10,... | collective-permute-start | bytes 24584 | tf_op jit(solution)/shard_map/ppermute | solution.py:622
  30.2 2.1 %collective-permute-done.4 = f32[8,256]{1,0:T(8,128)S(1)} collective-permute-done((f32[8,256]{1,0:T(8,128)S(1)}, f32[8,256]{1,0:T(8,128)S(1)}, u32[]{:S(2)}, u32[]{:S(2)}) %collective-permute-start.4) | collective-permute-done | bytes 8224 | tf_op jit(solution)/shard_map/ppermute | solution.py:622
  32.3 1.4 %collective-permute-start.5 = (f32[8,256]{1,0:T(8,128)S(1)}, f32[8,256]{1,0:T(8,128)S(1)}, u32[]{:S(2)}, u32[]{:S(2)}) collective-permute-start(f32[8,256]{1,0:T(8,128)S(1)} %add.25), channel_id=1, source_target_pairs={{0,4},{4,0},{8,12},{12,8},{16,20},{20,16},{24,28},{28,24},{1,5},{5... | collective-permute-start | bytes 24584 | tf_op jit(solution)/shard_map/ppermute | solution.py:622
  33.8 2.2 %collective-permute-done.5 = f32[8,256]{1,0:T(8,128)S(1)} collective-permute-done((f32[8,256]{1,0:T(8,128)S(1)}, f32[8,256]{1,0:T(8,128)S(1)}, u32[]{:S(2)}, u32[]{:S(2)}) %collective-permute-start.5) | collective-permute-done | bytes 8224 | tf_op jit(solution)/shard_map/ppermute | solution.py:622
  36.0 0.5 %collective-permute-start.6 = (f32[8,256]{1,0:T(8,128)S(1)}, f32[8,256]{1,0:T(8,128)S(1)}, u32[]{:S(2)}, u32[]{:S(2)}) collective-permute-start(f32[8,256]{1,0:T(8,128)S(1)} %add.26), channel_id=1, source_target_pairs={{0,8},{4,12},{8,0},{12,4},{16,24},{20,28},{24,16},{28,20},{1,9},{5... | collective-permute-start | bytes 24584 | tf_op jit(solution)/shard_map/ppermute | solution.py:622
  36.4 3.2 %collective-permute-done.6 = f32[8,256]{1,0:T(8,128)S(1)} collective-permute-done((f32[8,256]{1,0:T(8,128)S(1)}, f32[8,256]{1,0:T(8,128)S(1)}, u32[]{:S(2)}, u32[]{:S(2)}) %collective-permute-start.6) | collective-permute-done | bytes 8224 | tf_op jit(solution)/shard_map/ppermute | solution.py:622
  39.6 1.9 %collective-permute-start.7 = (f32[8,256]{1,0:T(8,128)S(1)}, f32[8,256]{1,0:T(8,128)S(1)}, u32[]{:S(2)}, u32[]{:S(2)}) collective-permute-start(f32[8,256]{1,0:T(8,128)S(1)} %add.27), channel_id=1, source_target_pairs={{0,16},{4,20},{8,24},{12,28},{16,0},{20,4},{24,8},{28,12},{1,17},{... | collective-permute-start | bytes 24584 | tf_op jit(solution)/shard_map/ppermute | solution.py:622
  41.5 2.7 %collective-permute-done.7 = f32[8,256]{1,0:T(8,128)S(1)} collective-permute-done((f32[8,256]{1,0:T(8,128)S(1)}, f32[8,256]{1,0:T(8,128)S(1)}, u32[]{:S(2)}, u32[]{:S(2)}) %collective-permute-start.7) | collective-permute-done | bytes 8224 | tf_op jit(solution)/shard_map/ppermute | solution.py:622
  44.2 0.5 %slice_bitcast_fusion = (f32[32]{0:T(128)}, f32[32]{0:T(128)}) fusion(f32[8,256]{1,0:T(8,128)S(1)} %add.28), kind=kLoop, calls=%fused_computation.8 | loop fusion | bytes 512 | tf_op jit(solution)/shard_map/squeeze | solution.py:684
  44.7 0.6 %slice.14 = f32[4,256]{1,0:T(4,128)} slice(f32[8,256]{1,0:T(8,128)S(1)} %add.28), slice={[0:4], [0:256]} | slice | bytes 8192 | tf_op jit(solution)/shard_map/slice | solution.py:684
  (8 shorter events, 0.0 us)
Async XLA Ops:
  0.6 12.9 %copy-start = (bf16[2048,8]{0,1:T(8,128)(2,1)S(1)}, bf16[2048,8]{0,1:T(8,128)(2,1)}, u32[]{:S(2)}) copy-start(bf16[2048,8]{0,1:T(8,128)(2,1)} %param.22) | copy-start | bytes 98308
  0.6 5.4 %collective-permute-start = (s32[1,256]{1,0:T(1,128)}, s32[1,256]{1,0:T(1,128)S(1)}, u32[]{:S(2)}, u32[]{:S(2)}) collective-permute-start(s32[1,256]{1,0:T(1,128)} %bitcast.21), channel_id=1, source_target_pairs={{0,4},{4,0},{8,12},{12,8},{16,20},{20,16},{24,28},{28,24},{1,5},{5... | collective-permute-start | bytes 3080 | tf_op jit(solution)/shard_map/ppermute | solution.py:622
  6.0 10.1 %copy-start.1 = (bf16[256,1024]{1,0:T(8,128)(2,1)S(1)}, bf16[256,1024]{1,0:T(8,128)(2,1)}, u32[]{:S(2)}) copy-start(bf16[256,1024]{1,0:T(8,128)(2,1)} %cot_ref.1) | copy-start | bytes 1572868
  6.0 10.1 %copy-start.2 = (f32[4,1024]{1,0:T(4,128)S(1)}, f32[4,1024]{1,0:T(4,128)}, u32[]{:S(2)}) copy-start(f32[4,1024]{1,0:T(4,128)} %cv_ref.1) | copy-start | bytes 49156
  6.0 10.1 %copy-start.3 = (f32[4,256]{1,0:T(4,128)S(1)}, f32[4,256]{1,0:T(4,128)}, u32[]{:S(2)}) copy-start(f32[4,256]{1,0:T(4,128)} %cs_ref.1) | copy-start | bytes 12292
  6.0 10.1 %copy-start.4 = (f32[1024]{0:T(1024)S(1)}, f32[1024]{0:T(1024)}, u32[]{:S(2)}) copy-start(f32[1024]{0:T(1024)} %param.28) | copy-start | bytes 12292
  6.1 10.1 %copy-start.5 = (s32[4]{0:T(128)S(1)}, s32[4]{0:T(128)}, u32[]{:S(2)}) copy-start(s32[4]{0:T(128)} %param.16) | copy-start | bytes 52
  6.1 10.1 %copy-start.6 = (f32[8]{0:T(128)S(1)}, f32[8]{0:T(128)}, u32[]{:S(2)}) copy-start(f32[8]{0:T(128)} %param.27) | copy-start | bytes 100
  6.1 10.1 %copy-start.7 = (f32[8]{0:T(128)S(1)}, f32[8]{0:T(128)}, u32[]{:S(2)}) copy-start(f32[8]{0:T(128)} %param.25) | copy-start | bytes 100
  6.1 10.1 %copy-start.8 = (f32[8]{0:T(128)S(1)}, f32[8]{0:T(128)}, u32[]{:S(2)}) copy-start(f32[8]{0:T(128)} %param.26) | copy-start | bytes 100
  6.1 4.7 %collective-permute-start.1 = (s32[2,256]{1,0:T(2,128)S(1)}, s32[2,256]{1,0:T(2,128)S(1)}, u32[]{:S(2)}, u32[]{:S(2)}) collective-permute-start(s32[2,256]{1,0:T(2,128)S(1)} %pad_add_fusion.1), channel_id=1, source_target_pairs={{0,8},{4,12},{8,0},{12,4},{16,24},{20,28},{24,16},{28,20},{1,9},{5... | collective-permute-start | bytes 6152 | tf_op jit(solution)/shard_map/ppermute | solution.py:622
  10.9 5.3 %collective-permute-start.2 = (s32[4,256]{1,0:T(4,128)S(1)}, s32[4,256]{1,0:T(4,128)S(1)}, u32[]{:S(2)}, u32[]{:S(2)}) collective-permute-start(s32[4,256]{1,0:T(4,128)S(1)} %pad_add_fusion.near_ref), channel_id=1, source_target_pairs={{0,16},{4,20},{8,24},{12,28},{16,0},{20,4},{24,8},{28,12},{1,17},{... | collective-permute-start | bytes 12296 | tf_op jit(solution)/shard_map/ppermute | solution.py:622
  27.4 1.2 %collective-permute-start.3 = (f32[8,256]{1,0:T(8,128)S(1)}, f32[8,256]{1,0:T(8,128)S(1)}, u32[]{:S(2)}, u32[]{:S(2)}) collective-permute-start(f32[8,256]{1,0:T(8,128)S(1)} %get-tuple-element.23), channel_id=1, source_target_pairs={{0,1},{1,0},{2,3},{3,2},{4,5},{5,4},{6,7},{7,6},{8,9},{9,8},{10,11... | collective-permute-start | bytes 24584 | tf_op jit(solution)/shard_map/ppermute | solution.py:622
  28.7 3.7 %collective-permute-start.4 = (f32[8,256]{1,0:T(8,128)S(1)}, f32[8,256]{1,0:T(8,128)S(1)}, u32[]{:S(2)}, u32[]{:S(2)}) collective-permute-start(f32[8,256]{1,0:T(8,128)S(1)} %add.24), channel_id=1, source_target_pairs={{0,2},{1,3},{2,0},{3,1},{4,6},{5,7},{6,4},{7,5},{8,10},{9,11},{10,... | collective-permute-start | bytes 24584 | tf_op jit(solution)/shard_map/ppermute | solution.py:622
  32.3 3.7 %collective-permute-start.5 = (f32[8,256]{1,0:T(8,128)S(1)}, f32[8,256]{1,0:T(8,128)S(1)}, u32[]{:S(2)}, u32[]{:S(2)}) collective-permute-start(f32[8,256]{1,0:T(8,128)S(1)} %add.25), channel_id=1, source_target_pairs={{0,4},{4,0},{8,12},{12,8},{16,20},{20,16},{24,28},{28,24},{1,5},{5... | collective-permute-start | bytes 24584 | tf_op jit(solution)/shard_map/ppermute | solution.py:622
  36.0 3.7 %collective-permute-start.6 = (f32[8,256]{1,0:T(8,128)S(1)}, f32[8,256]{1,0:T(8,128)S(1)}, u32[]{:S(2)}, u32[]{:S(2)}) collective-permute-start(f32[8,256]{1,0:T(8,128)S(1)} %add.26), channel_id=1, source_target_pairs={{0,8},{4,12},{8,0},{12,4},{16,24},{20,28},{24,16},{28,20},{1,9},{5... | collective-permute-start | bytes 24584 | tf_op jit(solution)/shard_map/ppermute | solution.py:622
  39.6 4.5 %collective-permute-start.7 = (f32[8,256]{1,0:T(8,128)S(1)}, f32[8,256]{1,0:T(8,128)S(1)}, u32[]{:S(2)}, u32[]{:S(2)}) collective-permute-start(f32[8,256]{1,0:T(8,128)S(1)} %add.27), channel_id=1, source_target_pairs={{0,16},{4,20},{8,24},{12,28},{16,0},{20,4},{24,8},{28,12},{1,17},{... | collective-permute-start | bytes 24584 | tf_op jit(solution)/shard_map/ppermute | solution.py:622

commit v6 on v5

--- a/solution.py
+++ b/solution.py
@@ -235,6 +235,30 @@
             jnp.where(row < here, totals[t] - inclusive, inclusive - masks[t]) + between
         )
 
+    own_tok = tok_s[pl.ds(here, 1), :]
+    own_masks = [(own_tok == t).astype(f32) for t in range(IDS)]
+    own_counts = [[], []]
+    for t in range(IDS):
+        inclusive = count_s[t, pl.ds(here, 1), :]
+        total = jnp.sum(own_masks[t], axis=1, keepdims=True)
+        own_counts[0].append(inclusive)
+        own_counts[1].append(total - inclusive + own_masks[t])
+    turned = []
+    for s in range(2):
+        logs = sum(log_of[s][t] * own_counts[s][t] for t in range(IDS))
+        alogs = sum(alog_of[s][t] * own_counts[s][t] for t in range(IDS))
+        row_s[s, 0] = logs
+        row_s[s, 1] = sum(step_of[s][t] * own_masks[t] for t in range(IDS))
+        row_s[s, 2] = sum(ratio_of[s][t] * own_masks[t] for t in range(IDS)) - alogs
+        turned += [logs, alogs]
+    own_ids = [ids_s[s, pl.ds(here, 1), :] for s in range(2)]
+    extra = jnp.concatenate(
+        [own_ids[0].astype(f32), own_ids[1].astype(f32), own_tok.astype(f32), jnp.zeros((5, count), f32)],
+        axis=0,
+    )
+    turned = jnp.concatenate(turned + [extra, jnp.zeros((120 - 4 * heads, count), f32)], axis=0).T
+    base = 4 * heads
+    tcol_s[...] = jnp.broadcast_to(turned[:, base + 2 : base + 3], (count, 128))
     window_rows = iota((ROWS, count), 0)
     def earlier(j):
         forward = j < here
@@ -322,35 +346,6 @@
     bc = split(bc_all)
     b_all = (bc[0][:, :STATE], bc[1][:, :STATE])
 
-    own_tok = tok_s[pl.ds(here, 1), :]
-    own_masks = [(own_tok == t).astype(f32) for t in range(IDS)]
-    own_counts = [[], []]
-    for t in range(IDS):
-        inclusive = count_s[t, pl.ds(here, 1), :]
-        total = jnp.sum(own_masks[t], axis=1, keepdims=True)
-        own_counts[0].append(inclusive)
-        own_counts[1].append(total - inclusive + own_masks[t])
-    turned = []
-    for s in range(2):
-        logs = sum(log_of[s][t] * own_counts[s][t] for t in range(IDS))
-        alogs = sum(alog_of[s][t] * own_counts[s][t] for t in range(IDS))
-        row_s[s, 0] = logs
-        row_s[s, 1] = sum(step_of[s][t] * own_masks[t] for t in range(IDS))
-        row_s[s, 2] = sum(ratio_of[s][t] * own_masks[t] for t in range(IDS)) - alogs
-        turned += [logs, alogs]
-    own_ids = [ids_s[s, pl.ds(here, 1), :] for s in range(2)]
-    extra = jnp.concatenate(
-        [own_ids[0].astype(f32), own_ids[1].astype(f32), own_tok.astype(f32), jnp.zeros((5, count), f32)],
-        axis=0,
-    )
-    turned = jnp.concatenate(turned + [extra, jnp.zeros((120 - 4 * heads, count), f32)], axis=0).T
-    for s in range(2):
-        for h in range(heads):
-            at = 2 * s * heads + h
-            lcol_s[s, h] = jnp.broadcast_to(turned[:, at : at + 1], (count, 128))
-            acol_s[s, h] = jnp.broadcast_to(turned[:, at + heads : at + heads + 1], (count, 128))
-    base = 4 * heads
-    tcol_s[...] = jnp.broadcast_to(turned[:, base + 2 : base + 3], (count, 128))
     own_onehot = []
     lane_k = iota((count, ROWS), 1).astype(f32)
     picks = []
@@ -420,6 +415,10 @@
 
     def mix(h):
         columns2 = slice(h * 2 * HEAD, (h + 1) * 2 * HEAD)
+        for s in range(2):
+            at = 2 * s * heads + h
+            lcol_s[s, h] = jnp.broadcast_to(turned[:, at : at + 1], (count, 128))
+            acol_s[s, h] = jnp.broadcast_to(turned[:, at + heads : at + heads + 1], (count, 128))
         factors, ys = [], []
         for s in range(2):
             log_row = row_s[s, 0, h : h + 1, :]
@@ -654,13 +653,13 @@
         if distance == 2:
             near, normed = lax.optimization_barrier((near, normed))
         if distance * 2 >= devices:
-            tbc, tv = tables(normed, [w_states, w_values], [1, 4])
+            tbc, tv = tables(normed, [w_states, w_values], [2, 8])
             near, tbc, tv, normed = lax.optimization_barrier((near, tbc, tv, normed))
         far = exchange(near, "ctx", distance)
         distance *= 2
     if tv is None:
-        tbc, tv = tables(normed, [w_states, w_values], [1, 4])
-    (tz,) = tables(normed, [w_gates], [4])
+        tbc, tv = tables(normed, [w_states, w_values], [2, 8])
+    (tz,) = tables(normed, [w_gates], [8])
     dt = lax.dot_general(w_steps, normed, (((0,), (1,)), ((), ())), preferred_element_type=f32)
     small = [
         tv,

time: 45.8 us -> 45.7 us (level)
  no operation moved by 1% of the time
where the time goes in v6:
time: 45.7 us; the launch traced here: 45.2 us
  Pallas kernels  16.7 us (37%)
  starting transfers between devices  12.7 us (28%)
  waiting for transfers between devices  11.3 us (25%)
  other arithmetic  2.37 us (5%)
  local copies, waits for them, and re-layouts  1.17 us (3%)
  between operations  0.84 us (2%)
    ppermute x8, starting transfers between devices, exchange(): return lax.ppermute(value, axis, [(i, i ^ distance) for i in range(size)])  12.7 us
    ppermute x8, waiting for transfers between devices, exchange(): return lax.ppermute(value, axis, [(i, i ^ distance) for i in range(size)])  11.3 us
    pallas_call x1, Pallas kernels, mixer(): pl.pallas_call(functools.partial(mixer_kernel, scale), in_specs=[vmem] *...  11.2 us
    pallas_call x2, Pallas kernels, tables(): pl.pallas_call(functools.partial(tables_kernel, len(weights)), in_specs=[...  5.44 us
  transfers between devices with their start and end apart: 8, of which 5 were waited for; matrix products, arithmetic and copies ran while one was open for 5% of the time, Pallas kernels for 12%

profile of v6, /device:TPU:0, one launch (start us, length us, event | category | flops | bytes accessed | tf_op | source)
XLA Modules:
  0.0 45.2 jit_solution(9823975069863557547)
XLA Ops:
  0.6 0.0 copy-start
  0.6 3.0 %collective-permute-start = (s32[1,256]{1,0:T(1,128)}, s32[1,256]{1,0:T(1,128)S(1)}, u32[]{:S(2)}, u32[]{:S(2)}) collective-permute-start(s32[1,256]{1,0:T(1,128)} %bitcast.21), channel_id=1, source_target_pairs={{0,4},{4,0},{8,12},{12,8},{16,20},{20,16},{24,28},{28,24},{1,5},{5... | collective-permute-start | bytes 3080 | tf_op jit(solution)/shard_map/ppermute | solution.py:621
  3.6 0.8 %fusion = f32[4]{0:T(128)S(1)} fusion(bf16[4,2048]{1,0:T(4,128)(2,1)} %param.17), kind=kLoop, calls=%fused_computation.3 | loop fusion | flops 24572 | bytes 16400 | tf_op jit(solution)/shard_map/reduce_sum | solution.py:645
  4.5 0.8 %fusion.2.normed_ref = bf16[4,2048]{1,0:T(4,128)(2,1)S(1)} fusion(bf16[4,2048]{1,0:T(4,128)(2,1)} %param.17, f32[2048]{0:T(1024)} %param.18, f32[4]{0:T(128)S(1)} %add_rsqrt_fusion), kind=kLoop, calls=%fused_computation.5 | loop fusion | flops 32768 | bytes 40976 | tf_op jit(solution)/shard_map/convert_element_type | solution.py:646
  5.3 0.7 %broadcast_minimum_fusion = s32[256]{0:T(256)S(1)} fusion(s32[256]{0:T(256)} %param.15), kind=kLoop, calls=%fused_computation.11 | loop fusion | flops 256 | bytes 2048 | tf_op jit(solution)/shard_map/min | solution.py:647
  6.0 0.0 collective-permute-done
  6.0 0.0 copy-start.1
  6.0 0.0 copy-start.2
  6.0 0.0 copy-start.3
  6.0 0.0 copy-start.4
  6.1 0.0 copy-start.5
  6.1 0.0 copy-start.6
  6.1 0.0 copy-start.7
  6.1 0.0 copy-start.8
  6.1 1.6 %collective-permute-start.1 = (s32[2,256]{1,0:T(2,128)S(1)}, s32[2,256]{1,0:T(2,128)S(1)}, u32[]{:S(2)}, u32[]{:S(2)}) collective-permute-start(s32[2,256]{1,0:T(2,128)S(1)} %pad_add_fusion.1), channel_id=1, source_target_pairs={{0,8},{4,12},{8,0},{12,4},{16,24},{20,28},{24,16},{28,20},{1,9},{5... | collective-permute-start | bytes 6152 | tf_op jit(solution)/shard_map/ppermute | solution.py:621
  7.7 3.0 %tables.2 = (f32[8,256]{1,0:T(8,128)S(1)}, f32[8,1024]{1,0:T(8,128)S(1)}) custom-call(bf16[4,2048]{1,0:T(4,128)(2,1)S(1)} %fusion.2.normed_ref, bf16[2048,256]{1,0:T(8,128)(2,1)} %refs_0_.2, bf16[2048,1024]{1,0:T(8,128)(2,1)} %refs_1_.1), custom_call_target="tpu_custom_call" | custom-call | tf_op jit(solution)/shard_map/tables/pallas_call | solution.py:107
  10.8 0.0 collective-permute-done.1
  10.8 2.7 %collective-permute-start.2 = (s32[4,256]{1,0:T(4,128)S(1)}, s32[4,256]{1,0:T(4,128)S(1)}, u32[]{:S(2)}, u32[]{:S(2)}) collective-permute-start(s32[4,256]{1,0:T(4,128)S(1)} %pad_add_fusion.near_ref), channel_id=1, source_target_pairs={{0,16},{4,20},{8,24},{12,28},{16,0},{20,4},{24,8},{28,12},{1,17},{... | collective-permute-start | bytes 12296 | tf_op jit(solution)/shard_map/ppermute | solution.py:621
  13.5 0.0 copy-done
  13.5 0.1 convolution_bitcast_fusion.dt_ref
  13.6 2.4 %tables.3.tz_ref = f32[8,1024]{1,0:T(8,128)S(1)} custom-call(bf16[4,2048]{1,0:T(4,128)(2,1)S(1)} %fusion.2.normed_ref, bf16[2048,1024]{1,0:T(8,128)(2,1)} %refs_0_.3), custom_call_target="tpu_custom_call" | custom-call | tf_op jit(solution)/shard_map/tables/pallas_call | solution.py:107
  16.0 0.0 collective-permute-done.2.far_ref
  16.0 0.0 copy-done.1
  16.0 0.0 copy-done.2
  16.0 0.0 copy-done.3
  16.1 0.0 copy-done.4
  16.1 0.0 copy-done.5
  16.1 0.0 copy-done.6
  16.1 0.0 copy-done.7
  16.1 0.0 copy-done.8
  16.1 11.2 %mixer.1 = (bf16[256,1024]{1,0:T(8,128)(2,1)}, f32[8,256]{1,0:T(8,128)S(1)}) custom-call(s32[4,256]{1,0:T(4,128)S(1)} %pad_add_fusion.near_ref, s32[4,256]{1,0:T(4,128)S(1)} %collective-permute-done.2.far_ref, s32[1,4]{1,0:T(1,128)S(1)} %bitcast.16, f32[1,8]{1,0:T(1,128)S(1)} %bitcast.17, f32[8,1024]{1,0:T(8,128)S(1)} %get-tuple-element.19.tv_ref, ...), custom_call_target="tpu_custom_call" | custom-call | tf_op jit(solution)/shard_map/mixer/pallas_call | solution.py:599
  27.4 0.1 collective-permute-start.3
  27.4 1.2 %collective-permute-done.3 = f32[8,256]{1,0:T(8,128)S(1)} collective-permute-done((f32[8,256]{1,0:T(8,128)S(1)}, f32[8,256]{1,0:T(8,128)S(1)}, u32[]{:S(2)}, u32[]{:S(2)}) %collective-permute-start.3) | collective-permute-done | bytes 8224 | tf_op jit(solution)/shard_map/ppermute | solution.py:621
  28.6 1.5 %collective-permute-start.4 = (f32[8,256]{1,0:T(8,128)S(1)}, f32[8,256]{1,0:T(8,128)S(1)}, u32[]{:S(2)}, u32[]{:S(2)}) collective-permute-start(f32[8,256]{1,0:T(8,128)S(1)} %add.24), channel_id=1, source_target_pairs={{0,2},{1,3},{2,0},{3,1},{4,6},{5,7},{6,4},{7,5},{8,10},{9,11},{10,... | collective-permute-start | bytes 24584 | tf_op jit(solution)/shard_map/ppermute | solution.py:621
  30.1 2.1 %collective-permute-done.4 = f32[8,256]{1,0:T(8,128)S(1)} collective-permute-done((f32[8,256]{1,0:T(8,128)S(1)}, f32[8,256]{1,0:T(8,128)S(1)}, u32[]{:S(2)}, u32[]{:S(2)}) %collective-permute-start.4) | collective-permute-done | bytes 8224 | tf_op jit(solution)/shard_map/ppermute | solution.py:621
  32.2 1.4 %collective-permute-start.5 = (f32[8,256]{1,0:T(8,128)S(1)}, f32[8,256]{1,0:T(8,128)S(1)}, u32[]{:S(2)}, u32[]{:S(2)}) collective-permute-start(f32[8,256]{1,0:T(8,128)S(1)} %add.25), channel_id=1, source_target_pairs={{0,4},{4,0},{8,12},{12,8},{16,20},{20,16},{24,28},{28,24},{1,5},{5... | collective-permute-start | bytes 24584 | tf_op jit(solution)/shard_map/ppermute | solution.py:621
  33.7 2.2 %collective-permute-done.5 = f32[8,256]{1,0:T(8,128)S(1)} collective-permute-done((f32[8,256]{1,0:T(8,128)S(1)}, f32[8,256]{1,0:T(8,128)S(1)}, u32[]{:S(2)}, u32[]{:S(2)}) %collective-permute-start.5) | collective-permute-done | bytes 8224 | tf_op jit(solution)/shard_map/ppermute | solution.py:621
  35.9 0.5 %collective-permute-start.6 = (f32[8,256]{1,0:T(8,128)S(1)}, f32[8,256]{1,0:T(8,128)S(1)}, u32[]{:S(2)}, u32[]{:S(2)}) collective-permute-start(f32[8,256]{1,0:T(8,128)S(1)} %add.26), channel_id=1, source_target_pairs={{0,8},{4,12},{8,0},{12,4},{16,24},{20,28},{24,16},{28,20},{1,9},{5... | collective-permute-start | bytes 24584 | tf_op jit(solution)/shard_map/ppermute | solution.py:621
  36.4 3.2 %collective-permute-done.6 = f32[8,256]{1,0:T(8,128)S(1)} collective-permute-done((f32[8,256]{1,0:T(8,128)S(1)}, f32[8,256]{1,0:T(8,128)S(1)}, u32[]{:S(2)}, u32[]{:S(2)}) %collective-permute-start.6) | collective-permute-done | bytes 8224 | tf_op jit(solution)/shard_map/ppermute | solution.py:621
  39.6 1.9 %collective-permute-start.7 = (f32[8,256]{1,0:T(8,128)S(1)}, f32[8,256]{1,0:T(8,128)S(1)}, u32[]{:S(2)}, u32[]{:S(2)}) collective-permute-start(f32[8,256]{1,0:T(8,128)S(1)} %add.27), channel_id=1, source_target_pairs={{0,16},{4,20},{8,24},{12,28},{16,0},{20,4},{24,8},{28,12},{1,17},{... | collective-permute-start | bytes 24584 | tf_op jit(solution)/shard_map/ppermute | solution.py:621
  41.5 2.6 %collective-permute-done.7 = f32[8,256]{1,0:T(8,128)S(1)} collective-permute-done((f32[8,256]{1,0:T(8,128)S(1)}, f32[8,256]{1,0:T(8,128)S(1)}, u32[]{:S(2)}, u32[]{:S(2)}) %collective-permute-start.7) | collective-permute-done | bytes 8224 | tf_op jit(solution)/shard_map/ppermute | solution.py:621
  44.1 0.5 %slice_bitcast_fusion = (f32[32]{0:T(128)}, f32[32]{0:T(128)}) fusion(f32[8,256]{1,0:T(8,128)S(1)} %add.28), kind=kLoop, calls=%fused_computation.8 | loop fusion | bytes 512 | tf_op jit(solution)/shard_map/squeeze | solution.py:683
  44.6 0.6 %slice.14 = f32[4,256]{1,0:T(4,128)} slice(f32[8,256]{1,0:T(8,128)S(1)} %add.28), slice={[0:4], [0:256]} | slice | bytes 8192 | tf_op jit(solution)/shard_map/slice | solution.py:683
  (8 shorter events, 0.0 us)
Async XLA Ops:
  0.6 12.8 %copy-start = (bf16[2048,8]{0,1:T(8,128)(2,1)S(1)}, bf16[2048,8]{0,1:T(8,128)(2,1)}, u32[]{:S(2)}) copy-start(bf16[2048,8]{0,1:T(8,128)(2,1)} %param.22) | copy-start | bytes 98308
  0.6 5.4 %collective-permute-start = (s32[1,256]{1,0:T(1,128)}, s32[1,256]{1,0:T(1,128)S(1)}, u32[]{:S(2)}, u32[]{:S(2)}) collective-permute-start(s32[1,256]{1,0:T(1,128)} %bitcast.21), channel_id=1, source_target_pairs={{0,4},{4,0},{8,12},{12,8},{16,20},{20,16},{24,28},{28,24},{1,5},{5... | collective-permute-start | bytes 3080 | tf_op jit(solution)/shard_map/ppermute | solution.py:621
  6.0 10.0 %copy-start.1 = (bf16[256,1024]{1,0:T(8,128)(2,1)S(1)}, bf16[256,1024]{1,0:T(8,128)(2,1)}, u32[]{:S(2)}) copy-start(bf16[256,1024]{1,0:T(8,128)(2,1)} %cot_ref.1) | copy-start | bytes 1572868
  6.0 10.0 %copy-start.2 = (f32[4,1024]{1,0:T(4,128)S(1)}, f32[4,1024]{1,0:T(4,128)}, u32[]{:S(2)}) copy-start(f32[4,1024]{1,0:T(4,128)} %cv_ref.1) | copy-start | bytes 49156
  6.0 10.0 %copy-start.3 = (f32[4,256]{1,0:T(4,128)S(1)}, f32[4,256]{1,0:T(4,128)}, u32[]{:S(2)}) copy-start(f32[4,256]{1,0:T(4,128)} %cs_ref.1) | copy-start | bytes 12292
  6.0 10.0 %copy-start.4 = (f32[1024]{0:T(1024)S(1)}, f32[1024]{0:T(1024)}, u32[]{:S(2)}) copy-start(f32[1024]{0:T(1024)} %param.28) | copy-start | bytes 12292
  6.1 10.0 %copy-start.5 = (s32[4]{0:T(128)S(1)}, s32[4]{0:T(128)}, u32[]{:S(2)}) copy-start(s32[4]{0:T(128)} %param.16) | copy-start | bytes 52
  6.1 10.0 %copy-start.6 = (f32[8]{0:T(128)S(1)}, f32[8]{0:T(128)}, u32[]{:S(2)}) copy-start(f32[8]{0:T(128)} %param.27) | copy-start | bytes 100
  6.1 10.0 %copy-start.7 = (f32[8]{0:T(128)S(1)}, f32[8]{0:T(128)}, u32[]{:S(2)}) copy-start(f32[8]{0:T(128)} %param.25) | copy-start | bytes 100
  6.1 10.0 %copy-start.8 = (f32[8]{0:T(128)S(1)}, f32[8]{0:T(128)}, u32[]{:S(2)}) copy-start(f32[8]{0:T(128)} %param.26) | copy-start | bytes 100
  6.1 4.7 %collective-permute-start.1 = (s32[2,256]{1,0:T(2,128)S(1)}, s32[2,256]{1,0:T(2,128)S(1)}, u32[]{:S(2)}, u32[]{:S(2)}) collective-permute-start(s32[2,256]{1,0:T(2,128)S(1)} %pad_add_fusion.1), channel_id=1, source_target_pairs={{0,8},{4,12},{8,0},{12,4},{16,24},{20,28},{24,16},{28,20},{1,9},{5... | collective-permute-start | bytes 6152 | tf_op jit(solution)/shard_map/ppermute | solution.py:621
  10.8 5.2 %collective-permute-start.2 = (s32[4,256]{1,0:T(4,128)S(1)}, s32[4,256]{1,0:T(4,128)S(1)}, u32[]{:S(2)}, u32[]{:S(2)}) collective-permute-start(s32[4,256]{1,0:T(4,128)S(1)} %pad_add_fusion.near_ref), channel_id=1, source_target_pairs={{0,16},{4,20},{8,24},{12,28},{16,0},{20,4},{24,8},{28,12},{1,17},{... | collective-permute-start | bytes 12296 | tf_op jit(solution)/shard_map/ppermute | solution.py:621
  27.4 1.2 %collective-permute-start.3 = (f32[8,256]{1,0:T(8,128)S(1)}, f32[8,256]{1,0:T(8,128)S(1)}, u32[]{:S(2)}, u32[]{:S(2)}) collective-permute-start(f32[8,256]{1,0:T(8,128)S(1)} %get-tuple-element.23), channel_id=1, source_target_pairs={{0,1},{1,0},{2,3},{3,2},{4,5},{5,4},{6,7},{7,6},{8,9},{9,8},{10,11... | collective-permute-start | bytes 24584 | tf_op jit(solution)/shard_map/ppermute | solution.py:621
  28.6 3.7 %collective-permute-start.4 = (f32[8,256]{1,0:T(8,128)S(1)}, f32[8,256]{1,0:T(8,128)S(1)}, u32[]{:S(2)}, u32[]{:S(2)}) collective-permute-start(f32[8,256]{1,0:T(8,128)S(1)} %add.24), channel_id=1, source_target_pairs={{0,2},{1,3},{2,0},{3,1},{4,6},{5,7},{6,4},{7,5},{8,10},{9,11},{10,... | collective-permute-start | bytes 24584 | tf_op jit(solution)/shard_map/ppermute | solution.py:621
  32.2 3.7 %collective-permute-start.5 = (f32[8,256]{1,0:T(8,128)S(1)}, f32[8,256]{1,0:T(8,128)S(1)}, u32[]{:S(2)}, u32[]{:S(2)}) collective-permute-start(f32[8,256]{1,0:T(8,128)S(1)} %add.25), channel_id=1, source_target_pairs={{0,4},{4,0},{8,12},{12,8},{16,20},{20,16},{24,28},{28,24},{1,5},{5... | collective-permute-start | bytes 24584 | tf_op jit(solution)/shard_map/ppermute | solution.py:621
  35.9 3.7 %collective-permute-start.6 = (f32[8,256]{1,0:T(8,128)S(1)}, f32[8,256]{1,0:T(8,128)S(1)}, u32[]{:S(2)}, u32[]{:S(2)}) collective-permute-start(f32[8,256]{1,0:T(8,128)S(1)} %add.26), channel_id=1, source_target_pairs={{0,8},{4,12},{8,0},{12,4},{16,24},{20,28},{24,16},{28,20},{1,9},{5... | collective-permute-start | bytes 24584 | tf_op jit(solution)/shard_map/ppermute | solution.py:621
  39.6 4.6 %collective-permute-start.7 = (f32[8,256]{1,0:T(8,128)S(1)}, f32[8,256]{1,0:T(8,128)S(1)}, u32[]{:S(2)}, u32[]{:S(2)}) collective-permute-start(f32[8,256]{1,0:T(8,128)S(1)} %add.27), channel_id=1, source_target_pairs={{0,16},{4,20},{8,24},{12,28},{16,0},{20,4},{24,8},{28,12},{1,17},{... | collective-permute-start | bytes 24584 | tf_op jit(solution)/shard_map/ppermute | solution.py:621
